TPU v7x, 512 devices: a whole 4x4x16 slice. The times are simulated.
512 devices in a mesh: gx: 32 (over z, core), gy: 16 (over x, y).
Axes of the slice: x: 4, y: 4, z: 16, core: 2. Of those that a mesh axis runs over, the one named last changes fastest.
Arguments:
- bin_resid: float32 [524288], P(('gx', 'gy')), may hold values from -0.3 to 0.3
- geometry: float32 [6, 524288], P(None, ('gx', 'gy')), may hold values from -6 to 6
- beam_weight: float32 [16, 524288], P(None, ('gx', 'gy')), may hold values from 0.05 to 1
- dest_device: int32 [524288, 1], P(('gx', 'gy')), may hold values from 0 to 511; in each aligned block of 1024 rows (0 to 1023, 1024 to 2047, ...) at most 4 rows name the same one
- dest_column: int32 [524288], P(('gx', 'gy')), may hold values from 0 to 4095
- live_count: int32 [512], P(('gx', 'gy')), may hold values from 256 to 1024, as said below
- field_sigma: float32 [6, 16], replicated, may hold values from 0.5 to 2
- x_gap: float32 [1024], replicated, may hold values from 0.00625 to 0.0625
- y_gap: float32 [2048], replicated, may hold values from 0.0015625 to 0.015625
Outputs:
- gradient: float32 [6, 16, 1024, 2048], P(None, None, 'gx', 'gy')
Inputs may be any that keep to these rules, and one draw needn't show every extreme that they name: `dest_device`: within each device's block of 1024 bins no device is named more than 4 times, and some device is named exactly 4 times. `live_count`: some device has all 1024 bins live.
All inputs are finite; a program needn't handle non-finite values.
Results may differ from a plain program's by a relative error of at most 0.000094.
Values sent between devices are 32-bit elements; how exact they have to be, the bound alone decides.
No kernel may reach another device: no remote copies, remote signals or barrier semaphores. Data moves between devices by JAX's collectives and lax.ppermute only.
A program may use at most 64 MiB of HBM per device.

v0:
```python
import functools
import jax
import jax.numpy as jnp
from jax import lax
from jax.experimental import pallas as pl
from jax.experimental.pallas import tpu as pltpu
from jax.sharding import PartitionSpec as P

F32 = jnp.float32
BF16 = jnp.bfloat16
I32 = jnp.int32
LANES = 128
FIELDS = 6
LEVELS = 16
DEPTH = FIELDS * LEVELS
SLOTS = 4
WIDTH = 32
CX = 32
CY = 128
NEAR = 4

params = functools.partial(pltpu.CompilerParams, vmem_limit_bytes=48 * 1024 * 1024)
vmem = pl.BlockSpec(memory_space=pltpu.VMEM)
smem = pl.BlockSpec(memory_space=pltpu.SMEM)


def iota(shape, dim):
    return lax.broadcasted_iota(I32, shape, dim)


def split_two(values):
    high = values.astype(BF16)
    return high, (values - high.astype(F32)).astype(BF16)


def dot_nt(left, right):
    return lax.dot_general(left, right, (((1,), (1,)), ((), ())), preferred_element_type=F32)


def dot_nn(left, right):
    return lax.dot_general(left, right, (((1,), (0,)), ((), ())), preferred_element_type=F32)


def pack_kernel(live_ref, resid_ref, dest_ref, column_ref, geometry_ref, beam_ref, send_ref):
    bins = resid_ref.shape[1]
    peers = send_ref.shape[0]
    dest = dest_ref[...]
    dest_f = dest.astype(F32)
    dest_t = jnp.broadcast_to(dest_f, (LANES, bins)).T
    ranks = []
    for chunk in range(bins // LANES):
        rows = (chunk + 1) * LANES
        same = dest_t[:rows] == dest_f[:, chunk * LANES : rows]
        before = iota((rows, LANES), 0) < iota((rows, LANES), 1) + chunk * LANES
        ranks.append(jnp.sum(jnp.where(same & before, 1.0, 0.0), axis=0, keepdims=True))
    rank = jnp.concatenate(ranks, axis=1)
    alive = jnp.where(iota((1, bins), 1) < live_ref[0], 1.0, 0.0)
    weighted = geometry_ref[...] * (alive * resid_ref[...])
    payload = jnp.concatenate(
        [
            beam_ref[...],
            weighted,
            column_ref[...].astype(F32),
            jnp.zeros((WIDTH - LEVELS - FIELDS - 1, bins), F32),
        ],
        axis=0,
    )
    spread = jnp.concatenate([jnp.where(rank == float(s), payload, 0.0) for s in range(SLOTS)], axis=0)
    high = spread.astype(BF16)
    rest = spread - high.astype(F32)
    middle = rest.astype(BF16)
    low = (rest - middle.astype(F32)).astype(BF16)
    onehot = jnp.where(iota((peers, bins), 0) == dest, 1.0, 0.0).astype(BF16)
    send_ref[...] = dot_nt(onehot, high) + (dot_nt(onehot, middle) + dot_nt(onehot, low))


def coef_kernel(y_flat, x_cols, y_cols, y_rows, dt_high, dt_low, edge_ref, block_ref, chain, alphas):
    own = lax.axis_index("gy")
    length = y_rows.shape[1] * LANES

    def block_scalars(cols, row):
        steps, blocks = cols.shape[1:]

        def forward(p, value):
            value = value * cols[0, pl.ds(p, 1), :]
            alphas[pl.ds(p, 1), :blocks] = value
            return value

        alpha = lax.fori_loop(0, steps, forward, jnp.ones((1, blocks), F32))

        def backward(k, carried):
            gamma, beta = carried
            p = steps - 1 - k
            later = cols[1, pl.ds(p, 1), :]
            gamma = cols[2, pl.ds(p, 1), :] * alphas[pl.ds(p, 1), :blocks] + later * gamma
            return gamma, beta * later

        gamma, beta = lax.fori_loop(
            0, steps, backward, (jnp.zeros((1, blocks), F32), jnp.ones((1, blocks), F32))
        )
        block_ref[row : row + 1, :blocks] = alpha
        block_ref[row + 1 : row + 2, :blocks] = beta
        block_ref[row + 2 : row + 3, :blocks] = gamma

    block_ref[...] = jnp.zeros(block_ref.shape, F32)
    block_scalars(x_cols, 0)
    block_scalars(y_cols, 3)

    first = own * CY
    lane = iota((1, LANES), 1)

    def fill(n, row):
        row = jnp.where(lane == n, 1.0, row * y_flat[first + n])
        chain[pl.ds(n, 1), :] = row
        return row

    lax.fori_loop(0, CY, fill, jnp.zeros((1, LANES), F32))

    def unfill(k, row):
        n = CY - 1 - k
        row = chain[pl.ds(n, 1), :] * y_flat[2 * length + first + n] + row * y_flat[length + first + n]
        chain[pl.ds(n, 1), :] = row
        return row

    lax.fori_loop(0, CY, unfill, jnp.zeros((1, LANES), F32))
    scale = y_rows[2, pl.ds(own, 1), :]
    filt = chain[...].T * scale
    high, low = split_two(filt)
    dt_high[...] = high
    dt_low[...] = low
    scale_first = jnp.broadcast_to(scale[:, :1], (1, LANES))
    scale_last = jnp.broadcast_to(scale[:, CY - 1 :], (1, LANES))
    edge_ref[...] = jnp.zeros(edge_ref.shape, F32)
    edge_ref[0:1] = filt[:1] * y_flat[first]
    edge_ref[1:2] = filt[CY - 1 :] * y_flat[length + first + CY - 1] / scale_last
    edge_ref[2:3] = 1.0 / jnp.where(lane % 64 < CX, scale_last * scale_last, scale_first)


def grid_kernel(recv_ref, sigma_ref, dt_high, dt_low, edge_ref, block_out, ends_out, outer, column):
    sources = recv_ref.shape[0]
    turned = recv_ref[...].T
    for s in range(SLOTS):
        at = slice(s * sources, (s + 1) * sources)
        base = s * WIDTH
        beam = turned[base : base + LEVELS]
        for f in range(FIELDS):
            weight = turned[base + LEVELS + f : base + LEVELS + f + 1]
            high, low = split_two(beam * weight)
            outer[f * LEVELS : (f + 1) * LEVELS, at] = high
            outer[DEPTH + f * LEVELS : DEPTH + (f + 1) * LEVELS, at] = low
        place = base + LEVELS + FIELDS
        column[at, :] = jnp.broadcast_to(recv_ref[:, place : place + 1], (sources, LANES))
    lane_f = iota((1, LANES), 1).astype(F32)
    lane = iota((DEPTH, LANES), 1)
    sigma = sigma_ref[...]

    def step(n, ends):
        cols = column[...]
        start = (n * (2 * CY)).astype(F32)
        hit = [jnp.where(cols == lane_f + (start + h * CY), 1.0, 0.0).astype(BF16) for h in range(2)]
        summed = dot_nn(outer[...], jnp.concatenate(hit, axis=1))
        summed = summed[:DEPTH] + summed[DEPTH:]
        scaled = jnp.concatenate([summed[:, :CY] * sigma, summed[:, CY:] * sigma], axis=0)
        high, low = split_two(scaled)
        passed = dot_nn(high, dt_high[...]) + (dot_nn(low, dt_high[...]) + dot_nn(high, dt_low[...]))
        for h in range(2):
            part = passed[h * DEPTH : (h + 1) * DEPTH]
            x = 2 * n + h
            block_out[x] = part
            ends = jnp.where(lane == x, part[:, CY - 1 :], ends)
            ends = jnp.where(lane == x + CX, part[:, :1], ends)
        return ends

    ends = lax.fori_loop(0, CX // 2, step, jnp.zeros((DEPTH, LANES), F32))
    half = DEPTH // 2
    both = jnp.where(iota((half, LANES), 1) < 64, ends[:half], pltpu.roll(ends[half:], 64, 1))
    both = both * edge_ref[2:3]
    for j in range(ends_out.shape[0]):
        ends_out[j] = both


def line_kernel(block_tab, x_flat, ends_ref, edge_ref, block_ref, block_out, sums_out):
    own_y = lax.axis_index("gy")
    first = lax.axis_index("gx") * CX
    length = x_flat.shape[0] // 3
    count, half, _ = ends_ref.shape
    zero = jnp.zeros((half, LANES), F32)
    fore, fore_own, fores = zero, zero, []
    for j in range(count):
        fores.append(fore)
        fore_own = jnp.where(own_y == j, fore, fore_own)
        fore = ends_ref[j] + block_tab[3, j] * fore
    back, back_own = zero, zero
    for j in reversed(range(count)):
        back_own = jnp.where(own_y == j, back, back_own)
        back = ends_ref[j] + block_tab[5, j] * pltpu.roll(fores[j], CX, 1) + block_tab[4, j] * back
    both = jnp.where(iota((half, LANES), 1) % 64 < CX, fore_own, back_own)
    both = jnp.concatenate([both, pltpu.roll(both, 64, 1)], axis=0)
    edge_fore = edge_ref[0:1]
    edge_back = edge_ref[1:2]
    run = jnp.zeros((DEPTH, LANES), F32)
    begin = jnp.zeros((DEPTH, LANES), F32)
    weight = jnp.float32(1.0)
    for x in range(CX):
        part = block_ref[x] + both[:, x : x + 1] * edge_fore + both[:, CX + x : CX + x + 1] * edge_back
        block_out[x] = part
        run = part if x == 0 else part + x_flat[first + x] * run
        begin = begin + (weight * x_flat[2 * length + first + x]) * run
        weight = weight * x_flat[length + first + x]
    rows = DEPTH // NEAR
    for k in range(NEAR):
        sums_out[k, :rows] = run[k * rows : (k + 1) * rows]
        sums_out[k, rows:] = begin[k * rows : (k + 1) * rows]


def join_kernel(block_tab, sums_ref, joined_out):
    start = lax.axis_index("gx") // NEAR * NEAR
    rows = sums_ref.shape[1] // 2
    fore = jnp.zeros((rows, LANES), F32)
    fores = []
    for k in range(NEAR):
        fores.append(fore)
        fore = sums_ref[k, :rows] + block_tab[0, start + k] * fore
    back = jnp.zeros((rows, LANES), F32)
    for k in reversed(range(NEAR)):
        back = (
            sums_ref[k, rows:]
            + block_tab[2, start + k] * fores[k]
            + block_tab[1, start + k] * back
        )
    for g in range(joined_out.shape[0]):
        joined_out[g, :rows] = fore
        joined_out[g, rows:] = back


def carry_kernel(block_tab, joined_ref, sums_ref, carry_out):
    own = lax.axis_index("gx") // NEAR
    start = own * NEAR
    groups = joined_ref.shape[0]
    rows = sums_ref.shape[1] // 2
    zero = jnp.zeros((rows, LANES), F32)
    fore, fore_own, fores, betas, gammas = zero, zero, [], [], []
    for g in range(groups):
        entries = [jnp.float32(1.0)]
        for k in range(NEAR):
            entries.append(entries[-1] * block_tab[0, g * NEAR + k])
        gamma, beta = jnp.float32(0.0), jnp.float32(1.0)
        for k in reversed(range(NEAR)):
            b = block_tab[1, g * NEAR + k]
            gamma = block_tab[2, g * NEAR + k] * entries[k] + b * gamma
            beta = beta * b
        gammas.append(gamma)
        betas.append(beta)
        fores.append(fore)
        fore_own = jnp.where(own == g, fore, fore_own)
        fore = joined_ref[g, :rows] + entries[NEAR] * fore
    back, back_own = zero, zero
    for g in reversed(range(groups)):
        back_own = jnp.where(own == g, back, back_own)
        back = joined_ref[g, rows:] + gammas[g] * fores[g] + betas[g] * back
    fore, back, fores = fore_own, back_own, []
    for k in range(NEAR):
        carry_out[k, :rows] = fore
        fores.append(fore)
        fore = sums_ref[k, :rows] + block_tab[0, start + k] * fore
    for k in reversed(range(NEAR)):
        carry_out[k, rows:] = back
        back = (
            sums_ref[k, rows:]
            + block_tab[2, start + k] * fores[k]
            + block_tab[1, start + k] * back
        )


def final_kernel(x_flat, carry_ref, block_ref, out_ref, scaled):
    first = lax.axis_index("gx") * CX
    length = x_flat.shape[0] // 3
    rows = carry_ref.shape[1] // 2
    run = jnp.concatenate([carry_ref[k, :rows] for k in range(NEAR)], axis=0)
    back = jnp.concatenate([carry_ref[k, rows:] for k in range(NEAR)], axis=0)
    for x in range(CX):
        run = block_ref[x] + x_flat[first + x] * run
        scaled[x] = x_flat[2 * length + first + x] * run
    for x in reversed(range(CX)):
        back = scaled[x] + x_flat[length + first + x] * back
        out_ref[pl.ds(x, DEPTH, stride=CX), :] = x_flat[2 * length + first + x] * back


def table(gap):
    decay = 1.0 - gap
    edge = jnp.zeros((1,), F32)
    prior = jnp.concatenate([edge, decay[:-1]])
    later = jnp.concatenate([decay[1:], edge])
    return jnp.stack([prior, later, jnp.sqrt(gap * (2.0 - gap))])


def call(kernel, outs, specs, scratch=()):
    shapes = tuple(jax.ShapeDtypeStruct(s, t) for s, t in outs)
    return pl.pallas_call(
        kernel,
        out_shape=shapes if len(shapes) > 1 else shapes[0],
        in_specs=specs,
        out_specs=(vmem,) * len(shapes) if len(shapes) > 1 else vmem,
        scratch_shapes=scratch,
        compiler_params=params(),
    )


def local(bin_resid, geometry, beam_weight, dest_device, dest_column, live_count, field_sigma, x_gap, y_gap):
    count_x = lax.axis_size("gx")
    count_y = lax.axis_size("gy")
    peers = count_x * count_y
    bins = bin_resid.shape[0]
    far = count_x // NEAR
    near_groups = [[g * NEAR + k for k in range(NEAR)] for g in range(far)]
    far_groups = [[g * NEAR + k for g in range(far)] for k in range(NEAR)]
    a2a = functools.partial(lax.all_to_all, tiled=True)

    send = call(pack_kernel, [((peers, LANES), F32)], [smem] + [vmem] * 5)(
        live_count,
        bin_resid.reshape(1, bins),
        dest_device.reshape(1, bins),
        dest_column.reshape(1, bins),
        geometry,
        beam_weight,
    )
    tab_x = table(x_gap)
    tab_y = table(y_gap)
    x_flat = tab_x.reshape(-1)
    dt_high, dt_low, edge, blocks = call(
        coef_kernel,
        [((CY, CY), BF16), ((CY, CY), BF16), ((8, LANES), F32), ((8, LANES), F32)],
        [smem, vmem, vmem, vmem],
        [pltpu.VMEM((CY, LANES), F32), pltpu.VMEM((CY, LANES), F32)],
    )(
        tab_y.reshape(-1),
        tab_x.reshape(3, count_x, CX).transpose(0, 2, 1),
        tab_y.reshape(3, count_y, CY).transpose(0, 2, 1),
        tab_y.reshape(3, count_y, CY),
    )
    sigma = jnp.broadcast_to(field_sigma.reshape(DEPTH, 1), (DEPTH, LANES))

    moved = a2a(send.reshape(count_x, count_y, LANES), "gx", split_axis=0, concat_axis=0)
    moved = a2a(moved, "gy", split_axis=1, concat_axis=1)
    block, ends = call(
        grid_kernel,
        [((CX, DEPTH, LANES), F32), ((count_y, DEPTH // 2, LANES), F32)],
        [vmem] * 5,
        [pltpu.VMEM((2 * DEPTH, SLOTS * peers), BF16), pltpu.VMEM((SLOTS * peers, LANES), F32)],
    )(moved.reshape(peers, LANES), sigma, dt_high, dt_low, edge)
    ends = a2a(ends, "gy", split_axis=0, concat_axis=0)
    block, sums = call(
        line_kernel,
        [((CX, DEPTH, LANES), F32), ((NEAR, 2 * DEPTH // NEAR, LANES), F32)],
        [smem, smem, vmem, vmem, vmem],
    )(blocks, x_flat, ends, edge, block)
    sums = a2a(sums, "gx", split_axis=0, concat_axis=0, axis_index_groups=near_groups)
    joined = call(join_kernel, [((far, 2 * DEPTH // NEAR, LANES), F32)], [smem, vmem])(blocks, sums)
    joined = a2a(joined, "gx", split_axis=0, concat_axis=0, axis_index_groups=far_groups)
    carry = call(carry_kernel, [((NEAR, 2 * DEPTH // NEAR, LANES), F32)], [smem, vmem, vmem])(
        blocks, joined, sums
    )
    carry = a2a(carry, "gx", split_axis=0, concat_axis=0, axis_index_groups=near_groups)
    out = call(
        final_kernel,
        [((DEPTH * CX, LANES), F32)],
        [smem, vmem, vmem],
        [pltpu.VMEM((CX, DEPTH, LANES), F32)],
    )(x_flat, carry, block)
    return out.reshape(FIELDS, LEVELS, CX, CY)


def solution(mesh):
    both = ("gx", "gy")
    placed = (P(both), P(None, both), P(None, both), P(both, None), P(both), P(both), P(), P(), P())
    return jax.shard_map(
        local, mesh=mesh, in_specs=placed, out_specs=P(None, None, "gx", "gy"), check_vma=False
    )
```

profile of v0, /device:TPU:1, one launch (start us, length us, event | category | flops | bytes accessed | tf_op | source)
XLA Modules:
  0.0 129.2 jit_solution(6881834472042988543)
XLA Ops:
  0.0 0.0 copy-start.5
  0.7 0.0 copy-start
  0.7 0.8 copy-done
  1.5 0.0 copy-start.1
  1.5 0.8 copy-done.1
  2.3 0.0 copy-start.2
  2.3 0.7 copy-done.2
  3.0 0.0 copy-start.3
  3.0 0.7 copy-done.3
  3.6 0.0 copy-start.4
  3.6 0.7 copy-done.4
  4.3 2.1 %shard_map.92 = f32[512,128]{1,0:T(8,128)} custom-call(s32[1]{0:T(128)S(6)} %copy.27.live_ref, f32[1,1024]{1,0:T(1,128)S(1)} %bitcast.23, s32[1,1024]{1,0:T(1,128)S(1)} %bitcast.24, s32[1,1024]{1,0:T(1,128)S(1)} %bitcast.25, f32[6,1024]{1,0:T(8,128)S(1)} %copy-done.1, f32[16,1024]{1,0:T(8,128)S(1)} %copy-done), custom_call_target="tpu_custom_call" | custom-call | tf_op jit(solution)/shard_map/pallas_call | solution.py:319
  6.4 16.7 %all-to-all-start = ((f32[32,16,128]{2,1,0:T(8,128)}), f32[32,16,128]{2,1,0:T(8,128)S(1)}, u32[]{:S(2)}, u32[]{:S(2)}) async-start(f32[32,16,128]{2,1,0:T(8,128)} %bitcast.14), calls=%async_computation | async-start | bytes 524288 | tf_op jit(solution)/shard_map/all_to_all | solution.py:343
  23.2 0.7 fusion.4
  23.9 0.1 fusion.6
  24.0 0.1 fusion.2
  24.1 0.7 broadcast_subtract_fusion.1
  24.8 0.1 fusion.7
  24.9 20.3 %all-to-all-done = f32[32,16,128]{2,1,0:T(8,128)S(1)} async-done(((f32[32,16,128]{2,1,0:T(8,128)}), f32[32,16,128]{2,1,0:T(8,128)S(1)}, u32[]{:S(2)}, u32[]{:S(2)}) %all-to-all-start) | async-done | bytes 262176 | tf_op jit(solution)/shard_map/all_to_all | solution.py:343
  45.2 0.8 copy.25
  46.0 6.8 %all-to-all-start.1 = ((f32[32,16,128]{2,0,1:T(8,128)}), f32[32,16,128]{2,0,1:T(8,128)S(1)}, u32[]{:S(2)}, u32[]{:S(2)}) async-start(f32[32,16,128]{2,0,1:T(8,128)} %copy.25), calls=%async_computation.1 | async-start | bytes 524288 | tf_op jit(solution)/shard_map/all_to_all | solution.py:344
  52.7 0.1 pad_maximum_fusion.5
  52.8 0.0 copy-done.5
  52.8 0.1 broadcast_in_dim.7
  52.9 0.1 stack.48
  53.0 0.1 copy.21
  53.0 0.1 stack.49
  53.1 0.1 copy.22
  53.2 0.1 stack.50
  53.3 0.1 copy.23
  53.4 0.1 copy.24.y_cols
  53.5 5.0 %shard_map.91 = (bf16[128,128]{1,0:T(8,128)(2,1)S(1)}, bf16[128,128]{1,0:T(8,128)(2,1)S(1)}, f32[8,128]{1,0:T(8,128)S(1)}, f32[8,128]{1,0:T(8,128)S(1)}) custom-call(f32[6144]{0:T(1024)S(1)} %reshape.42.y_flat, f32[3,32,32]{2,1,0:T(8,128)S(1)} %maximum_bitcast_fusion.x_cols, f32[3,128,16]{2,1,0:T(8,128)S(1)} %copy.24.y_cols, ...), custom_call_target="tpu_custom_call" | custom-call | tf_op jit(solution)/shard_map/pallas_call | solution.py:330
  58.6 1.7 %all-to-all-done.1 = f32[32,16,128]{2,0,1:T(8,128)S(1)} async-done(((f32[32,16,128]{2,0,1:T(8,128)}), f32[32,16,128]{2,0,1:T(8,128)S(1)}, u32[]{:S(2)}, u32[]{:S(2)}) %all-to-all-start.1) | async-done | bytes 262176 | tf_op jit(solution)/shard_map/all_to_all | solution.py:344
  60.2 0.2 copy.26
  60.4 0.1 broadcast_in_dim.8.sigma_ref
  60.5 12.7 %shard_map.93 = (f32[32,96,128]{2,1,0:T(8,128)S(1)}, f32[16,48,128]{2,1,0:T(8,128)}) custom-call(f32[512,128]{1,0:T(8,128)S(1)} %bitcast.22, f32[96,128]{1,0:T(8,128)S(1)} %broadcast_in_dim.8.sigma_ref, bf16[128,128]{1,0:T(8,128)(2,1)S(1)} %get-tuple-element.14.dt_high, bf16[128,128]{1,0:T(8,128)(2,1)S(1)} %get-tuple-element.15.dt_low, ...), custom_call_target="tpu_custom_call" | custom-call | tf_op jit(solution)/shard_map/pallas_call | solution.py:345
  73.1 5.0 %all-to-all-start.2 = ((f32[16,48,128]{2,1,0:T(8,128)}), f32[16,48,128]{2,1,0:T(8,128)S(1)}, u32[]{:S(2)}, u32[]{:S(2)}) async-start(f32[16,48,128]{2,1,0:T(8,128)} %get-tuple-element.17), calls=%async_computation.2 | async-start | bytes 786432 | tf_op jit(solution)/shard_map/all_to_all | solution.py:351
  78.2 7.9 %all-to-all-done.2.ends_ref = f32[16,48,128]{2,1,0:T(8,128)S(1)} async-done(((f32[16,48,128]{2,1,0:T(8,128)}), f32[16,48,128]{2,1,0:T(8,128)S(1)}, u32[]{:S(2)}, u32[]{:S(2)}) %all-to-all-start.2) | async-done | bytes 393248 | tf_op jit(solution)/shard_map/all_to_all | solution.py:351
  86.1 2.0 %shard_map.94 = (f32[32,96,128]{2,1,0:T(8,128)S(1)}, f32[4,48,128]{2,1,0:T(8,128)S(1)}) custom-call(f32[8,128]{1,0:T(8,128)S(1)} %get-tuple-element.13.block_tab, f32[3072]{0:T(1024)S(1)} %reshape.41.x_flat, f32[16,48,128]{2,1,0:T(8,128)S(1)} %all-to-all-done.2.ends_ref, f32[8,128]{1,0:T(8,128)S(1)} %get-tuple-element.16.edge_ref, ...), custom_call_target="tpu_custom_call" | custom-call | tf_op jit(solution)/shard_map/pallas_call | solution.py:352
  88.1 8.7 %all_to_all.30.sums_ref = f32[4,48,128]{2,1,0:T(8,128)S(1)} all-to-all(f32[4,48,128]{2,1,0:T(8,128)S(1)} %get-tuple-element.19), channel_id=1, replica_groups={{0,16,32,48},{64,80,96,112},{128,144,160,176},{192,208,224,240},{256,27..., dimensions={0} | all-to-all | bytes 196608 | tf_op jit(solution)/shard_map/all_to_all | solution.py:357
  96.8 0.6 shard_map.95
  97.4 17.1 %all_to_all.31.joined_ref = f32[8,48,128]{2,1,0:T(8,128)S(1)} all-to-all(f32[8,48,128]{2,1,0:T(8,128)S(1)} %shard_map.95), channel_id=1, replica_groups={{0,64,128,192,256,320,384,448},{16,80,144,208,272,336,400,464},{32,96,1..., dimensions={0} | all-to-all | bytes 393216 | tf_op jit(solution)/shard_map/all_to_all | solution.py:359
  114.6 0.7 shard_map.96
  115.3 10.3 %all_to_all.32.carry_ref = f32[4,48,128]{2,1,0:T(8,128)S(1)} all-to-all(f32[4,48,128]{2,1,0:T(8,128)S(1)} %shard_map.96), channel_id=1, replica_groups={{0,16,32,48},{64,80,96,112},{128,144,160,176},{192,208,224,240},{256,27..., dimensions={0} | all-to-all | bytes 196608 | tf_op jit(solution)/shard_map/all_to_all | solution.py:363
  125.6 3.6 %shard_map.97 = f32[3072,128]{1,0:T(8,128)} custom-call(f32[3072]{0:T(1024)S(1)} %reshape.41.x_flat, f32[4,48,128]{2,1,0:T(8,128)S(1)} %all_to_all.32.carry_ref, f32[32,96,128]{2,1,0:T(8,128)S(1)} %get-tuple-element.20.block_ref), custom_call_target="tpu_custom_call" | custom-call | tf_op jit(solution)/shard_map/pallas_call | solution.py:364
  (6 shorter events, 0.1 us)
Async XLA Ops:
  0.0 52.8 %copy-start.5 = (f32[6,16]{1,0:T(8,128)S(1)}, f32[6,16]{1,0:T(8,128)}, u32[]{:S(2)}) copy-start(f32[6,16]{1,0:T(8,128)} %param.15) | copy-start | bytes 1156
  0.7 0.8 copy-start
  1.5 0.8 copy-start.1
  2.3 0.7 copy-start.2
  3.0 0.7 copy-start.3
  3.6 0.7 copy-start.4
  6.4 38.8 %all-to-all-start = ((f32[32,16,128]{2,1,0:T(8,128)}), f32[32,16,128]{2,1,0:T(8,128)S(1)}, u32[]{:S(2)}, u32[]{:S(2)}) async-start(f32[32,16,128]{2,1,0:T(8,128)} %bitcast.14), calls=%async_computation | async-start | bytes 524288 | tf_op jit(solution)/shard_map/all_to_all | solution.py:343
  46.0 14.3 %all-to-all-start.1 = ((f32[32,16,128]{2,0,1:T(8,128)}), f32[32,16,128]{2,0,1:T(8,128)S(1)}, u32[]{:S(2)}, u32[]{:S(2)}) async-start(f32[32,16,128]{2,0,1:T(8,128)} %copy.25), calls=%async_computation.1 | async-start | bytes 524288 | tf_op jit(solution)/shard_map/all_to_all | solution.py:344
  73.1 13.0 %all-to-all-start.2 = ((f32[16,48,128]{2,1,0:T(8,128)}), f32[16,48,128]{2,1,0:T(8,128)S(1)}, u32[]{:S(2)}, u32[]{:S(2)}) async-start(f32[16,48,128]{2,1,0:T(8,128)} %get-tuple-element.17), calls=%async_computation.2 | async-start | bytes 786432 | tf_op jit(solution)/shard_map/all_to_all | solution.py:351
where the time goes:
time: 130 us; the launch traced here: 129 us
  blocking collectives  36.1 us (28%)
  waiting for transfers between devices  29.9 us (23%)
  starting transfers between devices  28.5 us (22%)
  Pallas kernels  26.7 us (21%)
  local copies, waits for them, and re-layouts  5.49 us (4%)
  other arithmetic  1.62 us (1%)
    all_to_all x1, waiting for transfers between devices, local(): a2a(send.reshape(count_x, count_y, LANES), 'gx', split_axis=0, concat_axi...  20.3 us
    all_to_all x1, blocking collectives, local(): a2a(joined, 'gx', split_axis=0, concat_axis=0, axis_index_groups=far_groups)  17.1 us
    all_to_all x1, starting transfers between devices, local(): a2a(send.reshape(count_x, count_y, LANES), 'gx', split_axis=0, concat_axi...  16.7 us
    pallas_call x1, Pallas kernels, local(): call(grid_kernel, [((CX, DEPTH, LANES), F32), ((count_y, DEPTH // 2, LANE...  12.7 us
    all_to_all x1, blocking collectives, local(): a2a(carry, 'gx', split_axis=0, concat_axis=0, axis_index_groups=near_groups)  10.3 us
    all_to_all x1, blocking collectives, local(): a2a(sums, 'gx', split_axis=0, concat_axis=0, axis_index_groups=near_groups)  8.7 us
    all_to_all x1, waiting for transfers between devices, local(): ends = a2a(ends, 'gy', split_axis=0, concat_axis=0)  7.94 us
    all_to_all x1, starting transfers between devices, local(): moved = a2a(moved, 'gy', split_axis=1, concat_axis=1)  6.75 us
  transfers between devices with their start and end apart: 3, of which 3 were waited for; matrix products, arithmetic and copies ran while one was open for 2% of the time, Pallas kernels for 4%

commit v1 on v0

--- a/solution.py
+++ b/solution.py
@@ -74,16 +74,18 @@
     send_ref[...] = dot_nt(onehot, high) + (dot_nt(onehot, middle) + dot_nt(onehot, low))
 
 
-def coef_kernel(y_flat, x_cols, y_cols, y_rows, dt_high, dt_low, edge_ref, block_ref, chain, alphas):
-    own = lax.axis_index("gy")
+def coef_kernel(x_flat, y_flat, x_cols, y_cols, y_rows, dt_high, dt_low, tab_ref, edge_ref, block_ref, ends_ref, chain, gammas, betas):
+    own_x = lax.axis_index("gx")
+    own_y = lax.axis_index("gy")
     length = y_rows.shape[1] * LANES
+    span = x_cols.shape[2] * CX
 
     def block_scalars(cols, row):
         steps, blocks = cols.shape[1:]
 
         def forward(p, value):
             value = value * cols[0, pl.ds(p, 1), :]
-            alphas[pl.ds(p, 1), :blocks] = value
+            gammas[pl.ds(p, 1), :blocks] = value
             return value
 
         alpha = lax.fori_loop(0, steps, forward, jnp.ones((1, blocks), F32))
@@ -92,8 +94,11 @@
             gamma, beta = carried
             p = steps - 1 - k
             later = cols[1, pl.ds(p, 1), :]
-            gamma = cols[2, pl.ds(p, 1), :] * alphas[pl.ds(p, 1), :blocks] + later * gamma
-            return gamma, beta * later
+            gamma = cols[2, pl.ds(p, 1), :] * gammas[pl.ds(p, 1), :blocks] + later * gamma
+            beta = beta * later
+            gammas[pl.ds(p, 1), :blocks] = gamma
+            betas[pl.ds(p, 1), :blocks] = beta
+            return gamma, beta
 
         gamma, beta = lax.fori_loop(
             0, steps, backward, (jnp.zeros((1, blocks), F32), jnp.ones((1, blocks), F32))
@@ -103,11 +108,38 @@
         block_ref[row + 2 : row + 3, :blocks] = gamma
 
     block_ref[...] = jnp.zeros(block_ref.shape, F32)
+    block_scalars(y_cols, 3)
     block_scalars(x_cols, 0)
-    block_scalars(y_cols, 3)
-
-    first = own * CY
+    blocks = x_cols.shape[2]
+    mine = iota((CX, blocks), 1) == own_x
+    for k, scratch in enumerate((gammas, betas)):
+        picked = jnp.where(mine, scratch[:CX, :blocks] * x_cols[2], 0.0)
+        ends_ref[k * CX : (k + 1) * CX] = jnp.broadcast_to(
+            jnp.sum(picked, axis=1, keepdims=True), (CX, LANES)
+        )
+
     lane = iota((1, LANES), 1)
+    first = own_x * CX
+    down = []
+    weight = jnp.float32(1.0)
+    for x in range(CX):
+        down.append(weight * x_flat[2 * span + first + x])
+        weight = weight * x_flat[span + first + x]
+    tail, start = jnp.float32(1.0), down[CX - 1]
+    tails, starts = [tail], [start]
+    for x in reversed(range(CX - 1)):
+        factor = x_flat[first + x + 1]
+        tail = tail * factor
+        start = down[x] + factor * start
+        tails.append(tail)
+        starts.append(start)
+    row_tail = jnp.zeros((1, LANES), F32)
+    row_start = jnp.zeros((1, LANES), F32)
+    for x in range(CX):
+        row_tail = jnp.where(lane % CX == x, tails[CX - 1 - x], row_tail)
+        row_start = jnp.where(lane % CX == x, starts[CX - 1 - x], row_start)
+
+    first = own_y * CY
 
     def fill(n, row):
         row = jnp.where(lane == n, 1.0, row * y_flat[first + n])
@@ -123,66 +155,109 @@
         return row
 
     lax.fori_loop(0, CY, unfill, jnp.zeros((1, LANES), F32))
-    scale = y_rows[2, pl.ds(own, 1), :]
+    scale = y_rows[2, pl.ds(own_y, 1), :]
     filt = chain[...].T * scale
     high, low = split_two(filt)
     dt_high[...] = high
     dt_low[...] = low
-    scale_first = jnp.broadcast_to(scale[:, :1], (1, LANES))
-    scale_last = jnp.broadcast_to(scale[:, CY - 1 :], (1, LANES))
+    scale_first = scale[:, :1]
+    scale_last = scale[:, CY - 1 :]
+    tab_ref[0] = jnp.broadcast_to(filt[:, CY - 1 :] / (scale_last * scale_last), (CY, LANES))
+    tab_ref[1] = jnp.broadcast_to(filt[:, :1] / scale_first, (CY, LANES))
     edge_ref[...] = jnp.zeros(edge_ref.shape, F32)
     edge_ref[0:1] = filt[:1] * y_flat[first]
     edge_ref[1:2] = filt[CY - 1 :] * y_flat[length + first + CY - 1] / scale_last
-    edge_ref[2:3] = 1.0 / jnp.where(lane % 64 < CX, scale_last * scale_last, scale_first)
-
-
-def grid_kernel(recv_ref, sigma_ref, dt_high, dt_low, edge_ref, block_out, ends_out, outer, column):
+    edge_ref[2:3] = row_tail
+    edge_ref[3:4] = row_start
+
+
+def ends_kernel(recv_ref, sigma_ref, tab_ref, outer_out, column_out, ends_out, outer):
     sources = recv_ref.shape[0]
     turned = recv_ref[...].T
+    weights = [jnp.concatenate([tab_ref[c]] * (sources // LANES), axis=1) for c in range(2)]
+    hits = []
     for s in range(SLOTS):
         at = slice(s * sources, (s + 1) * sources)
         base = s * WIDTH
         beam = turned[base : base + LEVELS]
+        place = turned[base + LEVELS + FIELDS : base + LEVELS + FIELDS + 1]
+        column_out[:, at] = place
+        place = place.astype(I32)
+        on_y = iota((CY, sources), 0) == (place & (CY - 1))
+        ends = [jnp.sum(jnp.where(on_y, w, 0.0), axis=0, keepdims=True) for w in weights]
+        hits.append(jnp.where((iota((LANES, sources), 0) & (CX - 1)) == (place >> 7), 1.0, 0.0).astype(BF16))
         for f in range(FIELDS):
-            weight = turned[base + LEVELS + f : base + LEVELS + f + 1]
-            high, low = split_two(beam * weight)
-            outer[f * LEVELS : (f + 1) * LEVELS, at] = high
-            outer[DEPTH + f * LEVELS : DEPTH + (f + 1) * LEVELS, at] = low
-        place = base + LEVELS + FIELDS
-        column[at, :] = jnp.broadcast_to(recv_ref[:, place : place + 1], (sources, LANES))
-    lane_f = iota((1, LANES), 1).astype(F32)
-    lane = iota((DEPTH, LANES), 1)
+            prod = beam * turned[base + LEVELS + f : base + LEVELS + f + 1]
+            rows = slice(f * LEVELS, (f + 1) * LEVELS)
+            high, low = split_two(prod)
+            outer_out[rows, at] = high
+            outer_out[DEPTH + f * LEVELS : DEPTH + (f + 1) * LEVELS, at] = low
+            for c in range(2):
+                high, low = split_two(prod * ends[c])
+                outer[(2 * c) * DEPTH + f * LEVELS : (2 * c) * DEPTH + (f + 1) * LEVELS, at] = high
+                outer[(2 * c + 1) * DEPTH + f * LEVELS : (2 * c + 1) * DEPTH + (f + 1) * LEVELS, at] = low
+    summed = dot_nt(outer[...], jnp.concatenate(hits, axis=1))
     sigma = sigma_ref[...]
-
-    def step(n, ends):
-        cols = column[...]
-        start = (n * (2 * CY)).astype(F32)
-        hit = [jnp.where(cols == lane_f + (start + h * CY), 1.0, 0.0).astype(BF16) for h in range(2)]
-        summed = dot_nn(outer[...], jnp.concatenate(hit, axis=1))
-        summed = summed[:DEPTH] + summed[DEPTH:]
-        scaled = jnp.concatenate([summed[:, :CY] * sigma, summed[:, CY:] * sigma], axis=0)
-        high, low = split_two(scaled)
-        passed = dot_nn(high, dt_high[...]) + (dot_nn(low, dt_high[...]) + dot_nn(high, dt_low[...]))
-        for h in range(2):
-            part = passed[h * DEPTH : (h + 1) * DEPTH]
-            x = 2 * n + h
-            block_out[x] = part
-            ends = jnp.where(lane == x, part[:, CY - 1 :], ends)
-            ends = jnp.where(lane == x + CX, part[:, :1], ends)
-        return ends
-
-    ends = lax.fori_loop(0, CX // 2, step, jnp.zeros((DEPTH, LANES), F32))
+    fore = (summed[:DEPTH] + summed[DEPTH : 2 * DEPTH]) * sigma
+    back = (summed[2 * DEPTH : 3 * DEPTH] + summed[3 * DEPTH :]) * sigma
     half = DEPTH // 2
-    both = jnp.where(iota((half, LANES), 1) < 64, ends[:half], pltpu.roll(ends[half:], 64, 1))
-    both = both * edge_ref[2:3]
+    lane = iota((half, LANES), 1)
+    both = jnp.where(
+        lane < 64,
+        jnp.where(lane < 32, fore[:half], back[:half]),
+        jnp.where(lane < 96, fore[half:], back[half:]),
+    )
     for j in range(ends_out.shape[0]):
         ends_out[j] = both
 
 
-def line_kernel(block_tab, x_flat, ends_ref, edge_ref, block_ref, block_out, sums_out):
-    own_y = lax.axis_index("gy")
+def grid_kernel(x_flat, outer_ref, column_ref, recv_ref, sigma_ref, dt_high, dt_low, block_out, sums_out, masked, hit):
+    sources = recv_ref.shape[0]
     first = lax.axis_index("gx") * CX
     length = x_flat.shape[0] // 3
+    lane2 = iota((1, 2 * LANES), 1)
+    for s in range(SLOTS):
+        place = s * WIDTH + LEVELS + FIELDS
+        cols = jnp.broadcast_to(recv_ref[:, place : place + 1], (sources, LANES)).astype(I32) & (2 * CY - 1)
+        cols = jnp.concatenate([cols, cols], axis=1)
+        hit[s * sources : (s + 1) * sources] = jnp.where(cols == lane2, 1.0, 0.0).astype(BF16)
+    pair = column_ref[...].astype(I32) >> 8
+    sigma = sigma_ref[...]
+    group = 4
+
+    def step(n, carried):
+        run, begin, weight = carried
+        for c in range(group):
+            keep = jnp.where(pair == n * group + c, 1.0, 0.0)
+            keep = jnp.broadcast_to(keep, (16, keep.shape[1])).astype(BF16)
+            for r in range(2 * DEPTH // 16):
+                masked[c * 2 * DEPTH + r * 16 : c * 2 * DEPTH + (r + 1) * 16] = (
+                    outer_ref[r * 16 : (r + 1) * 16] * keep
+                )
+        summed = dot_nn(masked[...], hit[...])
+        parts = []
+        for c in range(group):
+            both = summed[c * 2 * DEPTH : c * 2 * DEPTH + DEPTH] + summed[c * 2 * DEPTH + DEPTH : (c + 1) * 2 * DEPTH]
+            parts += [both[:, :CY] * sigma, both[:, CY:] * sigma]
+        high, low = split_two(jnp.concatenate(parts, axis=0))
+        passed = dot_nn(high, dt_high[...]) + (dot_nn(low, dt_high[...]) + dot_nn(high, dt_low[...]))
+        for h in range(2 * group):
+            part = passed[h * DEPTH : (h + 1) * DEPTH]
+            x = n * 2 * group + h
+            block_out[x] = part
+            run = part + jnp.where(x == 0, 0.0, x_flat[first + x]) * run
+            begin = begin + (weight * x_flat[2 * length + first + x]) * run
+            weight = weight * x_flat[length + first + x]
+        return run, begin, weight
+
+    zero = jnp.zeros((DEPTH, LANES), F32)
+    run, begin, _ = lax.fori_loop(0, CX // (2 * group), step, (zero, zero, jnp.float32(1.0)))
+    sums_out[0] = run
+    sums_out[1] = begin
+
+
+def line_kernel(block_tab, ends_ref, edge_ref, raw_ref, both_out, sums_out):
+    own_y = lax.axis_index("gy")
     count, half, _ = ends_ref.shape
     zero = jnp.zeros((half, LANES), F32)
     fore, fore_own, fores = zero, zero, []
@@ -196,21 +271,35 @@
         back = ends_ref[j] + block_tab[5, j] * pltpu.roll(fores[j], CX, 1) + block_tab[4, j] * back
     both = jnp.where(iota((half, LANES), 1) % 64 < CX, fore_own, back_own)
     both = jnp.concatenate([both, pltpu.roll(both, 64, 1)], axis=0)
+    both_out[...] = both
+    lane = iota((DEPTH, LANES), 1)
+    edge_fore = edge_ref[0:1]
+    edge_back = edge_ref[1:2]
+    rows = DEPTH // NEAR
+    for c in range(2):
+        weighted = both * edge_ref[2 + c : 3 + c]
+        fore_part = jnp.sum(jnp.where(lane < CX, weighted, 0.0), axis=1, keepdims=True)
+        back_part = jnp.sum(jnp.where((lane >= CX) & (lane < 2 * CX), weighted, 0.0), axis=1, keepdims=True)
+        total = raw_ref[c] + fore_part * edge_fore + back_part * edge_back
+        for k in range(NEAR):
+            sums_out[k, c * rows : (c + 1) * rows] = total[k * rows : (k + 1) * rows]
+
+
+def scan_kernel(x_flat, both_ref, edge_ref, block_ref, out_ref, scaled):
+    first = lax.axis_index("gx") * CX
+    length = x_flat.shape[0] // 3
+    both = both_ref[...]
     edge_fore = edge_ref[0:1]
     edge_back = edge_ref[1:2]
     run = jnp.zeros((DEPTH, LANES), F32)
-    begin = jnp.zeros((DEPTH, LANES), F32)
-    weight = jnp.float32(1.0)
     for x in range(CX):
         part = block_ref[x] + both[:, x : x + 1] * edge_fore + both[:, CX + x : CX + x + 1] * edge_back
-        block_out[x] = part
         run = part if x == 0 else part + x_flat[first + x] * run
-        begin = begin + (weight * x_flat[2 * length + first + x]) * run
-        weight = weight * x_flat[length + first + x]
-    rows = DEPTH // NEAR
-    for k in range(NEAR):
-        sums_out[k, :rows] = run[k * rows : (k + 1) * rows]
-        sums_out[k, rows:] = begin[k * rows : (k + 1) * rows]
+        scaled[x] = x_flat[2 * length + first + x] * run
+    back = jnp.zeros((DEPTH, LANES), F32)
+    for x in reversed(range(CX)):
+        back = scaled[x] if x == CX - 1 else scaled[x] + x_flat[length + first + x] * back
+        out_ref[pl.ds(x, DEPTH, stride=CX), :] = x_flat[2 * length + first + x] * back
 
 
 def join_kernel(block_tab, sums_ref, joined_out):
@@ -272,18 +361,17 @@
         )
 
 
-def final_kernel(x_flat, carry_ref, block_ref, out_ref, scaled):
-    first = lax.axis_index("gx") * CX
-    length = x_flat.shape[0] // 3
+def final_kernel(carry_ref, ends_ref, block_ref, out_ref):
     rows = carry_ref.shape[1] // 2
-    run = jnp.concatenate([carry_ref[k, :rows] for k in range(NEAR)], axis=0)
-    back = jnp.concatenate([carry_ref[k, rows:] for k in range(NEAR)], axis=0)
-    for x in range(CX):
-        run = block_ref[x] + x_flat[first + x] * run
-        scaled[x] = x_flat[2 * length + first + x] * run
-    for x in reversed(range(CX)):
-        back = scaled[x] + x_flat[length + first + x] * back
-        out_ref[pl.ds(x, DEPTH, stride=CX), :] = x_flat[2 * length + first + x] * back
+    fore = ends_ref[:CX]
+    back = ends_ref[CX:]
+    base = pl.program_id(0) * (rows * CX)
+    for r in range(rows):
+        out_ref[r * CX : (r + 1) * CX] = (
+            block_ref[pl.ds(pl.multiple_of(base + r * CX, CX), CX), :]
+            + carry_ref[0, r : r + 1] * fore
+            + carry_ref[0, rows + r : rows + r + 1] * back
+        )
 
 
 def table(gap):
@@ -311,12 +399,33 @@
     count_y = lax.axis_size("gy")
     peers = count_x * count_y
     bins = bin_resid.shape[0]
+    slots = SLOTS * peers
     far = count_x // NEAR
+    chunk = 2 * DEPTH // NEAR
     near_groups = [[g * NEAR + k for k in range(NEAR)] for g in range(far)]
     far_groups = [[g * NEAR + k for g in range(far)] for k in range(NEAR)]
+    side_groups = [[i * count_y + j for i in group for j in range(count_y)] for group in near_groups]
     a2a = functools.partial(lax.all_to_all, tiled=True)
-
-    send = call(pack_kernel, [((peers, LANES), F32)], [smem] + [vmem] * 5)(
+    tie = lax.optimization_barrier
+
+    def whole(*shape):
+        return pl.BlockSpec(shape, lambda k: (0,) * len(shape))
+
+    send = pl.pallas_call(
+        pack_kernel,
+        grid=(1,),
+        out_shape=jax.ShapeDtypeStruct((peers, LANES), F32),
+        in_specs=[
+            smem,
+            whole(1, bins),
+            whole(1, bins),
+            whole(1, bins),
+            whole(FIELDS, bins),
+            whole(LEVELS, bins),
+        ],
+        out_specs=whole(peers, LANES),
+        compiler_params=params(),
+    )(
         live_count,
         bin_resid.reshape(1, bins),
         dest_device.reshape(1, bins),
@@ -324,49 +433,73 @@
         geometry,
         beam_weight,
     )
+    moved = a2a(send.reshape(far, peers // far, LANES), "gx", split_axis=0, concat_axis=0, axis_index_groups=far_groups)
     tab_x = table(x_gap)
     tab_y = table(y_gap)
     x_flat = tab_x.reshape(-1)
-    dt_high, dt_low, edge, blocks = call(
+    sigma = jnp.broadcast_to(field_sigma.reshape(DEPTH, 1), (DEPTH, LANES))
+    coefs = call(
         coef_kernel,
-        [((CY, CY), BF16), ((CY, CY), BF16), ((8, LANES), F32), ((8, LANES), F32)],
-        [smem, vmem, vmem, vmem],
-        [pltpu.VMEM((CY, LANES), F32), pltpu.VMEM((CY, LANES), F32)],
+        [
+            ((CY, CY), BF16),
+            ((CY, CY), BF16),
+            ((2, CY, LANES), F32),
+            ((8, LANES), F32),
+            ((8, LANES), F32),
+            ((2 * CX, LANES), F32),
+        ],
+        [smem, smem, vmem, vmem, vmem],
+        [pltpu.VMEM((CY, LANES), F32)] * 3,
     )(
+        x_flat,
         tab_y.reshape(-1),
         tab_x.reshape(3, count_x, CX).transpose(0, 2, 1),
         tab_y.reshape(3, count_y, CY).transpose(0, 2, 1),
         tab_y.reshape(3, count_y, CY),
     )
-    sigma = jnp.broadcast_to(field_sigma.reshape(DEPTH, 1), (DEPTH, LANES))
-
-    moved = a2a(send.reshape(count_x, count_y, LANES), "gx", split_axis=0, concat_axis=0)
-    moved = a2a(moved, "gy", split_axis=1, concat_axis=1)
-    block, ends = call(
+    moved, coefs, sigma = tie((moved, coefs, sigma))
+    dt_high, dt_low, tab, edge, blocks, x_ends = coefs
+    moved = a2a(moved.transpose(1, 0, 2), ("gx", "gy"), split_axis=0, concat_axis=0, axis_index_groups=side_groups)
+    moved = moved.reshape(peers, LANES)
+    outer, column, ends = call(
+        ends_kernel,
+        [((2 * DEPTH, slots), BF16), ((1, slots), F32), ((count_y, DEPTH // 2, LANES), F32)],
+        [vmem] * 3,
+        [pltpu.VMEM((4 * DEPTH, slots), BF16)],
+    )(moved, sigma, tab)
+    ends = a2a(ends, "gy", split_axis=0, concat_axis=0)
+    block, raw = call(
         grid_kernel,
-        [((CX, DEPTH, LANES), F32), ((count_y, DEPTH // 2, LANES), F32)],
-        [vmem] * 5,
-        [pltpu.VMEM((2 * DEPTH, SLOTS * peers), BF16), pltpu.VMEM((SLOTS * peers, LANES), F32)],
-    )(moved.reshape(peers, LANES), sigma, dt_high, dt_low, edge)
-    ends = a2a(ends, "gy", split_axis=0, concat_axis=0)
-    block, sums = call(
+        [((CX, DEPTH, LANES), F32), ((2, DEPTH, LANES), F32)],
+        [smem] + [vmem] * 6,
+        [pltpu.VMEM((8 * DEPTH, slots), BF16), pltpu.VMEM((slots, 2 * CY), BF16)],
+    )(x_flat, outer, column, moved, sigma, dt_high, dt_low)
+    both, sums = call(
         line_kernel,
-        [((CX, DEPTH, LANES), F32), ((NEAR, 2 * DEPTH // NEAR, LANES), F32)],
-        [smem, smem, vmem, vmem, vmem],
-    )(blocks, x_flat, ends, edge, block)
+        [((DEPTH, LANES), F32), ((NEAR, chunk, LANES), F32)],
+        [smem, vmem, vmem, vmem],
+    )(blocks, ends, edge, raw)
     sums = a2a(sums, "gx", split_axis=0, concat_axis=0, axis_index_groups=near_groups)
-    joined = call(join_kernel, [((far, 2 * DEPTH // NEAR, LANES), F32)], [smem, vmem])(blocks, sums)
+    joined = call(join_kernel, [((far, chunk, LANES), F32)], [smem, vmem])(blocks, sums)
+    joined, block = tie((joined, block))
     joined = a2a(joined, "gx", split_axis=0, concat_axis=0, axis_index_groups=far_groups)
-    carry = call(carry_kernel, [((NEAR, 2 * DEPTH // NEAR, LANES), F32)], [smem, vmem, vmem])(
-        blocks, joined, sums
-    )
+    block = call(
+        scan_kernel,
+        [((DEPTH * CX, LANES), F32)],
+        [smem, vmem, vmem, vmem],
+        [pltpu.VMEM((CX, DEPTH, LANES), F32)],
+    )(x_flat, both, edge, block)
+    carry = call(carry_kernel, [((NEAR, chunk, LANES), F32)], [smem, vmem, vmem])(blocks, joined, sums)
     carry = a2a(carry, "gx", split_axis=0, concat_axis=0, axis_index_groups=near_groups)
-    out = call(
+    rows = DEPTH * CX // NEAR
+    out = pl.pallas_call(
         final_kernel,
-        [((DEPTH * CX, LANES), F32)],
-        [smem, vmem, vmem],
-        [pltpu.VMEM((CX, DEPTH, LANES), F32)],
-    )(x_flat, carry, block)
+        grid=(NEAR,),
+        out_shape=jax.ShapeDtypeStruct((DEPTH * CX, LANES), F32),
+        in_specs=[pl.BlockSpec((1, chunk, LANES), lambda k: (k, 0, 0)), vmem, vmem],
+        out_specs=pl.BlockSpec((rows, LANES), lambda k: (k, 0)),
+        compiler_params=params(),
+    )(carry, x_ends, block)
     return out.reshape(FIELDS, LEVELS, CX, CY)
 
 

time: 130 us -> 117 us (0.900)
  waiting for transfers between devices: 29.9 us -> 9.74 us
  blocking collectives: 36.1 us -> 47.5 us
  Pallas kernels: 26.7 us -> 24.3 us
  starting transfers between devices: 28.5 us -> 27 us
    all_to_all x2, waiting for transfers between devices: 22 us -> 8.51 us  [the longest x1 7.9 us: local(): a2a(send.reshape(far, peers // far, LANES), 'gx', split_axis=0, concat_ax...]
    all_to_all x1, blocking collectives: 10.3 us -> 21.8 us  [local(): a2a(moved.transpose(1, 0, 2), ('gx', 'gy'), split_axis=0, concat_axis=0,...]
    all_to_all x1, waiting for transfers between devices: 7.94 us -> 1.22 us  [local(): ends = a2a(ends, 'gy', split_axis=0, concat_axis=0)]
    pallas_call x7 -> x9, Pallas kernels: 26.7 us -> 24.3 us  [the longest x1 6.96 us: local(): call(grid_kernel, [((CX, DEPTH, LANES), F32), ((2, DEPTH, LANES), F32)],...]
    all_to_all x1, starting transfers between devices: 4.99 us -> 3.55 us  [local(): ends = a2a(ends, 'gy', split_axis=0, concat_axis=0)]
    unnamed x12 -> x10, local copies, waits for them, and re-layouts: 3.65 us -> 3.65 us
  transfers between devices with their start and end apart: 3 -> 3, of which waited for: 3 -> 3; matrix products, arithmetic and copies ran while one was open for 2% -> 3% of each run, Pallas kernels for 4% -> 14%
where the time goes in v1:
time: 117 us; the launch traced here: 116 us
  blocking collectives  47.5 us (41%)
  starting transfers between devices  27 us (23%)
  Pallas kernels  24.3 us (21%)
  waiting for transfers between devices  9.74 us (8%)
  local copies, waits for them, and re-layouts  5.36 us (5%)
  other arithmetic  1.63 us (1%)
    all_to_all x1, blocking collectives, local(): a2a(moved.transpose(1, 0, 2), ('gx', 'gy'), split_axis=0, concat_axis=0,...  21.8 us
    all_to_all x1, blocking collectives, local(): a2a(joined, 'gx', split_axis=0, concat_axis=0, axis_index_groups=far_groups)  17.5 us
    all_to_all x1, starting transfers between devices, local(): a2a(send.reshape(far, peers // far, LANES), 'gx', split_axis=0, concat_ax...  15.6 us
    all_to_all x1, blocking collectives, local(): a2a(sums, 'gx', split_axis=0, concat_axis=0, axis_index_groups=near_groups)  8.25 us
    all_to_all x1, waiting for transfers between devices, local(): a2a(send.reshape(far, peers // far, LANES), 'gx', split_axis=0, concat_ax...  7.9 us
    all_to_all x1, starting transfers between devices, local(): a2a(carry, 'gx', split_axis=0, concat_axis=0, axis_index_groups=near_groups)  7.85 us
    pallas_call x1, Pallas kernels, local(): call(grid_kernel, [((CX, DEPTH, LANES), F32), ((2, DEPTH, LANES), F32)],...  6.96 us
    pallas_call x1, Pallas kernels, local(): call(coef_kernel, [((CY, CY), BF16), ((CY, CY), BF16), ((2, CY, LANES), F...  6.08 us
  transfers between devices with their start and end apart: 3, of which 3 were waited for; matrix products, arithmetic and copies ran while one was open for 3% of the time, Pallas kernels for 14%

profile of v1, /device:TPU:1, one launch (start us, length us, event | category | flops | bytes accessed | tf_op | source)
XLA Modules:
  0.0 116.4 jit_solution(17814800340785577154)
XLA Ops:
  0.7 0.0 copy-start
  0.7 0.8 copy-done
  1.5 0.0 copy-start.1
  1.5 0.8 copy-done.1
  2.3 0.0 copy-start.2
  2.3 0.7 copy-done.2
  2.9 0.0 copy-start.3
  2.9 0.7 copy-done.3
  3.6 0.0 copy-start.4
  3.6 0.7 copy-done.4
  4.3 2.1 %shard_map.91 = f32[512,128]{1,0:T(8,128)} custom-call(s32[1]{0:T(128)S(6)} %copy.27.live_ref, f32[1,1024]{1,0:T(1,128)S(1)} %bitcast.25, s32[1,1024]{1,0:T(1,128)S(1)} %bitcast.26, s32[1,1024]{1,0:T(1,128)S(1)} %bitcast.27, f32[6,1024]{1,0:T(8,128)S(1)} %copy-done.1, f32[16,1024]{1,0:T(8,128)S(1)} %copy-done), custom_call_target="tpu_custom_call" | custom-call | tf_op jit(solution)/shard_map/pallas_call | solution.py:414
  6.4 15.6 %all-to-all-start = ((f32[8,64,128]{2,1,0:T(8,128)}), f32[8,64,128]{2,1,0:T(8,128)S(1)}, u32[]{:S(2)}, u32[]{:S(2)}) async-start(f32[8,64,128]{2,1,0:T(8,128)} %bitcast.3), calls=%async_computation | async-start | bytes 524288 | tf_op jit(solution)/shard_map/all_to_all | solution.py:436
  22.1 0.8 broadcast_in_dim.7
  22.8 0.7 broadcast_subtract_fusion.1
  23.5 0.1 fusion.7
  23.6 0.1 pad_maximum_fusion.5
  23.7 0.1 stack.48
  23.8 0.1 stack.49
  23.8 0.1 stack.50
  23.9 0.1 copy.22
  24.0 0.1 copy.23
  24.1 0.1 copy.24
  24.2 0.7 fusion.4
  24.9 0.1 fusion.6
  24.9 0.1 fusion.2
  25.1 0.1 copy.25.y_cols
  25.2 6.1 %shard_map.92 = (bf16[128,128]{1,0:T(8,128)(2,1)S(1)}, bf16[128,128]{1,0:T(8,128)(2,1)S(1)}, f32[2,128,128]{2,1,0:T(8,128)S(1)}, f32[8,128]{1,0:T(8,128)S(1)}, f...) custom-call(f32[3072]{0:T(1024)S(1)} %reshape.45.x_flat, f32[6144]{0:T(1024)S(1)} %reshape.46.y_flat, ...), custom_call_target="tpu_custom_call" | custom-call | tf_op jit(solution)/shard_map/pallas_call | solution.py:441
  31.3 7.9 %all-to-all-done = f32[8,64,128]{2,1,0:T(8,128)S(1)} async-done(((f32[8,64,128]{2,1,0:T(8,128)}), f32[8,64,128]{2,1,0:T(8,128)S(1)}, u32[]{:S(2)}, u32[]{:S(2)}) %all-to-all-start) | async-done | bytes 262176 | tf_op jit(solution)/shard_map/all_to_all | solution.py:436
  39.2 0.1 broadcast_in_dim.8.sigma_ref
  39.3 0.2 copy.26
  39.5 21.8 %all_to_all.30 = f32[64,8,128]{2,1,0:T(8,128)S(1)} all-to-all(f32[64,8,128]{2,1,0:T(8,128)S(1)} %copy.26), channel_id=1, replica_groups={{0,1,2,3,4,5,6,7,8,9,10,11,12,13,14,15,16,17,18,19,20,21,22,23,24,25,26..., dimensions={0} | all-to-all | bytes 524288 | tf_op jit(solution)/shard_map/all_to_all | solution.py:462
  61.2 1.7 %shard_map.93 = (bf16[192,2048]{1,0:T(8,128)(2,1)S(1)}, f32[1,2048]{1,0:T(1,128)S(1)}, f32[16,48,128]{2,1,0:T(8,128)}) custom-call(f32[512,128]{1,0:T(8,128)S(1)} %bitcast.23, f32[96,128]{1,0:T(8,128)S(1)} %broadcast_in_dim.8.sigma_ref, f32[2,128,128]{2,1,0:T(8,128)S(1)} %get-tuple-element.37.tab_ref), custom_call_target="tpu_custom_call" | custom-call | tf_op jit(solution)/shard_map/pallas_call | solution.py:464
  63.0 3.6 %all-to-all-start.2 = ((f32[16,48,128]{2,1,0:T(8,128)}), f32[16,48,128]{2,1,0:T(8,128)S(1)}, u32[]{:S(2)}, u32[]{:S(2)}) async-start(f32[16,48,128]{2,1,0:T(8,128)} %get-tuple-element.38), calls=%async_computation.2 | async-start | bytes 786432 | tf_op jit(solution)/shard_map/all_to_all | solution.py:470
  66.5 7.0 %shard_map.94 = (f32[32,96,128]{2,1,0:T(8,128)S(1)}, f32[2,96,128]{2,1,0:T(8,128)S(1)}) custom-call(f32[3072]{0:T(1024)S(1)} %reshape.45.x_flat, bf16[192,2048]{1,0:T(8,128)(2,1)S(1)} %get-tuple-element.40.outer_ref, f32[1,2048]{1,0:T(1,128)S(1)} %get-tuple-element.41.column_ref, f32[512,128]{1,0:T(8,128)S(1)} %bitcast.24, ...), custom_call_target="tpu_custom_call" | custom-call | tf_op jit(solution)/shard_map/pallas_call | solution.py:471
  73.5 1.2 %all-to-all-done.2.ends_ref = f32[16,48,128]{2,1,0:T(8,128)S(1)} async-done(((f32[16,48,128]{2,1,0:T(8,128)}), f32[16,48,128]{2,1,0:T(8,128)S(1)}, u32[]{:S(2)}, u32[]{:S(2)}) %all-to-all-start.2) | async-done | bytes 393248 | tf_op jit(solution)/shard_map/all_to_all | solution.py:470
  74.7 1.0 shard_map.95
  75.7 8.2 %all_to_all.31.sums_ref = f32[4,48,128]{2,1,0:T(8,128)S(1)} all-to-all(f32[4,48,128]{2,1,0:T(8,128)S(1)} %get-tuple-element.45), channel_id=1, replica_groups={{0,16,32,48},{64,80,96,112},{128,144,160,176},{192,208,224,240},{256,27..., dimensions={0} | all-to-all | bytes 196608 | tf_op jit(solution)/shard_map/all_to_all | solution.py:482
  84.0 0.6 shard_map.96
  84.6 17.5 %all_to_all.32.joined_ref = f32[8,48,128]{2,1,0:T(8,128)S(1)} all-to-all(f32[8,48,128]{2,1,0:T(8,128)S(1)} %shard_map.96), channel_id=1, replica_groups={{0,64,128,192,256,320,384,448},{16,80,144,208,272,336,400,464},{32,96,1..., dimensions={0} | all-to-all | bytes 393216 | tf_op jit(solution)/shard_map/all_to_all | solution.py:485
  102.1 1.4 %shard_map.97 = f32[4,48,128]{2,1,0:T(8,128)} custom-call(f32[8,128]{1,0:T(8,128)S(1)} %get-tuple-element.34.block_tab, f32[8,48,128]{2,1,0:T(8,128)S(1)} %all_to_all.32.joined_ref, f32[4,48,128]{2,1,0:T(8,128)S(1)} %all_to_all.31.sums_ref), custom_call_target="tpu_custom_call" | custom-call | tf_op jit(solution)/shard_map/pallas_call | solution.py:492
  103.4 7.8 %all-to-all-start.5 = ((f32[4,48,128]{2,1,0:T(8,128)}), f32[4,48,128]{2,1,0:T(8,128)S(1)}, u32[]{:S(2)}, u32[]{:S(2)}) async-start(f32[4,48,128]{2,1,0:T(8,128)} %shard_map.97), calls=%async_computation.5 | async-start | bytes 196608 | tf_op jit(solution)/shard_map/all_to_all | solution.py:493
  111.3 2.7 %shard_map.98.block_ref = f32[3072,128]{1,0:T(8,128)S(1)} custom-call(f32[3072]{0:T(1024)S(1)} %reshape.45.x_flat, f32[96,128]{1,0:T(8,128)S(1)} %get-tuple-element.49.both_ref, f32[8,128]{1,0:T(8,128)S(1)} %get-tuple-element.39.edge_ref, f32[32,96,128]{2,1,0:T(8,128)S(1)} %get-tuple-element.50.block_ref), custom_call_target="tpu_custom_call" | custom-call | tf_op jit(solution)/shard_map/pallas_call | solution.py:486
  114.0 0.6 all-to-all-done.5.carry_ref
  114.6 1.7 %shard_map.99 = f32[3072,128]{1,0:T(8,128)} custom-call(f32[4,48,128]{2,1,0:T(8,128)S(1)} %all-to-all-done.5.carry_ref, f32[64,128]{1,0:T(8,128)S(1)} %get-tuple-element.48.ends_ref, f32[3072,128]{1,0:T(8,128)S(1)} %shard_map.98.block_ref), custom_call_target="tpu_custom_call" | custom-call | tf_op jit(solution)/shard_map/pallas_call | solution.py:495
  (6 shorter events, 0.1 us)
Async XLA Ops:
  0.7 0.8 copy-start
  1.5 0.8 copy-start.1
  2.3 0.7 copy-start.2
  2.9 0.7 copy-start.3
  3.6 0.7 copy-start.4
  6.4 32.8 %all-to-all-start = ((f32[8,64,128]{2,1,0:T(8,128)}), f32[8,64,128]{2,1,0:T(8,128)S(1)}, u32[]{:S(2)}, u32[]{:S(2)}) async-start(f32[8,64,128]{2,1,0:T(8,128)} %bitcast.3), calls=%async_computation | async-start | bytes 524288 | tf_op jit(solution)/shard_map/all_to_all | solution.py:436
  63.0 11.7 %all-to-all-start.2 = ((f32[16,48,128]{2,1,0:T(8,128)}), f32[16,48,128]{2,1,0:T(8,128)S(1)}, u32[]{:S(2)}, u32[]{:S(2)}) async-start(f32[16,48,128]{2,1,0:T(8,128)} %get-tuple-element.38), calls=%async_computation.2 | async-start | bytes 786432 | tf_op jit(solution)/shard_map/all_to_all | solution.py:470
  103.4 11.2 %all-to-all-start.5 = ((f32[4,48,128]{2,1,0:T(8,128)}), f32[4,48,128]{2,1,0:T(8,128)S(1)}, u32[]{:S(2)}, u32[]{:S(2)}) async-start(f32[4,48,128]{2,1,0:T(8,128)} %shard_map.97), calls=%async_computation.5 | async-start | bytes 196608 | tf_op jit(solution)/shard_map/all_to_all | solution.py:493

commit v2 on v1

--- a/solution.py
+++ b/solution.py
@@ -14,14 +14,17 @@
 LEVELS = 16
 DEPTH = FIELDS * LEVELS
 SLOTS = 4
-WIDTH = 32
+WIDTH = 24
 CX = 32
 CY = 128
 NEAR = 4
+NX_GROUPS = 8
+NY_BLOCKS = 16
 
 params = functools.partial(pltpu.CompilerParams, vmem_limit_bytes=48 * 1024 * 1024)
 vmem = pl.BlockSpec(memory_space=pltpu.VMEM)
 smem = pl.BlockSpec(memory_space=pltpu.SMEM)
+hbm = pl.BlockSpec(memory_space=pltpu.HBM)
 
 
 def iota(shape, dim):
@@ -41,7 +44,14 @@
     return lax.dot_general(left, right, (((1,), (0,)), ((), ())), preferred_element_type=F32)
 
 
-def pack_kernel(live_ref, resid_ref, dest_ref, column_ref, geometry_ref, beam_ref, send_ref):
+def pack_kernel(live_ref, *refs):
+    sources, (send_ref, *buffers, sems) = refs[:5], refs[5:]
+    copies = [pltpu.make_async_copy(src, buf, sems.at[k]) for k, (src, buf) in enumerate(zip(sources, buffers))]
+    for copy in copies:
+        copy.start()
+    for copy in copies:
+        copy.wait()
+    resid_ref, dest_ref, column_ref, geometry_ref, beam_ref = buffers
     bins = resid_ref.shape[1]
     peers = send_ref.shape[0]
     dest = dest_ref[...]
@@ -171,7 +181,7 @@
     edge_ref[3:4] = row_start
 
 
-def ends_kernel(recv_ref, sigma_ref, tab_ref, outer_out, column_out, ends_out, outer):
+def ends_kernel(scalars, recv_ref, sigma_ref, tab_ref, outer_out, column_out, ends_out, outer):
     sources = recv_ref.shape[0]
     turned = recv_ref[...].T
     weights = [jnp.concatenate([tab_ref[c]] * (sources // LANES), axis=1) for c in range(2)]
@@ -200,15 +210,17 @@
     sigma = sigma_ref[...]
     fore = (summed[:DEPTH] + summed[DEPTH : 2 * DEPTH]) * sigma
     back = (summed[2 * DEPTH : 3 * DEPTH] + summed[3 * DEPTH :]) * sigma
-    half = DEPTH // 2
-    lane = iota((half, LANES), 1)
-    both = jnp.where(
-        lane < 64,
-        jnp.where(lane < 32, fore[:half], back[:half]),
-        jnp.where(lane < 96, fore[half:], back[half:]),
-    )
+    own = lax.axis_index("gy")
+    back = back + scalars[4, own] * fore
+    rows = DEPTH // 4
+    quarter = iota((rows, LANES), 1) // CX
+    fore_row, back_row = fore[:rows], back[:rows]
+    for q in range(1, 4):
+        at = slice(q * rows, (q + 1) * rows)
+        fore_row = jnp.where(quarter == q, fore[at], fore_row)
+        back_row = jnp.where(quarter == q, back[at], back_row)
     for j in range(ends_out.shape[0]):
-        ends_out[j] = both
+        ends_out[j] = jnp.where(own <= j, fore_row, back_row)
 
 
 def grid_kernel(x_flat, outer_ref, column_ref, recv_ref, sigma_ref, dt_high, dt_low, block_out, sums_out, masked, hit):
@@ -256,23 +268,24 @@
     sums_out[1] = begin
 
 
-def line_kernel(block_tab, ends_ref, edge_ref, raw_ref, both_out, sums_out):
-    own_y = lax.axis_index("gy")
-    count, half, _ = ends_ref.shape
-    zero = jnp.zeros((half, LANES), F32)
-    fore, fore_own, fores = zero, zero, []
-    for j in range(count):
-        fores.append(fore)
-        fore_own = jnp.where(own_y == j, fore, fore_own)
-        fore = ends_ref[j] + block_tab[3, j] * fore
-    back, back_own = zero, zero
-    for j in reversed(range(count)):
-        back_own = jnp.where(own_y == j, back, back_own)
-        back = ends_ref[j] + block_tab[5, j] * pltpu.roll(fores[j], CX, 1) + block_tab[4, j] * back
-    both = jnp.where(iota((half, LANES), 1) % 64 < CX, fore_own, back_own)
-    both = jnp.concatenate([both, pltpu.roll(both, 64, 1)], axis=0)
+def line_kernel(block_tab, scalars, ends_ref, edge_ref, raw_ref, both_out, sums_out):
+    own = lax.axis_index("gy")
+    count, rows, _ = ends_ref.shape
+    fore = jnp.zeros((rows, LANES), F32)
+    for j in range(count - 1):
+        fore = jnp.where(j < own, ends_ref[j] + block_tab[3, j] * fore, fore)
+    back = jnp.zeros((rows, LANES), F32)
+    for j in reversed(range(1, count)):
+        back = jnp.where(j > own, ends_ref[j] + block_tab[4, j] * back, back)
+    back = back + scalars[3, own + 1] * (ends_ref[own] + block_tab[3, own] * fore)
+    lane = iota((DEPTH, LANES), 1)
+    parts = []
+    for q in range(4):
+        left = fore if q == 0 else pltpu.roll(fore, LANES - q * CX, 1)
+        right = back if q == 1 else pltpu.roll(back, (LANES - q * CX + CX) % LANES, 1)
+        parts.append(jnp.where(lane[:rows] < CX, left, right))
+    both = jnp.concatenate(parts, axis=0)
     both_out[...] = both
-    lane = iota((DEPTH, LANES), 1)
     edge_fore = edge_ref[0:1]
     edge_back = edge_ref[1:2]
     rows = DEPTH // NEAR
@@ -302,8 +315,34 @@
         out_ref[pl.ds(x, DEPTH, stride=CX), :] = x_flat[2 * length + first + x] * back
 
 
-def join_kernel(block_tab, sums_ref, joined_out):
-    start = lax.axis_index("gx") // NEAR * NEAR
+def chain_kernel(block_tab, out):
+    groups = NX_GROUPS
+    zero, one = jnp.float32(0.0), jnp.float32(1.0)
+    out[2, groups] = zero
+    for g in reversed(range(groups)):
+        entries = [one]
+        for k in range(NEAR):
+            entries.append(entries[-1] * block_tab[0, g * NEAR + k])
+        gamma, beta = zero, one
+        for k in reversed(range(NEAR)):
+            step = block_tab[1, g * NEAR + k]
+            gamma = block_tab[2, g * NEAR + k] * entries[k] + step * gamma
+            beta = beta * step
+        out[0, g] = entries[NEAR]
+        out[1, g] = beta
+        out[5, g] = beta * out[2, g + 1]
+        out[2, g] = gamma + beta * entries[NEAR] * out[2, g + 1]
+    blocks = NY_BLOCKS
+    out[3, blocks] = zero
+    for j in reversed(range(blocks)):
+        beta = block_tab[4, j]
+        out[4, j] = beta * out[3, j + 1]
+        out[3, j] = block_tab[5, j] + beta * block_tab[3, j] * out[3, j + 1]
+
+
+def join_kernel(block_tab, scalars, sums_ref, joined_out):
+    own = lax.axis_index("gx") // NEAR
+    start = own * NEAR
     rows = sums_ref.shape[1] // 2
     fore = jnp.zeros((rows, LANES), F32)
     fores = []
@@ -317,37 +356,23 @@
             + block_tab[2, start + k] * fores[k]
             + block_tab[1, start + k] * back
         )
+    back = back + scalars[5, own] * fore
     for g in range(joined_out.shape[0]):
-        joined_out[g, :rows] = fore
-        joined_out[g, rows:] = back
-
-
-def carry_kernel(block_tab, joined_ref, sums_ref, carry_out):
+        joined_out[g] = jnp.where(own <= g, fore, back)
+
+
+def carry_kernel(block_tab, scalars, joined_ref, sums_ref, carry_out):
     own = lax.axis_index("gx") // NEAR
     start = own * NEAR
-    groups = joined_ref.shape[0]
-    rows = sums_ref.shape[1] // 2
-    zero = jnp.zeros((rows, LANES), F32)
-    fore, fore_own, fores, betas, gammas = zero, zero, [], [], []
-    for g in range(groups):
-        entries = [jnp.float32(1.0)]
-        for k in range(NEAR):
-            entries.append(entries[-1] * block_tab[0, g * NEAR + k])
-        gamma, beta = jnp.float32(0.0), jnp.float32(1.0)
-        for k in reversed(range(NEAR)):
-            b = block_tab[1, g * NEAR + k]
-            gamma = block_tab[2, g * NEAR + k] * entries[k] + b * gamma
-            beta = beta * b
-        gammas.append(gamma)
-        betas.append(beta)
-        fores.append(fore)
-        fore_own = jnp.where(own == g, fore, fore_own)
-        fore = joined_ref[g, :rows] + entries[NEAR] * fore
-    back, back_own = zero, zero
-    for g in reversed(range(groups)):
-        back_own = jnp.where(own == g, back, back_own)
-        back = joined_ref[g, rows:] + gammas[g] * fores[g] + betas[g] * back
-    fore, back, fores = fore_own, back_own, []
+    groups, rows, _ = joined_ref.shape
+    fore = jnp.zeros((rows, LANES), F32)
+    for g in range(groups - 1):
+        fore = jnp.where(g < own, joined_ref[g] + scalars[0, g] * fore, fore)
+    back = jnp.zeros((rows, LANES), F32)
+    for g in reversed(range(1, groups)):
+        back = jnp.where(g > own, joined_ref[g] + scalars[1, g] * back, back)
+    back = back + scalars[2, own + 1] * (joined_ref[own] + scalars[0, own] * fore)
+    fores = []
     for k in range(NEAR):
         carry_out[k, :rows] = fore
         fores.append(fore)
@@ -408,32 +433,28 @@
     a2a = functools.partial(lax.all_to_all, tiled=True)
     tie = lax.optimization_barrier
 
-    def whole(*shape):
-        return pl.BlockSpec(shape, lambda k: (0,) * len(shape))
-
-    send = pl.pallas_call(
+    row = (1, bins)
+    send = call(
         pack_kernel,
-        grid=(1,),
-        out_shape=jax.ShapeDtypeStruct((peers, LANES), F32),
-        in_specs=[
-            smem,
-            whole(1, bins),
-            whole(1, bins),
-            whole(1, bins),
-            whole(FIELDS, bins),
-            whole(LEVELS, bins),
+        [((peers, SLOTS * WIDTH), F32)],
+        [smem] + [hbm] * 5,
+        [
+            pltpu.VMEM(row, F32),
+            pltpu.VMEM(row, I32),
+            pltpu.VMEM(row, I32),
+            pltpu.VMEM((FIELDS, bins), F32),
+            pltpu.VMEM((LEVELS, bins), F32),
+            pltpu.SemaphoreType.DMA((5,)),
         ],
-        out_specs=whole(peers, LANES),
-        compiler_params=params(),
     )(
         live_count,
-        bin_resid.reshape(1, bins),
-        dest_device.reshape(1, bins),
-        dest_column.reshape(1, bins),
+        bin_resid.reshape(row),
+        dest_device.reshape(row),
+        dest_column.reshape(row),
         geometry,
         beam_weight,
     )
-    moved = a2a(send.reshape(far, peers // far, LANES), "gx", split_axis=0, concat_axis=0, axis_index_groups=far_groups)
+    moved = a2a(send.reshape(far, peers // far, SLOTS * WIDTH), "gx", split_axis=0, concat_axis=0, axis_index_groups=far_groups)
     tab_x = table(x_gap)
     tab_y = table(y_gap)
     x_flat = tab_x.reshape(-1)
@@ -457,16 +478,23 @@
         tab_y.reshape(3, count_y, CY).transpose(0, 2, 1),
         tab_y.reshape(3, count_y, CY),
     )
-    moved, coefs, sigma = tie((moved, coefs, sigma))
+    scalars = pl.pallas_call(
+        chain_kernel,
+        out_shape=jax.ShapeDtypeStruct((6, LANES), F32),
+        in_specs=[smem],
+        out_specs=smem,
+        compiler_params=params(),
+    )(coefs[4])
+    moved, coefs, sigma, scalars = tie((moved, coefs, sigma, scalars))
     dt_high, dt_low, tab, edge, blocks, x_ends = coefs
     moved = a2a(moved.transpose(1, 0, 2), ("gx", "gy"), split_axis=0, concat_axis=0, axis_index_groups=side_groups)
-    moved = moved.reshape(peers, LANES)
+    moved = moved.reshape(peers, SLOTS * WIDTH)
     outer, column, ends = call(
         ends_kernel,
-        [((2 * DEPTH, slots), BF16), ((1, slots), F32), ((count_y, DEPTH // 2, LANES), F32)],
-        [vmem] * 3,
+        [((2 * DEPTH, slots), BF16), ((1, slots), F32), ((count_y, DEPTH // 4, LANES), F32)],
+        [smem] + [vmem] * 3,
         [pltpu.VMEM((4 * DEPTH, slots), BF16)],
-    )(moved, sigma, tab)
+    )(scalars, moved, sigma, tab)
     ends = a2a(ends, "gy", split_axis=0, concat_axis=0)
     block, raw = call(
         grid_kernel,
@@ -477,10 +505,10 @@
     both, sums = call(
         line_kernel,
         [((DEPTH, LANES), F32), ((NEAR, chunk, LANES), F32)],
-        [smem, vmem, vmem, vmem],
-    )(blocks, ends, edge, raw)
+        [smem, smem, vmem, vmem, vmem],
+    )(blocks, scalars, ends, edge, raw)
     sums = a2a(sums, "gx", split_axis=0, concat_axis=0, axis_index_groups=near_groups)
-    joined = call(join_kernel, [((far, chunk, LANES), F32)], [smem, vmem])(blocks, sums)
+    joined = call(join_kernel, [((far, chunk // 2, LANES), F32)], [smem, smem, vmem])(blocks, scalars, sums)
     joined, block = tie((joined, block))
     joined = a2a(joined, "gx", split_axis=0, concat_axis=0, axis_index_groups=far_groups)
     block = call(
@@ -489,7 +517,10 @@
         [smem, vmem, vmem, vmem],
         [pltpu.VMEM((CX, DEPTH, LANES), F32)],
     )(x_flat, both, edge, block)
-    carry = call(carry_kernel, [((NEAR, chunk, LANES), F32)], [smem, vmem, vmem])(blocks, joined, sums)
+    joined, block = tie((joined, block))
+    carry = call(carry_kernel, [((NEAR, chunk, LANES), F32)], [smem, smem, vmem, vmem])(
+        blocks, scalars, joined, sums
+    )
     carry = a2a(carry, "gx", split_axis=0, concat_axis=0, axis_index_groups=near_groups)
     rows = DEPTH * CX // NEAR
     out = pl.pallas_call(

time: 117 us -> 112 us (0.957)
  blocking collectives: 47.5 us -> 38 us
  waiting for transfers between devices: 9.74 us -> 16.6 us
  starting transfers between devices: 27 us -> 22.5 us
  Pallas kernels: 24.3 us -> 26.4 us
    all_to_all x1, blocking collectives: 17.5 us -> 8.51 us  [local(): a2a(carry, 'gx', split_axis=0, concat_axis=0, axis_index_groups=near_groups)]
    all_to_all x2, waiting for transfers between devices: 8.51 us -> 16.4 us  [the longest x1 9.88 us: local(): a2a(joined, 'gx', split_axis=0, concat_axis=0, axis_index_groups=far_groups)]
    all_to_all x2, starting transfers between devices: 23.5 us -> 19 us  [the longest x1 15.7 us: local(): a2a(send.reshape(far, peers // far, SLOTS * WIDTH), 'gx', split_axis=0, c...]
    pallas_call x3 -> x4, Pallas kernels: 4.11 us -> 5.73 us  [the longest x1 2.29 us: local(): call(pack_kernel, [((peers, SLOTS * WIDTH), F32)], [smem] + [hbm] * 5, [p...]
  transfers between devices with their start and end apart: 3 -> 3, of which waited for: 3 -> 3; matrix products, arithmetic and copies ran while one was open for 3% -> 3% of each run, Pallas kernels for 14% -> 15%
where the time goes in v2:
time: 112 us; the launch traced here: 111 us
  blocking collectives  38 us (34%)
  Pallas kernels  26.4 us (24%)
  starting transfers between devices  22.5 us (20%)
  waiting for transfers between devices  16.6 us (15%)
  local copies, waits for them, and re-layouts  5.36 us (5%)
  other arithmetic  1.63 us (1%)
    all_to_all x1, blocking collectives, local(): a2a(moved.transpose(1, 0, 2), ('gx', 'gy'), split_axis=0, concat_axis=0,...  21.8 us
    all_to_all x1, starting transfers between devices, local(): a2a(send.reshape(far, peers // far, SLOTS * WIDTH), 'gx', split_axis=0, c...  15.7 us
    all_to_all x1, waiting for transfers between devices, local(): a2a(joined, 'gx', split_axis=0, concat_axis=0, axis_index_groups=far_groups)  9.88 us
    all_to_all x1, blocking collectives, local(): a2a(carry, 'gx', split_axis=0, concat_axis=0, axis_index_groups=near_groups)  8.51 us
    all_to_all x1, blocking collectives, local(): a2a(sums, 'gx', split_axis=0, concat_axis=0, axis_index_groups=near_groups)  7.68 us
    pallas_call x1, Pallas kernels, local(): call(grid_kernel, [((CX, DEPTH, LANES), F32), ((2, DEPTH, LANES), F32)],...  6.96 us
    all_to_all x1, waiting for transfers between devices, local(): a2a(send.reshape(far, peers // far, SLOTS * WIDTH), 'gx', split_axis=0, c...  6.51 us
    pallas_call x1, Pallas kernels, local(): call(coef_kernel, [((CY, CY), BF16), ((CY, CY), BF16), ((2, CY, LANES), F...  6.08 us
  transfers between devices with their start and end apart: 3, of which 3 were waited for; matrix products, arithmetic and copies ran while one was open for 3% of the time, Pallas kernels for 15%

profile of v2, /device:TPU:1, one launch (start us, length us, event | category | flops | bytes accessed | tf_op | source)
XLA Modules:
  0.0 111.3 jit_solution(9328367064042693755)
XLA Ops:
  0.7 0.0 copy-start
  0.7 0.8 copy-done
  1.5 0.0 copy-start.1
  1.5 0.8 copy-done.1
  2.3 0.0 copy-start.2
  2.3 0.7 copy-done.2
  2.9 0.0 copy-start.3
  2.9 0.7 copy-done.3
  3.6 0.0 copy-start.4
  3.6 0.7 copy-done.4
  4.3 2.3 %shard_map.91 = f32[512,96]{1,0:T(8,128)} custom-call(s32[1]{0:T(128)S(6)} %copy.27.live_ref, f32[1,1024]{1,0:T(1,128)S(1)} %bitcast.25, s32[1,1024]{1,0:T(1,128)S(1)} %bitcast.26, s32[1,1024]{1,0:T(1,128)S(1)} %bitcast.27, f32[6,1024]{1,0:T(8,128)S(1)} %copy-done.1, f32[16,1024]{1,0:T(8,128)S(1)} %copy-done), custom_call_target="tpu_custom_call" | custom-call | tf_op jit(solution)/shard_map/pallas_call | solution.py:437
  6.6 15.7 %all-to-all-start = ((f32[8,64,96]{2,1,0:T(8,128)}), f32[8,64,96]{2,1,0:T(8,128)S(1)}, u32[]{:S(2)}, u32[]{:S(2)}) async-start(f32[8,64,96]{2,1,0:T(8,128)} %bitcast.3), calls=%async_computation | async-start | bytes 524288 | tf_op jit(solution)/shard_map/all_to_all | solution.py:457
  22.3 0.8 broadcast_in_dim.7
  23.0 0.7 broadcast_subtract_fusion.1
  23.7 0.1 fusion.7
  23.8 0.1 pad_maximum_fusion.5
  23.9 0.1 stack.48
  23.9 0.1 stack.49
  24.0 0.1 stack.50
  24.1 0.1 copy.22
  24.2 0.1 copy.23
  24.3 0.1 copy.24
  24.3 0.7 fusion.4
  25.1 0.1 fusion.6
  25.1 0.1 fusion.2
  25.3 0.1 copy.25.y_cols
  25.4 6.1 %shard_map.92 = (bf16[128,128]{1,0:T(8,128)(2,1)S(1)}, bf16[128,128]{1,0:T(8,128)(2,1)S(1)}, f32[2,128,128]{2,1,0:T(8,128)S(1)}, f32[8,128]{1,0:T(8,128)S(1)}, f...) custom-call(f32[3072]{0:T(1024)S(1)} %reshape.45.x_flat, f32[6144]{0:T(1024)S(1)} %reshape.46.y_flat, ...), custom_call_target="tpu_custom_call" | custom-call | tf_op jit(solution)/shard_map/pallas_call | solution.py:462
  31.5 1.4 %shard_map.93.scalars = f32[6,128]{1,0:T(8,128)S(1)} custom-call(f32[8,128]{1,0:T(8,128)S(1)} %get-tuple-element.37.block_tab), custom_call_target="tpu_custom_call" | custom-call | tf_op jit(solution)/shard_map/pallas_call | solution.py:481
  32.9 6.5 %all-to-all-done = f32[8,64,96]{2,1,0:T(8,128)S(1)} async-done(((f32[8,64,96]{2,1,0:T(8,128)}), f32[8,64,96]{2,1,0:T(8,128)S(1)}, u32[]{:S(2)}, u32[]{:S(2)}) %all-to-all-start) | async-done | bytes 196640 | tf_op jit(solution)/shard_map/all_to_all | solution.py:457
  39.4 0.1 broadcast_in_dim.8.sigma_ref
  39.5 0.2 copy.26
  39.7 21.8 %all_to_all.30 = f32[64,8,96]{2,1,0:T(8,128)S(1)} all-to-all(f32[64,8,96]{2,1,0:T(8,128)S(1)} %copy.26), channel_id=1, replica_groups={{0,1,2,3,4,5,6,7,8,9,10,11,12,13,14,15,16,17,18,19,20,21,22,23,24,25,26..., dimensions={0} | all-to-all | bytes 393216 | tf_op jit(solution)/shard_map/all_to_all | solution.py:490
  61.4 2.3 %shard_map.94 = (bf16[192,2048]{1,0:T(8,128)(2,1)S(1)}, f32[1,2048]{1,0:T(1,128)S(1)}, f32[16,24,128]{2,1,0:T(8,128)}) custom-call(f32[6,128]{1,0:T(8,128)S(1)} %shard_map.93.scalars, f32[512,96]{1,0:T(8,128)S(1)} %bitcast.23, f32[96,128]{1,0:T(8,128)S(1)} %broadcast_in_dim.8.sigma_ref, f32[2,128,128]{2,1,0:T(8,128)S(1)} %get-tuple-element.41.tab_ref), custom_call_target="tpu_custom_call" | custom-call | tf_op jit(solution)/shard_map/pallas_call | solution.py:492
  63.7 3.5 %all-to-all-start.2 = ((f32[16,24,128]{2,1,0:T(8,128)}), f32[16,24,128]{2,1,0:T(8,128)S(1)}, u32[]{:S(2)}, u32[]{:S(2)}) async-start(f32[16,24,128]{2,1,0:T(8,128)} %get-tuple-element.42), calls=%async_computation.2 | async-start | bytes 393216 | tf_op jit(solution)/shard_map/all_to_all | solution.py:498
  67.2 7.0 %shard_map.95 = (f32[32,96,128]{2,1,0:T(8,128)S(1)}, f32[2,96,128]{2,1,0:T(8,128)S(1)}) custom-call(f32[3072]{0:T(1024)S(1)} %reshape.45.x_flat, bf16[192,2048]{1,0:T(8,128)(2,1)S(1)} %get-tuple-element.44.outer_ref, f32[1,2048]{1,0:T(1,128)S(1)} %get-tuple-element.45.column_ref, f32[512,96]{1,0:T(8,128)S(1)} %bitcast.24, ...), custom_call_target="tpu_custom_call" | custom-call | tf_op jit(solution)/shard_map/pallas_call | solution.py:499
  74.2 0.2 all-to-all-done.2.ends_ref
  74.4 0.9 shard_map.96
  75.3 7.7 %all_to_all.31.sums_ref = f32[4,48,128]{2,1,0:T(8,128)S(1)} all-to-all(f32[4,48,128]{2,1,0:T(8,128)S(1)} %get-tuple-element.49), channel_id=1, replica_groups={{0,16,32,48},{64,80,96,112},{128,144,160,176},{192,208,224,240},{256,27..., dimensions={0} | all-to-all | bytes 196608 | tf_op jit(solution)/shard_map/all_to_all | solution.py:510
  83.0 1.3 %shard_map.97 = f32[8,24,128]{2,1,0:T(8,128)} custom-call(f32[8,128]{1,0:T(8,128)S(1)} %get-tuple-element.37.block_tab, f32[6,128]{1,0:T(8,128)S(1)} %shard_map.93.scalars, f32[4,48,128]{2,1,0:T(8,128)S(1)} %all_to_all.31.sums_ref), custom_call_target="tpu_custom_call" | custom-call | tf_op jit(solution)/shard_map/pallas_call | solution.py:511
  84.3 3.4 %all-to-all-start.4 = ((f32[8,24,128]{2,1,0:T(8,128)}), f32[8,24,128]{2,1,0:T(8,128)S(1)}, u32[]{:S(2)}, u32[]{:S(2)}) async-start(f32[8,24,128]{2,1,0:T(8,128)} %shard_map.97), calls=%async_computation.4 | async-start | bytes 196608 | tf_op jit(solution)/shard_map/all_to_all | solution.py:513
  87.7 2.7 %shard_map.98.block_ref = f32[3072,128]{1,0:T(8,128)S(1)} custom-call(f32[3072]{0:T(1024)S(1)} %reshape.45.x_flat, f32[96,128]{1,0:T(8,128)S(1)} %get-tuple-element.52.both_ref, f32[8,128]{1,0:T(8,128)S(1)} %get-tuple-element.43.edge_ref, f32[32,96,128]{2,1,0:T(8,128)S(1)} %get-tuple-element.53.block_ref), custom_call_target="tpu_custom_call" | custom-call | tf_op jit(solution)/shard_map/pallas_call | solution.py:514
  90.4 9.9 %all-to-all-done.4.joined_ref = f32[8,24,128]{2,1,0:T(8,128)S(1)} async-done(((f32[8,24,128]{2,1,0:T(8,128)}), f32[8,24,128]{2,1,0:T(8,128)S(1)}, u32[]{:S(2)}, u32[]{:S(2)}) %all-to-all-start.4) | async-done | bytes 98336 | tf_op jit(solution)/shard_map/all_to_all | solution.py:513
  100.3 0.7 shard_map.99
  101.0 8.5 %all_to_all.32.carry_ref = f32[4,48,128]{2,1,0:T(8,128)S(1)} all-to-all(f32[4,48,128]{2,1,0:T(8,128)S(1)} %shard_map.99), channel_id=1, replica_groups={{0,16,32,48},{64,80,96,112},{128,144,160,176},{192,208,224,240},{256,27..., dimensions={0} | all-to-all | bytes 196608 | tf_op jit(solution)/shard_map/all_to_all | solution.py:524
  109.5 1.7 %shard_map.100 = f32[3072,128]{1,0:T(8,128)} custom-call(f32[4,48,128]{2,1,0:T(8,128)S(1)} %all_to_all.32.carry_ref, f32[64,128]{1,0:T(8,128)S(1)} %get-tuple-element.55.ends_ref, f32[3072,128]{1,0:T(8,128)S(1)} %shard_map.98.block_ref), custom_call_target="tpu_custom_call" | custom-call | tf_op jit(solution)/shard_map/pallas_call | solution.py:526
  (6 shorter events, 0.1 us)
Async XLA Ops:
  0.7 0.8 copy-start
  1.5 0.8 copy-start.1
  2.3 0.7 copy-start.2
  2.9 0.7 copy-start.3
  3.6 0.7 copy-start.4
  6.6 32.8 %all-to-all-start = ((f32[8,64,96]{2,1,0:T(8,128)}), f32[8,64,96]{2,1,0:T(8,128)S(1)}, u32[]{:S(2)}, u32[]{:S(2)}) async-start(f32[8,64,96]{2,1,0:T(8,128)} %bitcast.3), calls=%async_computation | async-start | bytes 524288 | tf_op jit(solution)/shard_map/all_to_all | solution.py:457
  63.7 10.7 %all-to-all-start.2 = ((f32[16,24,128]{2,1,0:T(8,128)}), f32[16,24,128]{2,1,0:T(8,128)S(1)}, u32[]{:S(2)}, u32[]{:S(2)}) async-start(f32[16,24,128]{2,1,0:T(8,128)} %get-tuple-element.42), calls=%async_computation.2 | async-start | bytes 393216 | tf_op jit(solution)/shard_map/all_to_all | solution.py:498
  84.3 16.0 %all-to-all-start.4 = ((f32[8,24,128]{2,1,0:T(8,128)}), f32[8,24,128]{2,1,0:T(8,128)S(1)}, u32[]{:S(2)}, u32[]{:S(2)}) async-start(f32[8,24,128]{2,1,0:T(8,128)} %shard_map.97), calls=%async_computation.4 | async-start | bytes 196608 | tf_op jit(solution)/shard_map/all_to_all | solution.py:513

commit v3 on v2

--- a/solution.py
+++ b/solution.py
@@ -19,9 +19,18 @@
 CY = 128
 NEAR = 4
 NX_GROUPS = 8
+NX_BLOCKS = NX_GROUPS * NEAR
 NY_BLOCKS = 16
-
-params = functools.partial(pltpu.CompilerParams, vmem_limit_bytes=48 * 1024 * 1024)
+ALPHA_X, BETA_X, GAMMA_X = 0, 32, 64
+ALPHA_Y, BETA_Y, FOLD_Y, TURN_Y = 96, 112, 128, 152
+ALPHA_G, BETA_G, FOLD_G, TURN_G = 168, 176, 184, 200
+TAB_ROWS = 208
+
+
+def params(mib=48):
+    return pltpu.CompilerParams(vmem_limit_bytes=mib * 1024 * 1024)
+
+
 vmem = pl.BlockSpec(memory_space=pltpu.VMEM)
 smem = pl.BlockSpec(memory_space=pltpu.SMEM)
 hbm = pl.BlockSpec(memory_space=pltpu.HBM)
@@ -84,7 +93,7 @@
     send_ref[...] = dot_nt(onehot, high) + (dot_nt(onehot, middle) + dot_nt(onehot, low))
 
 
-def coef_kernel(x_flat, y_flat, x_cols, y_cols, y_rows, dt_high, dt_low, tab_ref, edge_ref, block_ref, ends_ref, chain, gammas, betas):
+def coef_kernel(x_flat, y_flat, x_cols, y_cols, y_rows, mat_ref, tab_ref, edge_ref, block_ref, ends_ref, chain, gammas, betas):
     own_x = lax.axis_index("gx")
     own_y = lax.axis_index("gy")
     length = y_rows.shape[1] * LANES
@@ -168,8 +177,10 @@
     scale = y_rows[2, pl.ds(own_y, 1), :]
     filt = chain[...].T * scale
     high, low = split_two(filt)
-    dt_high[...] = high
-    dt_low[...] = low
+    mat_ref[:CY, :CY] = high
+    mat_ref[:CY, CY:] = low
+    mat_ref[CY:, :CY] = high
+    mat_ref[CY:, CY:] = jnp.zeros((CY, CY), BF16)
     scale_first = scale[:, :1]
     scale_last = scale[:, CY - 1 :]
     tab_ref[0] = jnp.broadcast_to(filt[:, CY - 1 :] / (scale_last * scale_last), (CY, LANES))
@@ -179,39 +190,59 @@
     edge_ref[1:2] = filt[CY - 1 :] * y_flat[length + first + CY - 1] / scale_last
     edge_ref[2:3] = row_tail
     edge_ref[3:4] = row_start
-
-
-def ends_kernel(scalars, recv_ref, sigma_ref, tab_ref, outer_out, column_out, ends_out, outer):
-    sources = recv_ref.shape[0]
-    turned = recv_ref[...].T
-    weights = [jnp.concatenate([tab_ref[c]] * (sources // LANES), axis=1) for c in range(2)]
-    hits = []
+    for c, row in enumerate((row_tail, row_start)):
+        tab_ref[2 + c] = jnp.broadcast_to(jnp.where(lane < CX, row, 0.0), (LANES, LANES)).T
+
+
+def weigh(turned, weights, outer):
+    sources = turned.shape[1]
     for s in range(SLOTS):
         at = slice(s * sources, (s + 1) * sources)
         base = s * WIDTH
-        beam = turned[base : base + LEVELS]
-        place = turned[base + LEVELS + FIELDS : base + LEVELS + FIELDS + 1]
-        column_out[:, at] = place
-        place = place.astype(I32)
-        on_y = iota((CY, sources), 0) == (place & (CY - 1))
-        ends = [jnp.sum(jnp.where(on_y, w, 0.0), axis=0, keepdims=True) for w in weights]
-        hits.append(jnp.where((iota((LANES, sources), 0) & (CX - 1)) == (place >> 7), 1.0, 0.0).astype(BF16))
         for f in range(FIELDS):
-            prod = beam * turned[base + LEVELS + f : base + LEVELS + f + 1]
-            rows = slice(f * LEVELS, (f + 1) * LEVELS)
-            high, low = split_two(prod)
-            outer_out[rows, at] = high
-            outer_out[DEPTH + f * LEVELS : DEPTH + (f + 1) * LEVELS, at] = low
+            prod = turned[base : base + LEVELS] * turned[base + LEVELS + f : base + LEVELS + f + 1]
             for c in range(2):
-                high, low = split_two(prod * ends[c])
-                outer[(2 * c) * DEPTH + f * LEVELS : (2 * c) * DEPTH + (f + 1) * LEVELS, at] = high
-                outer[(2 * c + 1) * DEPTH + f * LEVELS : (2 * c + 1) * DEPTH + (f + 1) * LEVELS, at] = low
+                high, low = split_two(prod * weights[s][c])
+                row = 2 * c * DEPTH + f * LEVELS
+                outer[row : row + LEVELS, at] = high
+                outer[row + DEPTH : row + DEPTH + LEVELS, at] = low
+
+
+def weighted_sums(outer, hits, sigma):
     summed = dot_nt(outer[...], jnp.concatenate(hits, axis=1))
-    sigma = sigma_ref[...]
-    fore = (summed[:DEPTH] + summed[DEPTH : 2 * DEPTH]) * sigma
-    back = (summed[2 * DEPTH : 3 * DEPTH] + summed[3 * DEPTH :]) * sigma
+    return [(summed[k : k + DEPTH] + summed[k + DEPTH : k + 2 * DEPTH]) * sigma for k in (0, 2 * DEPTH)]
+
+
+def on_lines(turned, s):
+    row = s * WIDTH + LEVELS + FIELDS
+    place = turned[row : row + 1].astype(I32)
+    on_y = iota((CY, place.shape[1]), 0) == (place & (CY - 1))
+    on_x = (iota((LANES, place.shape[1]), 0) & (CX - 1)) == (place >> 7)
+    return on_x, on_y
+
+
+def pick(on_line, column):
+    return jnp.sum(jnp.where(on_line, column, 0.0), axis=0, keepdims=True)
+
+
+def as_bits(on_line):
+    return jnp.where(on_line, 1.0, 0.0).astype(BF16)
+
+
+def ends_kernel(recv_ref, sigma_ref, tab_ref, scalars, turned_out, ends_out, outer):
+    sources = recv_ref.shape[0]
+    turned = recv_ref[...].T
+    turned_out[...] = turned
+    columns = [jnp.concatenate([tab_ref[c]] * (sources // LANES), axis=1) for c in range(2)]
+    hits, weights = [], []
+    for s in range(SLOTS):
+        on_x, on_y = on_lines(turned, s)
+        hits.append(as_bits(on_x))
+        weights.append([pick(on_y, column) for column in columns])
+    weigh(turned, weights, outer)
+    fore, back = weighted_sums(outer, hits, sigma_ref[...])
     own = lax.axis_index("gy")
-    back = back + scalars[4, own] * fore
+    back = back + scalars[pl.ds(TURN_Y + own, 1), :] * fore
     rows = DEPTH // 4
     quarter = iota((rows, LANES), 1) // CX
     fore_row, back_row = fore[:rows], back[:rows]
@@ -223,61 +254,96 @@
         ends_out[j] = jnp.where(own <= j, fore_row, back_row)
 
 
-def grid_kernel(x_flat, outer_ref, column_ref, recv_ref, sigma_ref, dt_high, dt_low, block_out, sums_out, masked, hit):
+def sums_kernel(turned_ref, sigma_ref, tab_ref, mat_ref, sums_out, outer):
+    turned = turned_ref[...]
+    sources = turned.shape[1]
+    columns = [jnp.concatenate([tab_ref[2 + c]] * (sources // LANES), axis=1) for c in range(2)]
+    hits, weights = [], []
+    for s in range(SLOTS):
+        on_x, on_y = on_lines(turned, s)
+        hits.append(as_bits(on_y))
+        weights.append([pick(on_x, column) for column in columns])
+    weigh(turned, weights, outer)
+    both = jnp.concatenate(weighted_sums(outer, hits, sigma_ref[...]), axis=0)
+    both = y_filter(both, mat_ref)
+    sums_out[0] = both[:DEPTH]
+    sums_out[1] = both[DEPTH:]
+
+
+def y_filter(values, mat_ref):
+    passed = dot_nn(jnp.concatenate(split_two(values), axis=1), mat_ref[...])
+    return passed[:, :CY] + passed[:, CY:]
+
+
+def grid_kernel(x_flat, turned_ref, recv_ref, sigma_ref, mat_ref, both_ref, edge_ref, out_ref, outer, masked, hit, scaled):
     sources = recv_ref.shape[0]
     first = lax.axis_index("gx") * CX
     length = x_flat.shape[0] // 3
     lane2 = iota((1, 2 * LANES), 1)
+    pairs = []
     for s in range(SLOTS):
-        place = s * WIDTH + LEVELS + FIELDS
+        at = slice(s * sources, (s + 1) * sources)
+        base = s * WIDTH
+        place = base + LEVELS + FIELDS
         cols = jnp.broadcast_to(recv_ref[:, place : place + 1], (sources, LANES)).astype(I32) & (2 * CY - 1)
         cols = jnp.concatenate([cols, cols], axis=1)
-        hit[s * sources : (s + 1) * sources] = jnp.where(cols == lane2, 1.0, 0.0).astype(BF16)
-    pair = column_ref[...].astype(I32) >> 8
+        hit[at] = as_bits(cols == lane2)
+        pairs.append(turned_ref[place : place + 1].astype(I32) >> 8)
+        for f in range(FIELDS):
+            high, low = split_two(
+                turned_ref[base : base + LEVELS] * turned_ref[base + LEVELS + f : base + LEVELS + f + 1]
+            )
+            outer[f * LEVELS : (f + 1) * LEVELS, at] = high
+            outer[DEPTH + f * LEVELS : DEPTH + (f + 1) * LEVELS, at] = low
+    pair = jnp.concatenate(pairs, axis=1)
     sigma = sigma_ref[...]
+    both = both_ref[...]
+    edge_fore = edge_ref[0:1]
+    edge_back = edge_ref[1:2]
+    lane = iota((DEPTH, LANES), 1)
     group = 4
 
-    def step(n, carried):
-        run, begin, weight = carried
+    def step(n, run):
         for c in range(group):
             keep = jnp.where(pair == n * group + c, 1.0, 0.0)
             keep = jnp.broadcast_to(keep, (16, keep.shape[1])).astype(BF16)
             for r in range(2 * DEPTH // 16):
                 masked[c * 2 * DEPTH + r * 16 : c * 2 * DEPTH + (r + 1) * 16] = (
-                    outer_ref[r * 16 : (r + 1) * 16] * keep
+                    outer[r * 16 : (r + 1) * 16] * keep
                 )
         summed = dot_nn(masked[...], hit[...])
         parts = []
         for c in range(group):
-            both = summed[c * 2 * DEPTH : c * 2 * DEPTH + DEPTH] + summed[c * 2 * DEPTH + DEPTH : (c + 1) * 2 * DEPTH]
-            parts += [both[:, :CY] * sigma, both[:, CY:] * sigma]
-        high, low = split_two(jnp.concatenate(parts, axis=0))
-        passed = dot_nn(high, dt_high[...]) + (dot_nn(low, dt_high[...]) + dot_nn(high, dt_low[...]))
+            total = summed[c * 2 * DEPTH : c * 2 * DEPTH + DEPTH] + summed[c * 2 * DEPTH + DEPTH : (c + 1) * 2 * DEPTH]
+            parts += [total[:, :CY] * sigma, total[:, CY:] * sigma]
+        passed = y_filter(jnp.concatenate(parts, axis=0), mat_ref)
+        turn = pltpu.roll(both, lax.rem(LANES - n * 2 * group, LANES), 1)
         for h in range(2 * group):
+            x = n * 2 * group + h
             part = passed[h * DEPTH : (h + 1) * DEPTH]
-            x = n * 2 * group + h
-            block_out[x] = part
+            part = part + turn[:, h : h + 1] * edge_fore + turn[:, CX + h : CX + h + 1] * edge_back
             run = part + jnp.where(x == 0, 0.0, x_flat[first + x]) * run
-            begin = begin + (weight * x_flat[2 * length + first + x]) * run
-            weight = weight * x_flat[length + first + x]
-        return run, begin, weight
-
-    zero = jnp.zeros((DEPTH, LANES), F32)
-    run, begin, _ = lax.fori_loop(0, CX // (2 * group), step, (zero, zero, jnp.float32(1.0)))
-    sums_out[0] = run
-    sums_out[1] = begin
-
-
-def line_kernel(block_tab, scalars, ends_ref, edge_ref, raw_ref, both_out, sums_out):
+            scaled[x] = x_flat[2 * length + first + x] * run
+        return run
+
+    lax.fori_loop(0, CX // (2 * group), step, jnp.zeros((DEPTH, LANES), F32))
+    back = jnp.zeros((DEPTH, LANES), F32)
+    for x in reversed(range(CX)):
+        back = scaled[x] if x == CX - 1 else scaled[x] + x_flat[length + first + x] * back
+        out_ref[pl.ds(x, DEPTH, stride=CX), :] = x_flat[2 * length + first + x] * back
+
+
+def line_kernel(tab, ends_ref, edge_ref, raw_ref, both_out, sums_out):
     own = lax.axis_index("gy")
     count, rows, _ = ends_ref.shape
     fore = jnp.zeros((rows, LANES), F32)
     for j in range(count - 1):
-        fore = jnp.where(j < own, ends_ref[j] + block_tab[3, j] * fore, fore)
+        fore = jnp.where(j < own, ends_ref[j] + tab[ALPHA_Y + j : ALPHA_Y + j + 1, :] * fore, fore)
     back = jnp.zeros((rows, LANES), F32)
     for j in reversed(range(1, count)):
-        back = jnp.where(j > own, ends_ref[j] + block_tab[4, j] * back, back)
-    back = back + scalars[3, own + 1] * (ends_ref[own] + block_tab[3, own] * fore)
+        back = jnp.where(j > own, ends_ref[j] + tab[BETA_Y + j : BETA_Y + j + 1, :] * back, back)
+    mine = ends_ref[own] + tab[pl.ds(ALPHA_Y + own, 1), :] * fore
+    back = back + tab[pl.ds(FOLD_Y + own + 1, 1), :] * mine
     lane = iota((DEPTH, LANES), 1)
     parts = []
     for q in range(4):
@@ -298,28 +364,19 @@
             sums_out[k, c * rows : (c + 1) * rows] = total[k * rows : (k + 1) * rows]
 
 
-def scan_kernel(x_flat, both_ref, edge_ref, block_ref, out_ref, scaled):
-    first = lax.axis_index("gx") * CX
-    length = x_flat.shape[0] // 3
-    both = both_ref[...]
-    edge_fore = edge_ref[0:1]
-    edge_back = edge_ref[1:2]
-    run = jnp.zeros((DEPTH, LANES), F32)
-    for x in range(CX):
-        part = block_ref[x] + both[:, x : x + 1] * edge_fore + both[:, CX + x : CX + x + 1] * edge_back
-        run = part if x == 0 else part + x_flat[first + x] * run
-        scaled[x] = x_flat[2 * length + first + x] * run
-    back = jnp.zeros((DEPTH, LANES), F32)
-    for x in reversed(range(CX)):
-        back = scaled[x] if x == CX - 1 else scaled[x] + x_flat[length + first + x] * back
-        out_ref[pl.ds(x, DEPTH, stride=CX), :] = x_flat[2 * length + first + x] * back
-
-
 def chain_kernel(block_tab, out):
-    groups = NX_GROUPS
     zero, one = jnp.float32(0.0), jnp.float32(1.0)
-    out[2, groups] = zero
-    for g in reversed(range(groups)):
+
+    def put(row, value):
+        out[row : row + 1, :] = jnp.full((1, LANES), value, F32)
+
+    for i in range(NX_BLOCKS):
+        put(ALPHA_X + i, block_tab[0, i])
+        put(BETA_X + i, block_tab[1, i])
+        put(GAMMA_X + i, block_tab[2, i])
+    fold = zero
+    put(FOLD_G + NX_GROUPS, fold)
+    for g in reversed(range(NX_GROUPS)):
         entries = [one]
         for k in range(NEAR):
             entries.append(entries[-1] * block_tab[0, g * NEAR + k])
@@ -328,19 +385,23 @@
             step = block_tab[1, g * NEAR + k]
             gamma = block_tab[2, g * NEAR + k] * entries[k] + step * gamma
             beta = beta * step
-        out[0, g] = entries[NEAR]
-        out[1, g] = beta
-        out[5, g] = beta * out[2, g + 1]
-        out[2, g] = gamma + beta * entries[NEAR] * out[2, g + 1]
-    blocks = NY_BLOCKS
-    out[3, blocks] = zero
-    for j in reversed(range(blocks)):
-        beta = block_tab[4, j]
-        out[4, j] = beta * out[3, j + 1]
-        out[3, j] = block_tab[5, j] + beta * block_tab[3, j] * out[3, j + 1]
-
-
-def join_kernel(block_tab, scalars, sums_ref, joined_out):
+        put(ALPHA_G + g, entries[NEAR])
+        put(BETA_G + g, beta)
+        put(TURN_G + g, beta * fold)
+        fold = gamma + beta * entries[NEAR] * fold
+        put(FOLD_G + g, fold)
+    fold = zero
+    put(FOLD_Y + NY_BLOCKS, fold)
+    for j in reversed(range(NY_BLOCKS)):
+        alpha, beta = block_tab[3, j], block_tab[4, j]
+        put(ALPHA_Y + j, alpha)
+        put(BETA_Y + j, beta)
+        put(TURN_Y + j, beta * fold)
+        fold = block_tab[5, j] + beta * alpha * fold
+        put(FOLD_Y + j, fold)
+
+
+def join_kernel(tab, sums_ref, joined_out):
     own = lax.axis_index("gx") // NEAR
     start = own * NEAR
     rows = sums_ref.shape[1] // 2
@@ -348,41 +409,42 @@
     fores = []
     for k in range(NEAR):
         fores.append(fore)
-        fore = sums_ref[k, :rows] + block_tab[0, start + k] * fore
+        fore = sums_ref[k, :rows] + tab[pl.ds(ALPHA_X + start + k, 1), :] * fore
     back = jnp.zeros((rows, LANES), F32)
     for k in reversed(range(NEAR)):
         back = (
             sums_ref[k, rows:]
-            + block_tab[2, start + k] * fores[k]
-            + block_tab[1, start + k] * back
+            + tab[pl.ds(GAMMA_X + start + k, 1), :] * fores[k]
+            + tab[pl.ds(BETA_X + start + k, 1), :] * back
         )
-    back = back + scalars[5, own] * fore
+    back = back + tab[pl.ds(TURN_G + own, 1), :] * fore
     for g in range(joined_out.shape[0]):
         joined_out[g] = jnp.where(own <= g, fore, back)
 
 
-def carry_kernel(block_tab, scalars, joined_ref, sums_ref, carry_out):
+def carry_kernel(tab, joined_ref, sums_ref, carry_out):
     own = lax.axis_index("gx") // NEAR
     start = own * NEAR
     groups, rows, _ = joined_ref.shape
     fore = jnp.zeros((rows, LANES), F32)
     for g in range(groups - 1):
-        fore = jnp.where(g < own, joined_ref[g] + scalars[0, g] * fore, fore)
+        fore = jnp.where(g < own, joined_ref[g] + tab[ALPHA_G + g : ALPHA_G + g + 1, :] * fore, fore)
     back = jnp.zeros((rows, LANES), F32)
     for g in reversed(range(1, groups)):
-        back = jnp.where(g > own, joined_ref[g] + scalars[1, g] * back, back)
-    back = back + scalars[2, own + 1] * (joined_ref[own] + scalars[0, own] * fore)
+        back = jnp.where(g > own, joined_ref[g] + tab[BETA_G + g : BETA_G + g + 1, :] * back, back)
+    mine = joined_ref[own] + tab[pl.ds(ALPHA_G + own, 1), :] * fore
+    back = back + tab[pl.ds(FOLD_G + own + 1, 1), :] * mine
     fores = []
     for k in range(NEAR):
         carry_out[k, :rows] = fore
         fores.append(fore)
-        fore = sums_ref[k, :rows] + block_tab[0, start + k] * fore
+        fore = sums_ref[k, :rows] + tab[pl.ds(ALPHA_X + start + k, 1), :] * fore
     for k in reversed(range(NEAR)):
         carry_out[k, rows:] = back
         back = (
             sums_ref[k, rows:]
-            + block_tab[2, start + k] * fores[k]
-            + block_tab[1, start + k] * back
+            + tab[pl.ds(GAMMA_X + start + k, 1), :] * fores[k]
+            + tab[pl.ds(BETA_X + start + k, 1), :] * back
         )
 
 
@@ -407,7 +469,7 @@
     return jnp.stack([prior, later, jnp.sqrt(gap * (2.0 - gap))])
 
 
-def call(kernel, outs, specs, scratch=()):
+def call(kernel, outs, specs, scratch=(), mib=48):
     shapes = tuple(jax.ShapeDtypeStruct(s, t) for s, t in outs)
     return pl.pallas_call(
         kernel,
@@ -415,7 +477,7 @@
         in_specs=specs,
         out_specs=(vmem,) * len(shapes) if len(shapes) > 1 else vmem,
         scratch_shapes=scratch,
-        compiler_params=params(),
+        compiler_params=params(mib),
     )
 
 
@@ -446,6 +508,7 @@
             pltpu.VMEM((LEVELS, bins), F32),
             pltpu.SemaphoreType.DMA((5,)),
         ],
+        60,
     )(
         live_count,
         bin_resid.reshape(row),
@@ -462,9 +525,8 @@
     coefs = call(
         coef_kernel,
         [
-            ((CY, CY), BF16),
-            ((CY, CY), BF16),
-            ((2, CY, LANES), F32),
+            ((2 * CY, 2 * CY), BF16),
+            ((4, CY, LANES), F32),
             ((8, LANES), F32),
             ((8, LANES), F32),
             ((2 * CX, LANES), F32),
@@ -478,49 +540,42 @@
         tab_y.reshape(3, count_y, CY).transpose(0, 2, 1),
         tab_y.reshape(3, count_y, CY),
     )
-    scalars = pl.pallas_call(
-        chain_kernel,
-        out_shape=jax.ShapeDtypeStruct((6, LANES), F32),
-        in_specs=[smem],
-        out_specs=smem,
-        compiler_params=params(),
-    )(coefs[4])
+    scalars = call(chain_kernel, [((TAB_ROWS, LANES), F32)], [smem])(coefs[3])
     moved, coefs, sigma, scalars = tie((moved, coefs, sigma, scalars))
-    dt_high, dt_low, tab, edge, blocks, x_ends = coefs
+    mat, tab, edge, _, x_ends = coefs
     moved = a2a(moved.transpose(1, 0, 2), ("gx", "gy"), split_axis=0, concat_axis=0, axis_index_groups=side_groups)
     moved = moved.reshape(peers, SLOTS * WIDTH)
-    outer, column, ends = call(
+    weighted = pltpu.VMEM((4 * DEPTH, slots), BF16)
+    turned, ends = call(
         ends_kernel,
-        [((2 * DEPTH, slots), BF16), ((1, slots), F32), ((count_y, DEPTH // 4, LANES), F32)],
-        [smem] + [vmem] * 3,
-        [pltpu.VMEM((4 * DEPTH, slots), BF16)],
-    )(scalars, moved, sigma, tab)
+        [((SLOTS * WIDTH, peers), F32), ((count_y, DEPTH // 4, LANES), F32)],
+        [vmem] * 4,
+        [weighted],
+    )(moved, sigma, tab, scalars)
     ends = a2a(ends, "gy", split_axis=0, concat_axis=0)
-    block, raw = call(
-        grid_kernel,
-        [((CX, DEPTH, LANES), F32), ((2, DEPTH, LANES), F32)],
-        [smem] + [vmem] * 6,
-        [pltpu.VMEM((8 * DEPTH, slots), BF16), pltpu.VMEM((slots, 2 * CY), BF16)],
-    )(x_flat, outer, column, moved, sigma, dt_high, dt_low)
+    raw = call(sums_kernel, [((2, DEPTH, LANES), F32)], [vmem] * 4, [weighted])(turned, sigma, tab, mat)
     both, sums = call(
         line_kernel,
         [((DEPTH, LANES), F32), ((NEAR, chunk, LANES), F32)],
-        [smem, smem, vmem, vmem, vmem],
-    )(blocks, scalars, ends, edge, raw)
+        [vmem] * 4,
+    )(scalars, ends, edge, raw)
     sums = a2a(sums, "gx", split_axis=0, concat_axis=0, axis_index_groups=near_groups)
-    joined = call(join_kernel, [((far, chunk // 2, LANES), F32)], [smem, smem, vmem])(blocks, scalars, sums)
-    joined, block = tie((joined, block))
+    joined = call(join_kernel, [((far, chunk // 2, LANES), F32)], [vmem, vmem])(scalars, sums)
+    joined, both = tie((joined, both))
     joined = a2a(joined, "gx", split_axis=0, concat_axis=0, axis_index_groups=far_groups)
     block = call(
-        scan_kernel,
+        grid_kernel,
         [((DEPTH * CX, LANES), F32)],
-        [smem, vmem, vmem, vmem],
-        [pltpu.VMEM((CX, DEPTH, LANES), F32)],
-    )(x_flat, both, edge, block)
+        [smem] + [vmem] * 6,
+        [
+            pltpu.VMEM((2 * DEPTH, slots), BF16),
+            pltpu.VMEM((8 * DEPTH, slots), BF16),
+            pltpu.VMEM((slots, 2 * CY), BF16),
+            pltpu.VMEM((CX, DEPTH, LANES), F32),
+        ],
+    )(x_flat, turned, moved, sigma, mat, both, edge)
     joined, block = tie((joined, block))
-    carry = call(carry_kernel, [((NEAR, chunk, LANES), F32)], [smem, smem, vmem, vmem])(
-        blocks, scalars, joined, sums
-    )
+    carry = call(carry_kernel, [((NEAR, chunk, LANES), F32)], [vmem] * 3)(scalars, joined, sums)
     carry = a2a(carry, "gx", split_axis=0, concat_axis=0, axis_index_groups=near_groups)
     rows = DEPTH * CX // NEAR
     out = pl.pallas_call(

time: 112 us -> 106 us (0.946)
  local copies, waits for them, and re-layouts: 5.36 us -> 1.72 us
  Pallas kernels: 26.4 us -> 23.1 us
  waiting for transfers between devices: 16.6 us -> 18 us
    all_to_all x1, waiting for transfers between devices: 0.18 us -> 6.2 us  [local(): ends = a2a(ends, 'gy', split_axis=0, concat_axis=0)]
    all_to_all x1, waiting for transfers between devices: 9.88 us -> 4.79 us  [local(): a2a(joined, 'gx', split_axis=0, concat_axis=0, axis_index_groups=far_groups)]
    unnamed x10 -> x0, local copies, waits for them, and re-layouts: 3.65 us -> none
    pallas_call x7, Pallas kernels: 21.5 us -> 18 us  [the longest x1 7.82 us: local(): call(grid_kernel, [((DEPTH * CX, LANES), F32)], [smem] + [vmem] * 6, [plt...]
where the time goes in v3:
time: 106 us
  blocking collectives  38 us (36%)
  Pallas kernels  23.1 us (22%)
  starting transfers between devices  22.5 us (21%)
  waiting for transfers between devices  18 us (17%)
  local copies, waits for them, and re-layouts  1.72 us (2%)
  other arithmetic  1.63 us (2%)
    all_to_all x1, blocking collectives, local(): a2a(moved.transpose(1, 0, 2), ('gx', 'gy'), split_axis=0, concat_axis=0,...  21.8 us
    all_to_all x1, starting transfers between devices, local(): a2a(send.reshape(far, peers // far, SLOTS * WIDTH), 'gx', split_axis=0, c...  15.7 us
    all_to_all x1, blocking collectives, local(): a2a(carry, 'gx', split_axis=0, concat_axis=0, axis_index_groups=near_groups)  8.51 us
    pallas_call x1, Pallas kernels, local(): call(grid_kernel, [((DEPTH * CX, LANES), F32)], [smem] + [vmem] * 6, [plt...  7.82 us
    all_to_all x1, blocking collectives, local(): a2a(sums, 'gx', split_axis=0, concat_axis=0, axis_index_groups=near_groups)  7.68 us
    all_to_all x1, waiting for transfers between devices, local(): a2a(send.reshape(far, peers // far, SLOTS * WIDTH), 'gx', split_axis=0, c...  7 us
    pallas_call x1, Pallas kernels, local(): call(coef_kernel, [((2 * CY, 2 * CY), BF16), ((4, CY, LANES), F32), ((8,...  6.21 us
    all_to_all x1, waiting for transfers between devices, local(): ends = a2a(ends, 'gy', split_axis=0, concat_axis=0)  6.2 us
  transfers between devices with their start and end apart: 3, of which 3 were waited for; matrix products, arithmetic and copies ran while one was open for 3% of the time, Pallas kernels for 15%

profile of v3, /device:TPU:1, one launch (start us, length us, event | category | flops | bytes accessed | tf_op | source)
XLA Modules:
  0.0 105.7 jit_solution(2426758662419773657)
XLA Ops:
  0.7 3.1 %shard_map.91 = f32[512,96]{1,0:T(8,128)} custom-call(s32[1]{0:T(128)S(6)} %copy.27.live_ref, f32[1,1024]{1,0:T(1,128)} %bitcast.33, s32[1,1024]{1,0:T(1,128)} %bitcast.34, s32[1,1024]{1,0:T(1,128)} %bitcast.35, f32[6,1024]{1,0:T(8,128)} %refs_3_.1, f32[16,1024]{1,0:T(8,128)} %refs_4_.1), custom_call_target="tpu_custom_call" | custom-call | tf_op jit(solution)/shard_map/pallas_call | solution.py:499
  3.7 15.7 %all-to-all-start = ((f32[8,64,96]{2,1,0:T(8,128)}), f32[8,64,96]{2,1,0:T(8,128)S(1)}, u32[]{:S(2)}, u32[]{:S(2)}) async-start(f32[8,64,96]{2,1,0:T(8,128)} %bitcast.26), calls=%async_computation | async-start | bytes 524288 | tf_op jit(solution)/shard_map/all_to_all | solution.py:520
  19.4 0.8 broadcast_in_dim.7
  20.1 0.7 broadcast_subtract_fusion.1
  20.8 0.1 fusion.7
  20.9 0.1 pad_maximum_fusion.5
  21.0 0.1 stack.48
  21.1 0.1 stack.49
  21.1 0.1 stack.50
  21.2 0.1 copy.22
  21.3 0.1 copy.23
  21.4 0.1 copy.24
  21.5 0.7 fusion.4
  22.2 0.1 fusion.6
  22.3 0.1 fusion.2
  22.4 0.1 copy.25.y_cols
  22.6 6.2 %shard_map.92 = (bf16[256,256]{1,0:T(8,128)(2,1)S(1)}, f32[4,128,128]{2,1,0:T(8,128)S(1)}, f32[8,128]{1,0:T(8,128)S(1)}, f32[8,128]{1,0:T(8,128)S(1)}, f32[64,128]{1,0:T(8,128)S(1)}) custom-call(f32[3072]{0:T(1024)S(1)} %reshape.45.x_flat, f32[6144]{0:T(1024)S(1)} %reshape.46.y_flat, f32[3,32,32]{2,1,0:T(8,128)S(1)} %maximum_bitcast_fusion.x_cols, ...), custom_call_target="tpu_custom_call" | custom-call | tf_op jit(solution)/shard_map/pallas_call | solution.py:525
  28.8 0.8 shard_map.93.scalars.tab
  29.5 7.0 %all-to-all-done = f32[8,64,96]{2,1,0:T(8,128)S(1)} async-done(((f32[8,64,96]{2,1,0:T(8,128)}), f32[8,64,96]{2,1,0:T(8,128)S(1)}, u32[]{:S(2)}, u32[]{:S(2)}) %all-to-all-start) | async-done | bytes 196640 | tf_op jit(solution)/shard_map/all_to_all | solution.py:520
  36.5 0.1 broadcast_in_dim.8.sigma_ref
  36.6 0.2 copy.26
  36.8 21.8 %all_to_all.30 = f32[64,8,96]{2,1,0:T(8,128)S(1)} all-to-all(f32[64,8,96]{2,1,0:T(8,128)S(1)} %copy.26), channel_id=1, replica_groups={{0,1,2,3,4,5,6,7,8,9,10,11,12,13,14,15,16,17,18,19,20,21,22,23,24,25,26..., dimensions={0} | all-to-all | bytes 393216 | tf_op jit(solution)/shard_map/all_to_all | solution.py:546
  58.6 1.6 %shard_map.94 = (f32[96,512]{1,0:T(8,128)S(1)}, f32[16,24,128]{2,1,0:T(8,128)}) custom-call(f32[512,96]{1,0:T(8,128)S(1)} %bitcast.23, f32[96,128]{1,0:T(8,128)S(1)} %broadcast_in_dim.8.sigma_ref, f32[4,128,128]{2,1,0:T(8,128)S(1)} %get-tuple-element.33.tab_ref, f32[208,128]{1,0:T(8,128)S(1)} %shard_map.93.scalars.tab), custom_call_target="tpu_custom_call" | custom-call | tf_op jit(solution)/shard_map/pallas_call | solution.py:549
  60.1 3.5 %all-to-all-start.2 = ((f32[16,24,128]{2,1,0:T(8,128)}), f32[16,24,128]{2,1,0:T(8,128)S(1)}, u32[]{:S(2)}, u32[]{:S(2)}) async-start(f32[16,24,128]{2,1,0:T(8,128)} %get-tuple-element.34), calls=%async_computation.2 | async-start | bytes 393216 | tf_op jit(solution)/shard_map/all_to_all | solution.py:555
  63.6 0.9 shard_map.95.raw_ref
  64.6 6.2 %all-to-all-done.2.ends_ref = f32[16,24,128]{2,1,0:T(8,128)S(1)} async-done(((f32[16,24,128]{2,1,0:T(8,128)}), f32[16,24,128]{2,1,0:T(8,128)S(1)}, u32[]{:S(2)}, u32[]{:S(2)}) %all-to-all-start.2) | async-done | bytes 196640 | tf_op jit(solution)/shard_map/all_to_all | solution.py:555
  70.8 0.2 shard_map.96
  71.0 7.7 %all_to_all.31.sums_ref = f32[4,48,128]{2,1,0:T(8,128)S(1)} all-to-all(f32[4,48,128]{2,1,0:T(8,128)S(1)} %get-tuple-element.38), channel_id=1, replica_groups={{0,16,32,48},{64,80,96,112},{128,144,160,176},{192,208,224,240},{256,27..., dimensions={0} | all-to-all | bytes 196608 | tf_op jit(solution)/shard_map/all_to_all | solution.py:562
  78.7 0.7 shard_map.97
  79.4 3.4 %all-to-all-start.4 = ((f32[8,24,128]{2,1,0:T(8,128)}), f32[8,24,128]{2,1,0:T(8,128)S(1)}, u32[]{:S(2)}, u32[]{:S(2)}) async-start(f32[8,24,128]{2,1,0:T(8,128)} %shard_map.97), calls=%async_computation.4 | async-start | bytes 196608 | tf_op jit(solution)/shard_map/all_to_all | solution.py:565
  82.8 7.8 %shard_map.98.block_ref = f32[3072,128]{1,0:T(8,128)S(1)} custom-call(f32[3072]{0:T(1024)S(1)} %reshape.45.x_flat, f32[96,512]{1,0:T(8,128)S(1)} %get-tuple-element.36.turned_ref, f32[512,96]{1,0:T(8,128)S(1)} %bitcast.24, f32[96,128]{1,0:T(8,128)S(1)} %broadcast_in_dim.8.sigma_ref, bf16[256,256]{1,0:T(8,128)(2,1)S(1)} %get-tuple-element.37.mat_ref, ...), custom_call_target="tpu_custom_call" | custom-call | tf_op jit(solution)/shard_map/pallas_call | solution.py:566
  90.6 4.8 %all-to-all-done.4.joined_ref = f32[8,24,128]{2,1,0:T(8,128)S(1)} async-done(((f32[8,24,128]{2,1,0:T(8,128)}), f32[8,24,128]{2,1,0:T(8,128)S(1)}, u32[]{:S(2)}, u32[]{:S(2)}) %all-to-all-start.4) | async-done | bytes 98336 | tf_op jit(solution)/shard_map/all_to_all | solution.py:565
  95.4 8.5 %all_to_all.32.carry_ref = f32[4,48,128]{2,1,0:T(8,128)S(1)} all-to-all(f32[4,48,128]{2,1,0:T(8,128)S(1)} %shard_map.99), channel_id=1, replica_groups={{0,16,32,48},{64,80,96,112},{128,144,160,176},{192,208,224,240},{256,27..., dimensions={0} | all-to-all | bytes 196608 | tf_op jit(solution)/shard_map/all_to_all | solution.py:579
  103.9 1.7 %shard_map.100 = f32[3072,128]{1,0:T(8,128)} custom-call(f32[4,48,128]{2,1,0:T(8,128)S(1)} %all_to_all.32.carry_ref, f32[64,128]{1,0:T(8,128)S(1)} %get-tuple-element.43.ends_ref, f32[3072,128]{1,0:T(8,128)S(1)} %shard_map.98.block_ref), custom_call_target="tpu_custom_call" | custom-call | tf_op jit(solution)/shard_map/pallas_call | solution.py:581
  (7 shorter events, 0.1 us)
Async XLA Ops:
  3.7 32.8 %all-to-all-start = ((f32[8,64,96]{2,1,0:T(8,128)}), f32[8,64,96]{2,1,0:T(8,128)S(1)}, u32[]{:S(2)}, u32[]{:S(2)}) async-start(f32[8,64,96]{2,1,0:T(8,128)} %bitcast.26), calls=%async_computation | async-start | bytes 524288 | tf_op jit(solution)/shard_map/all_to_all | solution.py:520
  60.1 10.7 %all-to-all-start.2 = ((f32[16,24,128]{2,1,0:T(8,128)}), f32[16,24,128]{2,1,0:T(8,128)S(1)}, u32[]{:S(2)}, u32[]{:S(2)}) async-start(f32[16,24,128]{2,1,0:T(8,128)} %get-tuple-element.34), calls=%async_computation.2 | async-start | bytes 393216 | tf_op jit(solution)/shard_map/all_to_all | solution.py:555
  79.4 16.0 %all-to-all-start.4 = ((f32[8,24,128]{2,1,0:T(8,128)}), f32[8,24,128]{2,1,0:T(8,128)S(1)}, u32[]{:S(2)}, u32[]{:S(2)}) async-start(f32[8,24,128]{2,1,0:T(8,128)} %shard_map.97), calls=%async_computation.4 | async-start | bytes 196608 | tf_op jit(solution)/shard_map/all_to_all | solution.py:565

commit v4 on v3

--- a/solution.py
+++ b/solution.py
@@ -18,6 +18,8 @@
 CX = 32
 CY = 128
 NEAR = 4
+GROUP = 4
+EARLY = 1
 NX_GROUPS = 8
 NX_BLOCKS = NX_GROUPS * NEAR
 NY_BLOCKS = 16
@@ -85,12 +87,10 @@
         axis=0,
     )
     spread = jnp.concatenate([jnp.where(rank == float(s), payload, 0.0) for s in range(SLOTS)], axis=0)
-    high = spread.astype(BF16)
-    rest = spread - high.astype(F32)
-    middle = rest.astype(BF16)
-    low = (rest - middle.astype(F32)).astype(BF16)
+    high, low = split_two(spread)
     onehot = jnp.where(iota((peers, bins), 0) == dest, 1.0, 0.0).astype(BF16)
-    send_ref[...] = dot_nt(onehot, high) + (dot_nt(onehot, middle) + dot_nt(onehot, low))
+    both = dot_nt(onehot, jnp.concatenate([high, low], axis=0))
+    send_ref[...] = both[:, : SLOTS * WIDTH] + both[:, SLOTS * WIDTH :]
 
 
 def coef_kernel(x_flat, y_flat, x_cols, y_cols, y_rows, mat_ref, tab_ref, edge_ref, block_ref, ends_ref, chain, gammas, betas):
@@ -194,80 +194,53 @@
         tab_ref[2 + c] = jnp.broadcast_to(jnp.where(lane < CX, row, 0.0), (LANES, LANES)).T
 
 
-def weigh(turned, weights, outer):
-    sources = turned.shape[1]
-    for s in range(SLOTS):
-        at = slice(s * sources, (s + 1) * sources)
-        base = s * WIDTH
-        for f in range(FIELDS):
-            prod = turned[base : base + LEVELS] * turned[base + LEVELS + f : base + LEVELS + f + 1]
-            for c in range(2):
-                high, low = split_two(prod * weights[s][c])
-                row = 2 * c * DEPTH + f * LEVELS
-                outer[row : row + LEVELS, at] = high
-                outer[row + DEPTH : row + DEPTH + LEVELS, at] = low
-
-
-def weighted_sums(outer, hits, sigma):
-    summed = dot_nt(outer[...], jnp.concatenate(hits, axis=1))
-    return [(summed[k : k + DEPTH] + summed[k + DEPTH : k + 2 * DEPTH]) * sigma for k in (0, 2 * DEPTH)]
-
-
 def on_lines(turned, s):
     row = s * WIDTH + LEVELS + FIELDS
     place = turned[row : row + 1].astype(I32)
     on_y = iota((CY, place.shape[1]), 0) == (place & (CY - 1))
-    on_x = (iota((LANES, place.shape[1]), 0) & (CX - 1)) == (place >> 7)
+    on_x = iota((CX, place.shape[1]), 0) == (place >> 7)
     return on_x, on_y
 
 
-def pick(on_line, column):
-    return jnp.sum(jnp.where(on_line, column, 0.0), axis=0, keepdims=True)
-
-
-def as_bits(on_line):
-    return jnp.where(on_line, 1.0, 0.0).astype(BF16)
-
-
-def ends_kernel(recv_ref, sigma_ref, tab_ref, scalars, turned_out, ends_out, outer):
+def weighted_hits(on_line, on_cross, columns):
+    rows = []
+    for column in columns:
+        weight = jnp.sum(jnp.where(on_cross, column, 0.0), axis=0, keepdims=True)
+        rows += list(split_two(jnp.where(on_line, weight, 0.0)))
+    return jnp.concatenate(rows, axis=0)
+
+
+def ends_kernel(recv_ref, sigma_ref, tab_ref, scalars, turned_out, outer_out, ends_out):
     sources = recv_ref.shape[0]
     turned = recv_ref[...].T
     turned_out[...] = turned
     columns = [jnp.concatenate([tab_ref[c]] * (sources // LANES), axis=1) for c in range(2)]
-    hits, weights = [], []
+    hits = []
     for s in range(SLOTS):
+        at = slice(s * sources, (s + 1) * sources)
+        base = s * WIDTH
         on_x, on_y = on_lines(turned, s)
-        hits.append(as_bits(on_x))
-        weights.append([pick(on_y, column) for column in columns])
-    weigh(turned, weights, outer)
-    fore, back = weighted_sums(outer, hits, sigma_ref[...])
+        hits.append(weighted_hits(on_x, on_y, columns))
+        for f in range(FIELDS):
+            high, low = split_two(
+                turned[base : base + LEVELS] * turned[base + LEVELS + f : base + LEVELS + f + 1]
+            )
+            outer_out[f * LEVELS : (f + 1) * LEVELS, at] = high
+            outer_out[DEPTH + f * LEVELS : DEPTH + (f + 1) * LEVELS, at] = low
+    summed = dot_nt(outer_out[...], jnp.concatenate(hits, axis=1))
+    summed = (summed[:DEPTH] + summed[DEPTH:]) * sigma_ref[...]
+    summed = summed + pltpu.roll(summed, LANES - CX, 1)
     own = lax.axis_index("gy")
-    back = back + scalars[pl.ds(TURN_Y + own, 1), :] * fore
+    folded = pltpu.roll(summed, 64, 1) + scalars[pl.ds(TURN_Y + own, 1), :] * summed
     rows = DEPTH // 4
     quarter = iota((rows, LANES), 1) // CX
-    fore_row, back_row = fore[:rows], back[:rows]
+    fore_row, back_row = summed[:rows], folded[:rows]
     for q in range(1, 4):
         at = slice(q * rows, (q + 1) * rows)
-        fore_row = jnp.where(quarter == q, fore[at], fore_row)
-        back_row = jnp.where(quarter == q, back[at], back_row)
+        fore_row = jnp.where(quarter == q, pltpu.roll(summed[at], q * CX, 1), fore_row)
+        back_row = jnp.where(quarter == q, pltpu.roll(folded[at], q * CX, 1), back_row)
     for j in range(ends_out.shape[0]):
         ends_out[j] = jnp.where(own <= j, fore_row, back_row)
-
-
-def sums_kernel(turned_ref, sigma_ref, tab_ref, mat_ref, sums_out, outer):
-    turned = turned_ref[...]
-    sources = turned.shape[1]
-    columns = [jnp.concatenate([tab_ref[2 + c]] * (sources // LANES), axis=1) for c in range(2)]
-    hits, weights = [], []
-    for s in range(SLOTS):
-        on_x, on_y = on_lines(turned, s)
-        hits.append(as_bits(on_y))
-        weights.append([pick(on_x, column) for column in columns])
-    weigh(turned, weights, outer)
-    both = jnp.concatenate(weighted_sums(outer, hits, sigma_ref[...]), axis=0)
-    both = y_filter(both, mat_ref)
-    sums_out[0] = both[:DEPTH]
-    sums_out[1] = both[DEPTH:]
 
 
 def y_filter(values, mat_ref):
@@ -275,37 +248,10 @@
     return passed[:, :CY] + passed[:, CY:]
 
 
-def grid_kernel(x_flat, turned_ref, recv_ref, sigma_ref, mat_ref, both_ref, edge_ref, out_ref, outer, masked, hit, scaled):
-    sources = recv_ref.shape[0]
-    first = lax.axis_index("gx") * CX
-    length = x_flat.shape[0] // 3
-    lane2 = iota((1, 2 * LANES), 1)
-    pairs = []
-    for s in range(SLOTS):
-        at = slice(s * sources, (s + 1) * sources)
-        base = s * WIDTH
-        place = base + LEVELS + FIELDS
-        cols = jnp.broadcast_to(recv_ref[:, place : place + 1], (sources, LANES)).astype(I32) & (2 * CY - 1)
-        cols = jnp.concatenate([cols, cols], axis=1)
-        hit[at] = as_bits(cols == lane2)
-        pairs.append(turned_ref[place : place + 1].astype(I32) >> 8)
-        for f in range(FIELDS):
-            high, low = split_two(
-                turned_ref[base : base + LEVELS] * turned_ref[base + LEVELS + f : base + LEVELS + f + 1]
-            )
-            outer[f * LEVELS : (f + 1) * LEVELS, at] = high
-            outer[DEPTH + f * LEVELS : DEPTH + (f + 1) * LEVELS, at] = low
-    pair = jnp.concatenate(pairs, axis=1)
-    sigma = sigma_ref[...]
-    both = both_ref[...]
-    edge_fore = edge_ref[0:1]
-    edge_back = edge_ref[1:2]
-    lane = iota((DEPTH, LANES), 1)
-    group = 4
-
-    def step(n, run):
-        for c in range(group):
-            keep = jnp.where(pair == n * group + c, 1.0, 0.0)
+def place_steps(begin, end, pair, outer, hit, sigma, mat_ref, masked, emit):
+    def step(n, carried):
+        for c in range(GROUP):
+            keep = jnp.where(pair == n * GROUP + c, 1.0, 0.0)
             keep = jnp.broadcast_to(keep, (16, keep.shape[1])).astype(BF16)
             for r in range(2 * DEPTH // 16):
                 masked[c * 2 * DEPTH + r * 16 : c * 2 * DEPTH + (r + 1) * 16] = (
@@ -313,20 +259,78 @@
                 )
         summed = dot_nn(masked[...], hit[...])
         parts = []
-        for c in range(group):
-            total = summed[c * 2 * DEPTH : c * 2 * DEPTH + DEPTH] + summed[c * 2 * DEPTH + DEPTH : (c + 1) * 2 * DEPTH]
+        for c in range(GROUP):
+            base = c * 2 * DEPTH
+            total = summed[base : base + DEPTH] + summed[base + DEPTH : base + 2 * DEPTH]
             parts += [total[:, :CY] * sigma, total[:, CY:] * sigma]
         passed = y_filter(jnp.concatenate(parts, axis=0), mat_ref)
-        turn = pltpu.roll(both, lax.rem(LANES - n * 2 * group, LANES), 1)
-        for h in range(2 * group):
-            x = n * 2 * group + h
+        return emit(n, passed, carried)
+
+    return functools.partial(lax.fori_loop, begin, end, step)
+
+
+def pairs_of(turned_ref):
+    rows = [turned_ref[s * WIDTH + LEVELS + FIELDS : s * WIDTH + LEVELS + FIELDS + 1] for s in range(SLOTS)]
+    return jnp.concatenate(rows, axis=1).astype(I32) >> 8
+
+
+def early_kernel(turned_ref, outer, recv_ref, sigma_ref, tab_ref, mat_ref, sums_out, hit, block_out, masked):
+    turned = turned_ref[...]
+    sources = turned.shape[1]
+    sigma = sigma_ref[...]
+    columns = [jnp.concatenate([tab_ref[2 + c, :CX]] * (sources // LANES), axis=1) for c in range(2)]
+    hits = []
+    for s in range(SLOTS):
+        on_x, on_y = on_lines(turned, s)
+        hits.append(weighted_hits(on_y, on_x, columns))
+    summed = dot_nt(outer[...], jnp.concatenate(hits, axis=1))
+    summed = summed[:DEPTH] + summed[DEPTH:]
+    both = [(summed[:, k : k + CY] + summed[:, k + CY : k + 2 * CY]) * sigma for k in (0, 2 * CY)]
+    both = y_filter(jnp.concatenate(both, axis=0), mat_ref)
+    sums_out[0] = both[:DEPTH]
+    sums_out[1] = both[DEPTH:]
+
+    lane2 = iota((1, 2 * LANES), 1)
+    for s in range(SLOTS):
+        place = s * WIDTH + LEVELS + FIELDS
+        cols = jnp.broadcast_to(recv_ref[:, place : place + 1], (sources, LANES)).astype(I32) & (2 * CY - 1)
+        cols = jnp.concatenate([cols, cols], axis=1)
+        hit[s * sources : (s + 1) * sources] = jnp.where(cols == lane2, 1.0, 0.0).astype(BF16)
+
+    def emit(n, passed, carried):
+        for h in range(2 * GROUP):
+            block_out[n * 2 * GROUP + h] = passed[h * DEPTH : (h + 1) * DEPTH]
+        return carried
+
+    place_steps(0, EARLY, pairs_of(turned_ref), outer, hit, sigma, mat_ref, masked, emit)(0)
+
+
+def grid_kernel(x_flat, turned_ref, outer, hit, block_ref, sigma_ref, mat_ref, both_ref, edge_ref, out_ref, masked, scaled):
+    first = lax.axis_index("gx") * CX
+    length = x_flat.shape[0] // 3
+    both = both_ref[...]
+    edge_fore = edge_ref[0:1]
+    edge_back = edge_ref[1:2]
+
+    def advance(x, part, fore, back, run):
+        part = part + fore * edge_fore + back * edge_back
+        run = part + jnp.where(x == 0, 0.0, x_flat[first + x]) * run
+        scaled[x] = x_flat[2 * length + first + x] * run
+        return run
+
+    run = jnp.zeros((DEPTH, LANES), F32)
+    for x in range(EARLY * 2 * GROUP):
+        run = advance(x, block_ref[x], both[:, x : x + 1], both[:, CX + x : CX + x + 1], run)
+
+    def emit(n, passed, run):
+        turn = pltpu.roll(both, lax.rem(LANES - n * 2 * GROUP, LANES), 1)
+        for h in range(2 * GROUP):
             part = passed[h * DEPTH : (h + 1) * DEPTH]
-            part = part + turn[:, h : h + 1] * edge_fore + turn[:, CX + h : CX + h + 1] * edge_back
-            run = part + jnp.where(x == 0, 0.0, x_flat[first + x]) * run
-            scaled[x] = x_flat[2 * length + first + x] * run
+            run = advance(n * 2 * GROUP + h, part, turn[:, h : h + 1], turn[:, CX + h : CX + h + 1], run)
         return run
 
-    lax.fori_loop(0, CX // (2 * group), step, jnp.zeros((DEPTH, LANES), F32))
+    steps = CX // (2 * GROUP)
+    place_steps(EARLY, steps, pairs_of(turned_ref), outer, hit, sigma_ref[...], mat_ref, masked, emit)(run)
     back = jnp.zeros((DEPTH, LANES), F32)
     for x in reversed(range(CX)):
         back = scaled[x] if x == CX - 1 else scaled[x] + x_flat[length + first + x] * back
@@ -452,12 +456,13 @@
     rows = carry_ref.shape[1] // 2
     fore = ends_ref[:CX]
     back = ends_ref[CX:]
-    base = pl.program_id(0) * (rows * CX)
+    step = pl.program_id(0)
+    base = step * (rows * CX)
     for r in range(rows):
         out_ref[r * CX : (r + 1) * CX] = (
             block_ref[pl.ds(pl.multiple_of(base + r * CX, CX), CX), :]
-            + carry_ref[0, r : r + 1] * fore
-            + carry_ref[0, rows + r : rows + r + 1] * back
+            + carry_ref[step, r : r + 1] * fore
+            + carry_ref[step, rows + r : rows + r + 1] * back
         )
 
 
@@ -496,7 +501,7 @@
     tie = lax.optimization_barrier
 
     row = (1, bins)
-    send = call(
+    moved = call(
         pack_kernel,
         [((peers, SLOTS * WIDTH), F32)],
         [smem] + [hbm] * 5,
@@ -517,7 +522,6 @@
         geometry,
         beam_weight,
     )
-    moved = a2a(send.reshape(far, peers // far, SLOTS * WIDTH), "gx", split_axis=0, concat_axis=0, axis_index_groups=far_groups)
     tab_x = table(x_gap)
     tab_y = table(y_gap)
     x_flat = tab_x.reshape(-1)
@@ -541,19 +545,27 @@
         tab_y.reshape(3, count_y, CY),
     )
     scalars = call(chain_kernel, [((TAB_ROWS, LANES), F32)], [smem])(coefs[3])
+    mat, tab, edge, _, x_ends = coefs
+    moved = a2a(moved.reshape(peers, 1, SLOTS * WIDTH), ("gx", "gy"), split_axis=0, concat_axis=0)
     moved, coefs, sigma, scalars = tie((moved, coefs, sigma, scalars))
-    mat, tab, edge, _, x_ends = coefs
-    moved = a2a(moved.transpose(1, 0, 2), ("gx", "gy"), split_axis=0, concat_axis=0, axis_index_groups=side_groups)
     moved = moved.reshape(peers, SLOTS * WIDTH)
-    weighted = pltpu.VMEM((4 * DEPTH, slots), BF16)
-    turned, ends = call(
+    turned, outer, ends = call(
         ends_kernel,
-        [((SLOTS * WIDTH, peers), F32), ((count_y, DEPTH // 4, LANES), F32)],
+        [((SLOTS * WIDTH, peers), F32), ((2 * DEPTH, slots), BF16), ((count_y, DEPTH // 4, LANES), F32)],
         [vmem] * 4,
-        [weighted],
     )(moved, sigma, tab, scalars)
     ends = a2a(ends, "gy", split_axis=0, concat_axis=0)
-    raw = call(sums_kernel, [((2, DEPTH, LANES), F32)], [vmem] * 4, [weighted])(turned, sigma, tab, mat)
+    masked = pltpu.VMEM((GROUP * 2 * DEPTH, slots), BF16)
+    raw, hit, block = call(
+        early_kernel,
+        [
+            ((2, DEPTH, LANES), F32),
+            ((slots, 2 * CY), BF16),
+            ((EARLY * 2 * GROUP, DEPTH, LANES), F32),
+        ],
+        [vmem] * 6,
+        [masked],
+    )(turned, outer, moved, sigma, tab, mat)
     both, sums = call(
         line_kernel,
         [((DEPTH, LANES), F32), ((NEAR, chunk, LANES), F32)],
@@ -566,14 +578,9 @@
     block = call(
         grid_kernel,
         [((DEPTH * CX, LANES), F32)],
-        [smem] + [vmem] * 6,
-        [
-            pltpu.VMEM((2 * DEPTH, slots), BF16),
-            pltpu.VMEM((8 * DEPTH, slots), BF16),
-            pltpu.VMEM((slots, 2 * CY), BF16),
-            pltpu.VMEM((CX, DEPTH, LANES), F32),
-        ],
-    )(x_flat, turned, moved, sigma, mat, both, edge)
+        [smem] + [vmem] * 8,
+        [masked, pltpu.VMEM((CX, DEPTH, LANES), F32)],
+    )(x_flat, turned, outer, hit, block, sigma, mat, both, edge)
     joined, block = tie((joined, block))
     carry = call(carry_kernel, [((NEAR, chunk, LANES), F32)], [vmem] * 3)(scalars, joined, sums)
     carry = a2a(carry, "gx", split_axis=0, concat_axis=0, axis_index_groups=near_groups)
@@ -582,7 +589,7 @@
         final_kernel,
         grid=(NEAR,),
         out_shape=jax.ShapeDtypeStruct((DEPTH * CX, LANES), F32),
-        in_specs=[pl.BlockSpec((1, chunk, LANES), lambda k: (k, 0, 0)), vmem, vmem],
+        in_specs=[vmem] * 3,
         out_specs=pl.BlockSpec((rows, LANES), lambda k: (k, 0)),
         compiler_params=params(),
     )(carry, x_ends, block)

time: 106 us -> 105 us (level)
  blocking collectives: 38 us -> 16.2 us
  starting transfers between devices: 22.5 us -> 31.8 us
  local copies, waits for them, and re-layouts: 1.72 us -> 9.72 us
  waiting for transfers between devices: 18 us -> 20.8 us
    all_to_all x1 -> x0, blocking collectives: 21.8 us -> none  [local(): a2a(moved.transpose(1, 0, 2), ('gx', 'gy'), split_axis=0, concat_axis=0,...]
    unnamed x0 -> x34, local copies, waits for them, and re-layouts: none -> 8.83 us
    all_to_all x1, starting transfers between devices: 15.7 us -> 24.3 us  [local(): a2a(moved.reshape(peers, 1, SLOTS * WIDTH), ('gx', 'gy'), split_axis=0, c...]
    all_to_all x1, waiting for transfers between devices: 7 us -> 14.8 us  [local(): a2a(moved.reshape(peers, 1, SLOTS * WIDTH), ('gx', 'gy'), split_axis=0, c...]
    all_to_all x1, waiting for transfers between devices: 4.79 us -> 1.84 us  [local(): a2a(joined, 'gx', split_axis=0, concat_axis=0, axis_index_groups=far_groups)]
    all_to_all x1, waiting for transfers between devices: 6.2 us -> 4.21 us  [local(): ends = a2a(ends, 'gy', split_axis=0, concat_axis=0)]
  transfers between devices with their start and end apart: 3 -> 3, of which waited for: 3 -> 3; matrix products, arithmetic and copies ran while one was open for 3% -> 2% of each run, Pallas kernels for 15% -> 15%
where the time goes in v4:
time: 105 us; the launch traced here: 104 us
  starting transfers between devices  31.8 us (30%)
  Pallas kernels  23.3 us (22%)
  waiting for transfers between devices  20.8 us (20%)
  blocking collectives  16.2 us (15%)
  local copies, waits for them, and re-layouts  9.72 us (9%)
  other arithmetic  1.62 us (2%)
    all_to_all x1, starting transfers between devices, local(): a2a(moved.reshape(peers, 1, SLOTS * WIDTH), ('gx', 'gy'), split_axis=0, c...  24.3 us
    all_to_all x1, waiting for transfers between devices, local(): a2a(moved.reshape(peers, 1, SLOTS * WIDTH), ('gx', 'gy'), split_axis=0, c...  14.8 us
    unnamed x34, local copies, waits for them, and re-layouts  8.83 us
    all_to_all x1, blocking collectives, local(): a2a(carry, 'gx', split_axis=0, concat_axis=0, axis_index_groups=near_groups)  8.54 us
    all_to_all x1, blocking collectives, local(): a2a(sums, 'gx', split_axis=0, concat_axis=0, axis_index_groups=near_groups)  7.65 us
    pallas_call x1, Pallas kernels, local(): call(grid_kernel, [((DEPTH * CX, LANES), F32)], [smem] + [vmem] * 8, [mas...  6.4 us
    pallas_call x1, Pallas kernels, local(): call(coef_kernel, [((2 * CY, 2 * CY), BF16), ((4, CY, LANES), F32), ((8,...  6.21 us
    all_to_all x1, waiting for transfers between devices, local(): ends = a2a(ends, 'gy', split_axis=0, concat_axis=0)  4.21 us
  transfers between devices with their start and end apart: 3, of which 3 were waited for; matrix products, arithmetic and copies ran while one was open for 2% of the time, Pallas kernels for 15%

profile of v4, /device:TPU:1, one launch (start us, length us, event | category | flops | bytes accessed | tf_op | source)
XLA Modules:
  0.0 104.4 jit_solution(18126287501406274321)
XLA Ops:
  0.0 0.0 copy-start.16
  0.7 2.6 %shard_map.91 = f32[512,96]{1,0:T(8,128)} custom-call(s32[1]{0:T(128)S(6)} %copy.20.live_ref, f32[1,1024]{1,0:T(1,128)} %bitcast.33, s32[1,1024]{1,0:T(1,128)} %bitcast.34, s32[1,1024]{1,0:T(1,128)} %bitcast.35, f32[6,1024]{1,0:T(8,128)} %refs_3_.1, f32[16,1024]{1,0:T(8,128)} %refs_4_.1), custom_call_target="tpu_custom_call" | custom-call | tf_op jit(solution)/shard_map/pallas_call | solution.py:504
  3.2 24.3 %all-to-all-start = ((f32[512,1,96]{2,1,0:T(1,128)}), f32[512,1,96]{2,1,0:T(1,128)S(1)}, u32[]{:S(2)}, u32[]{:S(2)}) async-start(f32[512,1,96]{2,1,0:T(1,128)} %bitcast.26), calls=%async_computation | async-start | bytes 524288 | tf_op jit(solution)/shard_map/all_to_all | solution.py:549
  27.6 0.7 broadcast_subtract_fusion.1
  28.2 0.1 fusion.7
  28.3 0.1 stack.50
  28.4 0.1 pad_maximum_fusion.5
  28.5 0.1 stack.49
  28.5 0.1 stack.48
  28.7 0.7 fusion.4
  29.4 0.1 fusion.6
  29.4 0.1 fusion.2
  29.6 0.1 copy.18
  29.7 0.1 copy.17
  29.7 0.1 copy.16
  29.8 0.1 copy.19.y_cols
  29.9 0.0 copy-done.16
  30.0 0.1 broadcast_in_dim.7
  30.0 6.2 %shard_map.92 = (bf16[256,256]{1,0:T(8,128)(2,1)S(1)}, f32[4,128,128]{2,1,0:T(8,128)S(1)}, f32[8,128]{1,0:T(8,128)S(1)}, f32[8,128]{1,0:T(8,128)S(1)}, f32[64,128]{1,0:T(8,128)S(1)}) custom-call(f32[3072]{0:T(1024)S(1)} %reshape.45.x_flat, f32[6144]{0:T(1024)S(1)} %reshape.46.y_flat, f32[3,32,32]{2,1,0:T(8,128)S(1)} %maximum_bitcast_fusion.x_cols, ...), custom_call_target="tpu_custom_call" | custom-call | tf_op jit(solution)/shard_map/pallas_call | solution.py:529
  36.3 0.0 copy-start.14
  36.3 0.6 copy-done.14
  36.9 0.8 shard_map.93.scalars.tab
  37.6 14.8 %all-to-all-done = f32[512,1,96]{2,1,0:T(1,128)S(1)} async-done(((f32[512,1,96]{2,1,0:T(1,128)}), f32[512,1,96]{2,1,0:T(1,128)S(1)}, u32[]{:S(2)}, u32[]{:S(2)}) %all-to-all-start) | async-done | bytes 196640 | tf_op jit(solution)/shard_map/all_to_all | solution.py:549
  52.4 0.1 broadcast_in_dim.8.sigma_ref
  52.5 0.0 copy-start.2
  52.5 1.8 %shard_map.94 = (f32[96,512]{1,0:T(8,128)S(1)}, bf16[192,2048]{1,0:T(8,128)(2,1)S(1)}, f32[16,24,128]{2,1,0:T(8,128)}) custom-call(f32[512,96]{1,0:T(8,128)S(1)} %bitcast.24, f32[96,128]{1,0:T(8,128)S(1)} %broadcast_in_dim.8.sigma_ref, f32[4,128,128]{2,1,0:T(8,128)S(1)} %get-tuple-element.26.tab_ref, f32[208,128]{1,0:T(8,128)S(1)} %shard_map.93.scalars.tab), custom_call_target="tpu_custom_call" | custom-call | tf_op jit(solution)/shard_map/pallas_call | solution.py:552
  54.2 0.0 copy-start.4
  54.2 3.5 %all-to-all-start.1 = ((f32[16,24,128]{2,1,0:T(8,128)}), f32[16,24,128]{2,1,0:T(8,128)S(1)}, u32[]{:S(2)}, u32[]{:S(2)}) async-start(f32[16,24,128]{2,1,0:T(8,128)} %get-tuple-element.33), calls=%async_computation.1 | async-start | bytes 393216 | tf_op jit(solution)/shard_map/all_to_all | solution.py:557
  57.8 2.1 %shard_map.95 = (f32[2,96,128]{2,1,0:T(8,128)S(1)}, bf16[2048,256]{1,0:T(8,128)(2,1)S(1)}, f32[8,96,128]{2,1,0:T(8,128)S(1)}) custom-call(f32[96,512]{1,0:T(8,128)S(1)} %get-tuple-element.34.turned_ref, bf16[192,2048]{1,0:T(8,128)(2,1)S(1)} %get-tuple-element.35.outer, f32[512,96]{1,0:T(8,128)S(1)} %bitcast.25, f32[96,128]{1,0:T(8,128)S(1)} %broadcast_in_dim.8.sigma_ref, ...), custom_call_target="tpu_custom_call" | custom-call | tf_op jit(solution)/shard_map/pallas_call | solution.py:559
  59.9 0.0 copy-start.10
  59.9 0.6 copy-done.10
  60.5 0.0 copy-start.8
  60.5 4.2 %all-to-all-done.1.ends_ref = f32[16,24,128]{2,1,0:T(8,128)S(1)} async-done(((f32[16,24,128]{2,1,0:T(8,128)}), f32[16,24,128]{2,1,0:T(8,128)S(1)}, u32[]{:S(2)}, u32[]{:S(2)}) %all-to-all-start.1) | async-done | bytes 196640 | tf_op jit(solution)/shard_map/all_to_all | solution.py:557
  64.7 0.0 copy-start.11
  64.7 0.9 copy-done.11
  65.6 0.2 shard_map.96
  65.8 0.0 copy-done.6
  65.8 0.0 copy-done.2
  65.9 0.0 copy-start.12
  65.9 7.7 %all_to_all.25.sums_ref = f32[4,48,128]{2,1,0:T(8,128)S(1)} all-to-all(f32[4,48,128]{2,1,0:T(8,128)S(1)} %get-tuple-element.37), channel_id=1, replica_groups={{0,16,32,48},{64,80,96,112},{128,144,160,176},{192,208,224,240},{256,27..., dimensions={0} | all-to-all | bytes 196608 | tf_op jit(solution)/shard_map/all_to_all | solution.py:574
  73.5 0.7 shard_map.97
  74.2 0.0 copy-start
  74.2 0.6 copy-done
  74.8 0.0 copy-done.4
  74.8 4.0 %all-to-all-start.3 = ((f32[8,24,128]{2,1,0:T(8,128)}), f32[8,24,128]{2,1,0:T(8,128)}, u32[]{:S(2)}, u32[]{:S(2)}) async-start(f32[8,24,128]{2,1,0:T(8,128)} %shard_map.97), calls=%async_computation.3 | async-start | bytes 196608 | tf_op jit(solution)/shard_map/all_to_all | solution.py:577
  78.8 0.0 copy-done.8
  78.8 0.0 copy-done.12
  78.8 0.0 copy-start.3
  78.8 0.8 copy-done.3
  79.6 0.0 copy-start.5
  79.6 0.9 copy-done.5
  80.5 0.0 copy-start.7
  80.5 0.9 copy-done.7
  81.5 0.0 copy-start.9
  81.5 1.0 copy-done.9
  82.4 0.0 copy-start.13
  82.4 0.8 copy-done.13
  83.2 6.4 %shard_map.98.block_ref = f32[3072,128]{1,0:T(8,128)S(1)} custom-call(f32[3072]{0:T(1024)S(1)} %reshape.45.x_flat, f32[96,512]{1,0:T(8,128)S(1)} %copy-done.5, bf16[192,2048]{1,0:T(8,128)(2,1)S(1)} %get-tuple-element.35.outer, bf16[2048,256]{1,0:T(8,128)(2,1)S(1)} %get-tuple-element.40.hit, f32[8,96,128]{2,1,0:T(8,128)S(1)} %copy-done.9, ...), custom_call_target="tpu_custom_call" | custom-call | tf_op jit(solution)/shard_map/pallas_call | solution.py:578
  89.7 1.8 %all-to-all-done.3.joined_ref = f32[8,24,128]{2,1,0:T(8,128)} async-done(((f32[8,24,128]{2,1,0:T(8,128)}), f32[8,24,128]{2,1,0:T(8,128)}, u32[]{:S(2)}, u32[]{:S(2)}) %all-to-all-start.3) | async-done | bytes 98336 | tf_op jit(solution)/shard_map/all_to_all | solution.py:577
  91.5 0.9 copy-done.1
  92.4 0.9 shard_map.99
  93.3 8.5 %all_to_all.26.carry_ref = f32[4,48,128]{2,1,0:T(8,128)S(1)} all-to-all(f32[4,48,128]{2,1,0:T(8,128)S(1)} %shard_map.99), channel_id=1, replica_groups={{0,16,32,48},{64,80,96,112},{128,144,160,176},{192,208,224,240},{256,27..., dimensions={0} | all-to-all | bytes 196608 | tf_op jit(solution)/shard_map/all_to_all | solution.py:586
  101.9 0.8 copy-done.15
  102.6 1.7 %shard_map.100 = f32[3072,128]{1,0:T(8,128)} custom-call(f32[4,48,128]{2,1,0:T(8,128)S(1)} %all_to_all.26.carry_ref, f32[64,128]{1,0:T(8,128)S(1)} %copy-done.15, f32[3072,128]{1,0:T(8,128)S(1)} %shard_map.98.block_ref), custom_call_target="tpu_custom_call" | custom-call | tf_op jit(solution)/shard_map/pallas_call | solution.py:588
  (9 shorter events, 0.1 us)
Async XLA Ops:
  0.0 29.9 %copy-start.16 = (f32[6,16]{1,0:T(8,128)S(1)}, f32[6,16]{1,0:T(8,128)}, u32[]{:S(2)}) copy-start(f32[6,16]{1,0:T(8,128)} %param.15) | copy-start | bytes 1156
  3.2 49.2 %all-to-all-start = ((f32[512,1,96]{2,1,0:T(1,128)}), f32[512,1,96]{2,1,0:T(1,128)S(1)}, u32[]{:S(2)}, u32[]{:S(2)}) async-start(f32[512,1,96]{2,1,0:T(1,128)} %bitcast.26), calls=%async_computation | async-start | bytes 524288 | tf_op jit(solution)/shard_map/all_to_all | solution.py:549
  36.3 0.6 copy-start.14
  36.9 29.0 %copy-start.6 = (bf16[256,256]{1,0:T(8,128)(2,1)}, bf16[256,256]{1,0:T(8,128)(2,1)S(1)}, u32[]{:S(2)}) copy-start(bf16[256,256]{1,0:T(8,128)(2,1)S(1)} %get-tuple-element.25.mat_ref) | copy-start | bytes 393220
  52.5 13.4 %copy-start.2 = (f32[96,128]{1,0:T(8,128)}, f32[96,128]{1,0:T(8,128)S(1)}, u32[]{:S(2)}) copy-start(f32[96,128]{1,0:T(8,128)S(1)} %broadcast_in_dim.8.sigma_ref) | copy-start | bytes 147460
  54.2 20.6 %copy-start.4 = (f32[96,512]{1,0:T(8,128)}, f32[96,512]{1,0:T(8,128)S(1)}, u32[]{:S(2)}) copy-start(f32[96,512]{1,0:T(8,128)S(1)} %get-tuple-element.34.turned_ref) | copy-start | bytes 589828
  54.2 10.4 %all-to-all-start.1 = ((f32[16,24,128]{2,1,0:T(8,128)}), f32[16,24,128]{2,1,0:T(8,128)S(1)}, u32[]{:S(2)}, u32[]{:S(2)}) async-start(f32[16,24,128]{2,1,0:T(8,128)} %get-tuple-element.33), calls=%async_computation.1 | async-start | bytes 393216 | tf_op jit(solution)/shard_map/all_to_all | solution.py:557
  59.9 0.6 copy-start.10
  60.5 18.3 %copy-start.8 = (f32[8,96,128]{2,1,0:T(8,128)}, f32[8,96,128]{2,1,0:T(8,128)S(1)}, u32[]{:S(2)}) copy-start(f32[8,96,128]{2,1,0:T(8,128)S(1)} %get-tuple-element.41.block_ref) | copy-start | bytes 1179652
  64.7 0.9 copy-start.11
  65.9 13.0 %copy-start.12 = (f32[96,128]{1,0:T(8,128)}, f32[96,128]{1,0:T(8,128)S(1)}, u32[]{:S(2)}) copy-start(f32[96,128]{1,0:T(8,128)S(1)} %get-tuple-element.42.both_ref) | copy-start | bytes 147460
  74.2 0.6 copy-start
  74.8 16.7 %all-to-all-start.3 = ((f32[8,24,128]{2,1,0:T(8,128)}), f32[8,24,128]{2,1,0:T(8,128)}, u32[]{:S(2)}, u32[]{:S(2)}) async-start(f32[8,24,128]{2,1,0:T(8,128)} %shard_map.97), calls=%async_computation.3 | async-start | bytes 196608 | tf_op jit(solution)/shard_map/all_to_all | solution.py:577
  78.8 0.8 copy-start.3
  79.6 0.9 copy-start.5
  80.5 0.9 copy-start.7
  81.5 1.0 copy-start.9
  82.4 0.8 copy-start.13
  91.5 0.9 copy-start.1
  101.9 0.8 copy-start.15

commit v5 on v4

--- a/solution.py
+++ b/solution.py
@@ -19,6 +19,7 @@
 CY = 128
 NEAR = 4
 GROUP = 4
+FINAL_STEPS = 2
 EARLY = 1
 NX_GROUPS = 8
 NX_BLOCKS = NX_GROUPS * NEAR
@@ -58,10 +59,9 @@
 def pack_kernel(live_ref, *refs):
     sources, (send_ref, *buffers, sems) = refs[:5], refs[5:]
     copies = [pltpu.make_async_copy(src, buf, sems.at[k]) for k, (src, buf) in enumerate(zip(sources, buffers))]
-    for copy in copies:
-        copy.start()
-    for copy in copies:
-        copy.wait()
+    for k in (1, 0, 2, 3, 4):
+        copies[k].start()
+    copies[1].wait()
     resid_ref, dest_ref, column_ref, geometry_ref, beam_ref = buffers
     bins = resid_ref.shape[1]
     peers = send_ref.shape[0]
@@ -75,6 +75,9 @@
         before = iota((rows, LANES), 0) < iota((rows, LANES), 1) + chunk * LANES
         ranks.append(jnp.sum(jnp.where(same & before, 1.0, 0.0), axis=0, keepdims=True))
     rank = jnp.concatenate(ranks, axis=1)
+    onehot = jnp.where(iota((peers, bins), 0) == dest, 1.0, 0.0).astype(BF16)
+    for k in (0, 2, 3, 4):
+        copies[k].wait()
     alive = jnp.where(iota((1, bins), 1) < live_ref[0], 1.0, 0.0)
     weighted = geometry_ref[...] * (alive * resid_ref[...])
     payload = jnp.concatenate(
@@ -88,7 +91,6 @@
     )
     spread = jnp.concatenate([jnp.where(rank == float(s), payload, 0.0) for s in range(SLOTS)], axis=0)
     high, low = split_two(spread)
-    onehot = jnp.where(iota((peers, bins), 0) == dest, 1.0, 0.0).astype(BF16)
     both = dot_nt(onehot, jnp.concatenate([high, low], axis=0))
     send_ref[...] = both[:, : SLOTS * WIDTH] + both[:, SLOTS * WIDTH :]
 
@@ -210,24 +212,30 @@
     return jnp.concatenate(rows, axis=0)
 
 
-def ends_kernel(recv_ref, sigma_ref, tab_ref, scalars, turned_out, outer_out, ends_out):
+def fill_outer(turned_ref, outer):
+    sources = turned_ref.shape[1]
+    for s in range(SLOTS):
+        at = slice(s * sources, (s + 1) * sources)
+        base = s * WIDTH
+        for f in range(FIELDS):
+            high, low = split_two(
+                turned_ref[base : base + LEVELS] * turned_ref[base + LEVELS + f : base + LEVELS + f + 1]
+            )
+            outer[f * LEVELS : (f + 1) * LEVELS, at] = high
+            outer[DEPTH + f * LEVELS : DEPTH + (f + 1) * LEVELS, at] = low
+
+
+def ends_kernel(recv_ref, sigma_ref, tab_ref, scalars, turned_out, ends_out, outer):
     sources = recv_ref.shape[0]
     turned = recv_ref[...].T
     turned_out[...] = turned
     columns = [jnp.concatenate([tab_ref[c]] * (sources // LANES), axis=1) for c in range(2)]
     hits = []
     for s in range(SLOTS):
-        at = slice(s * sources, (s + 1) * sources)
-        base = s * WIDTH
         on_x, on_y = on_lines(turned, s)
         hits.append(weighted_hits(on_x, on_y, columns))
-        for f in range(FIELDS):
-            high, low = split_two(
-                turned[base : base + LEVELS] * turned[base + LEVELS + f : base + LEVELS + f + 1]
-            )
-            outer_out[f * LEVELS : (f + 1) * LEVELS, at] = high
-            outer_out[DEPTH + f * LEVELS : DEPTH + (f + 1) * LEVELS, at] = low
-    summed = dot_nt(outer_out[...], jnp.concatenate(hits, axis=1))
+    fill_outer(turned_out, outer)
+    summed = dot_nt(outer[...], jnp.concatenate(hits, axis=1))
     summed = (summed[:DEPTH] + summed[DEPTH:]) * sigma_ref[...]
     summed = summed + pltpu.roll(summed, LANES - CX, 1)
     own = lax.axis_index("gy")
@@ -274,7 +282,18 @@
     return jnp.concatenate(rows, axis=1).astype(I32) >> 8
 
 
-def early_kernel(turned_ref, outer, recv_ref, sigma_ref, tab_ref, mat_ref, sums_out, hit, block_out, masked):
+def fill_hit(recv_ref, hit):
+    sources = recv_ref.shape[0]
+    lane2 = iota((1, 2 * LANES), 1)
+    for s in range(SLOTS):
+        place = s * WIDTH + LEVELS + FIELDS
+        cols = jnp.broadcast_to(recv_ref[:, place : place + 1], (sources, LANES)).astype(I32) & (2 * CY - 1)
+        cols = jnp.concatenate([cols, cols], axis=1)
+        hit[s * sources : (s + 1) * sources] = jnp.where(cols == lane2, 1.0, 0.0).astype(BF16)
+
+
+def early_kernel(turned_ref, recv_ref, sigma_ref, tab_ref, mat_ref, sums_out, block_out, masked, hit, outer):
+    fill_outer(turned_ref, outer)
     turned = turned_ref[...]
     sources = turned.shape[1]
     sigma = sigma_ref[...]
@@ -290,12 +309,7 @@
     sums_out[0] = both[:DEPTH]
     sums_out[1] = both[DEPTH:]
 
-    lane2 = iota((1, 2 * LANES), 1)
-    for s in range(SLOTS):
-        place = s * WIDTH + LEVELS + FIELDS
-        cols = jnp.broadcast_to(recv_ref[:, place : place + 1], (sources, LANES)).astype(I32) & (2 * CY - 1)
-        cols = jnp.concatenate([cols, cols], axis=1)
-        hit[s * sources : (s + 1) * sources] = jnp.where(cols == lane2, 1.0, 0.0).astype(BF16)
+    fill_hit(recv_ref, hit)
 
     def emit(n, passed, carried):
         for h in range(2 * GROUP):
@@ -305,7 +319,9 @@
     place_steps(0, EARLY, pairs_of(turned_ref), outer, hit, sigma, mat_ref, masked, emit)(0)
 
 
-def grid_kernel(x_flat, turned_ref, outer, hit, block_ref, sigma_ref, mat_ref, both_ref, edge_ref, out_ref, masked, scaled):
+def grid_kernel(x_flat, turned_ref, recv_ref, block_ref, sigma_ref, mat_ref, both_ref, edge_ref, out_ref, masked, scaled, hit, outer):
+    fill_hit(recv_ref, hit)
+    fill_outer(turned_ref, outer)
     first = lax.axis_index("gx") * CX
     length = x_flat.shape[0] // 3
     both = both_ref[...]
@@ -456,13 +472,18 @@
     rows = carry_ref.shape[1] // 2
     fore = ends_ref[:CX]
     back = ends_ref[CX:]
+    per = DEPTH // FINAL_STEPS
     step = pl.program_id(0)
-    base = step * (rows * CX)
-    for r in range(rows):
+    base = step * (per * CX)
+    for r in range(per):
+        if per <= rows:
+            chunk, row = step * per // rows, (step * per) % rows + r
+        else:
+            chunk, row = step * (per // rows) + r // rows, r % rows
         out_ref[r * CX : (r + 1) * CX] = (
             block_ref[pl.ds(pl.multiple_of(base + r * CX, CX), CX), :]
-            + carry_ref[step, r : r + 1] * fore
-            + carry_ref[step, rows + r : rows + r + 1] * back
+            + carry_ref[chunk, pl.ds(row, 1), :] * fore
+            + carry_ref[chunk, pl.ds(rows + row, 1), :] * back
         )
 
 
@@ -549,23 +570,25 @@
     moved = a2a(moved.reshape(peers, 1, SLOTS * WIDTH), ("gx", "gy"), split_axis=0, concat_axis=0)
     moved, coefs, sigma, scalars = tie((moved, coefs, sigma, scalars))
     moved = moved.reshape(peers, SLOTS * WIDTH)
-    turned, outer, ends = call(
+    outer = pltpu.VMEM((2 * DEPTH, slots), BF16)
+    hit = pltpu.VMEM((slots, 2 * CY), BF16)
+    turned, ends = call(
         ends_kernel,
-        [((SLOTS * WIDTH, peers), F32), ((2 * DEPTH, slots), BF16), ((count_y, DEPTH // 4, LANES), F32)],
+        [((SLOTS * WIDTH, peers), F32), ((count_y, DEPTH // 4, LANES), F32)],
         [vmem] * 4,
+        [outer],
     )(moved, sigma, tab, scalars)
     ends = a2a(ends, "gy", split_axis=0, concat_axis=0)
     masked = pltpu.VMEM((GROUP * 2 * DEPTH, slots), BF16)
-    raw, hit, block = call(
+    raw, block = call(
         early_kernel,
         [
             ((2, DEPTH, LANES), F32),
-            ((slots, 2 * CY), BF16),
             ((EARLY * 2 * GROUP, DEPTH, LANES), F32),
         ],
-        [vmem] * 6,
-        [masked],
-    )(turned, outer, moved, sigma, tab, mat)
+        [vmem] * 5,
+        [masked, hit, outer],
+    )(turned, moved, sigma, tab, mat)
     both, sums = call(
         line_kernel,
         [((DEPTH, LANES), F32), ((NEAR, chunk, LANES), F32)],
@@ -578,16 +601,16 @@
     block = call(
         grid_kernel,
         [((DEPTH * CX, LANES), F32)],
-        [smem] + [vmem] * 8,
-        [masked, pltpu.VMEM((CX, DEPTH, LANES), F32)],
-    )(x_flat, turned, outer, hit, block, sigma, mat, both, edge)
+        [smem] + [vmem] * 7,
+        [masked, pltpu.VMEM((CX, DEPTH, LANES), F32), hit, outer],
+    )(x_flat, turned, moved, block, sigma, mat, both, edge)
     joined, block = tie((joined, block))
     carry = call(carry_kernel, [((NEAR, chunk, LANES), F32)], [vmem] * 3)(scalars, joined, sums)
     carry = a2a(carry, "gx", split_axis=0, concat_axis=0, axis_index_groups=near_groups)
-    rows = DEPTH * CX // NEAR
+    rows = DEPTH * CX // FINAL_STEPS
     out = pl.pallas_call(
         final_kernel,
-        grid=(NEAR,),
+        grid=(FINAL_STEPS,),
         out_shape=jax.ShapeDtypeStruct((DEPTH * CX, LANES), F32),
         in_specs=[vmem] * 3,
         out_specs=pl.BlockSpec((rows, LANES), lambda k: (k, 0)),

time: 105 us -> 99.6 us (0.949)
  local copies, waits for them, and re-layouts: 9.72 us -> 1.56 us
  waiting for transfers between devices: 20.8 us -> 25.4 us
  Pallas kernels: 23.3 us -> 22.2 us
    unnamed x34 -> x0, local copies, waits for them, and re-layouts: 8.83 us -> none
    all_to_all x1, waiting for transfers between devices: 1.84 us -> 5.86 us  [local(): a2a(joined, 'gx', split_axis=0, concat_axis=0, axis_index_groups=far_groups)]
  transfers between devices with their start and end apart: 3 -> 3, of which waited for: 3 -> 3; matrix products, arithmetic and copies ran while one was open for 2% -> 3% of each run, Pallas kernels for 15% -> 16%
where the time goes in v5:
time: 99.6 us; the launch traced here: 99 us
  starting transfers between devices  31.2 us (31%)
  waiting for transfers between devices  25.4 us (26%)
  Pallas kernels  22.2 us (22%)
  blocking collectives  16.2 us (16%)
  other arithmetic  1.63 us (2%)
  local copies, waits for them, and re-layouts  1.56 us (2%)
    all_to_all x1, starting transfers between devices, local(): a2a(moved.reshape(peers, 1, SLOTS * WIDTH), ('gx', 'gy'), split_axis=0, c...  24.3 us
    all_to_all x1, waiting for transfers between devices, local(): a2a(moved.reshape(peers, 1, SLOTS * WIDTH), ('gx', 'gy'), split_axis=0, c...  14.7 us
    all_to_all x1, blocking collectives, local(): a2a(carry, 'gx', split_axis=0, concat_axis=0, axis_index_groups=near_groups)  8.54 us
    all_to_all x1, blocking collectives, local(): a2a(sums, 'gx', split_axis=0, concat_axis=0, axis_index_groups=near_groups)  7.65 us
    pallas_call x1, Pallas kernels, local(): call(grid_kernel, [((DEPTH * CX, LANES), F32)], [smem] + [vmem] * 7, [mas...  6.75 us
    pallas_call x1, Pallas kernels, local(): call(coef_kernel, [((2 * CY, 2 * CY), BF16), ((4, CY, LANES), F32), ((8,...  6.21 us
    all_to_all x1, waiting for transfers between devices, local(): a2a(joined, 'gx', split_axis=0, concat_axis=0, axis_index_groups=far_groups)  5.86 us
    all_to_all x1, waiting for transfers between devices, local(): ends = a2a(ends, 'gy', split_axis=0, concat_axis=0)  4.84 us
  transfers between devices with their start and end apart: 3, of which 3 were waited for; matrix products, arithmetic and copies ran while one was open for 3% of the time, Pallas kernels for 16%

profile of v5, /device:TPU:1, one launch (start us, length us, event | category | flops | bytes accessed | tf_op | source)
XLA Modules:
  0.0 99.0 jit_solution(5884227565192966336)
XLA Ops:
  0.7 2.5 %shard_map.91 = f32[512,96]{1,0:T(8,128)} custom-call(s32[1]{0:T(128)S(6)} %copy.20.live_ref, f32[1,1024]{1,0:T(1,128)} %bitcast.34, s32[1,1024]{1,0:T(1,128)} %bitcast.35, s32[1,1024]{1,0:T(1,128)} %bitcast.36, f32[6,1024]{1,0:T(8,128)} %refs_3_.1, f32[16,1024]{1,0:T(8,128)} %refs_4_.1), custom_call_target="tpu_custom_call" | custom-call | tf_op jit(solution)/shard_map/pallas_call | solution.py:525
  3.2 24.3 %all-to-all-start = ((f32[512,1,96]{2,1,0:T(1,128)}), f32[512,1,96]{2,1,0:T(1,128)S(1)}, u32[]{:S(2)}, u32[]{:S(2)}) async-start(f32[512,1,96]{2,1,0:T(1,128)} %bitcast.27), calls=%async_computation | async-start | bytes 524288 | tf_op jit(solution)/shard_map/all_to_all | solution.py:570
  27.5 0.8 broadcast_in_dim.7
  28.2 0.7 broadcast_subtract_fusion.1
  28.9 0.1 fusion.7
  29.0 0.1 pad_maximum_fusion.5
  29.1 0.1 stack.48
  29.2 0.1 stack.49
  29.2 0.1 stack.50
  29.3 0.1 copy.16
  29.4 0.1 copy.17
  29.5 0.1 copy.18
  29.6 0.7 fusion.4
  30.3 0.1 fusion.6
  30.4 0.1 fusion.2
  30.5 0.1 copy.19.y_cols
  30.7 6.2 %shard_map.92 = (bf16[256,256]{1,0:T(8,128)(2,1)S(1)}, f32[4,128,128]{2,1,0:T(8,128)S(1)}, f32[8,128]{1,0:T(8,128)S(1)}, f32[8,128]{1,0:T(8,128)S(1)}, f32[64,128]{1,0:T(8,128)S(1)}) custom-call(f32[3072]{0:T(1024)S(1)} %reshape.45.x_flat, f32[6144]{0:T(1024)S(1)} %reshape.46.y_flat, f32[3,32,32]{2,1,0:T(8,128)S(1)} %maximum_bitcast_fusion.x_cols, ...), custom_call_target="tpu_custom_call" | custom-call | tf_op jit(solution)/shard_map/pallas_call | solution.py:550
  36.9 0.8 shard_map.93.scalars.tab
  37.6 14.7 %all-to-all-done = f32[512,1,96]{2,1,0:T(1,128)S(1)} async-done(((f32[512,1,96]{2,1,0:T(1,128)}), f32[512,1,96]{2,1,0:T(1,128)S(1)}, u32[]{:S(2)}, u32[]{:S(2)}) %all-to-all-start) | async-done | bytes 196640 | tf_op jit(solution)/shard_map/all_to_all | solution.py:570
  52.3 0.1 broadcast_in_dim.8.sigma_ref
  52.4 1.7 %shard_map.94 = (f32[96,512]{1,0:T(8,128)S(1)}, f32[16,24,128]{2,1,0:T(8,128)}) custom-call(f32[512,96]{1,0:T(8,128)S(1)} %bitcast.24, f32[96,128]{1,0:T(8,128)S(1)} %broadcast_in_dim.8.sigma_ref, f32[4,128,128]{2,1,0:T(8,128)S(1)} %get-tuple-element.24.tab_ref, f32[208,128]{1,0:T(8,128)S(1)} %shard_map.93.scalars.tab), custom_call_target="tpu_custom_call" | custom-call | tf_op jit(solution)/shard_map/pallas_call | solution.py:575
  54.1 3.5 %all-to-all-start.1 = ((f32[16,24,128]{2,1,0:T(8,128)}), f32[16,24,128]{2,1,0:T(8,128)S(1)}, u32[]{:S(2)}, u32[]{:S(2)}) async-start(f32[16,24,128]{2,1,0:T(8,128)} %get-tuple-element.31), calls=%async_computation.1 | async-start | bytes 393216 | tf_op jit(solution)/shard_map/all_to_all | solution.py:581
  57.6 2.1 %shard_map.95 = (f32[2,96,128]{2,1,0:T(8,128)S(1)}, f32[8,96,128]{2,1,0:T(8,128)S(1)}) custom-call(f32[96,512]{1,0:T(8,128)S(1)} %get-tuple-element.32.turned_ref, f32[512,96]{1,0:T(8,128)S(1)} %bitcast.25, f32[96,128]{1,0:T(8,128)S(1)} %broadcast_in_dim.8.sigma_ref, f32[4,128,128]{2,1,0:T(8,128)S(1)} %get-tuple-element.24.tab_ref, ...), custom_call_target="tpu_custom_call" | custom-call | tf_op jit(solution)/shard_map/pallas_call | solution.py:583
  59.7 4.8 %all-to-all-done.1.ends_ref = f32[16,24,128]{2,1,0:T(8,128)S(1)} async-done(((f32[16,24,128]{2,1,0:T(8,128)}), f32[16,24,128]{2,1,0:T(8,128)S(1)}, u32[]{:S(2)}, u32[]{:S(2)}) %all-to-all-start.1) | async-done | bytes 196640 | tf_op jit(solution)/shard_map/all_to_all | solution.py:581
  64.6 0.2 shard_map.96
  64.8 7.7 %all_to_all.25.sums_ref = f32[4,48,128]{2,1,0:T(8,128)S(1)} all-to-all(f32[4,48,128]{2,1,0:T(8,128)S(1)} %get-tuple-element.34), channel_id=1, replica_groups={{0,16,32,48},{64,80,96,112},{128,144,160,176},{192,208,224,240},{256,27..., dimensions={0} | all-to-all | bytes 196608 | tf_op jit(solution)/shard_map/all_to_all | solution.py:597
  72.5 0.7 shard_map.97
  73.1 3.4 %all-to-all-start.3 = ((f32[8,24,128]{2,1,0:T(8,128)}), f32[8,24,128]{2,1,0:T(8,128)S(1)}, u32[]{:S(2)}, u32[]{:S(2)}) async-start(f32[8,24,128]{2,1,0:T(8,128)} %shard_map.97), calls=%async_computation.3 | async-start | bytes 196608 | tf_op jit(solution)/shard_map/all_to_all | solution.py:600
  76.5 6.7 %shard_map.98.block_ref = f32[3072,128]{1,0:T(8,128)S(1)} custom-call(f32[3072]{0:T(1024)S(1)} %reshape.45.x_flat, f32[96,512]{1,0:T(8,128)S(1)} %get-tuple-element.32.turned_ref, f32[512,96]{1,0:T(8,128)S(1)} %bitcast.26, f32[8,96,128]{2,1,0:T(8,128)S(1)} %get-tuple-element.37.block_ref, f32[96,128]{1,0:T(8,128)S(1)} %broadcast_in_dim.8.sigma_ref, ...), custom_call_target="tpu_custom_call" | custom-call | tf_op jit(solution)/shard_map/pallas_call | solution.py:601
  83.3 5.9 %all-to-all-done.3.joined_ref = f32[8,24,128]{2,1,0:T(8,128)S(1)} async-done(((f32[8,24,128]{2,1,0:T(8,128)}), f32[8,24,128]{2,1,0:T(8,128)S(1)}, u32[]{:S(2)}, u32[]{:S(2)}) %all-to-all-start.3) | async-done | bytes 98336 | tf_op jit(solution)/shard_map/all_to_all | solution.py:600
  89.2 8.5 %all_to_all.26.carry_ref = f32[4,48,128]{2,1,0:T(8,128)S(1)} all-to-all(f32[4,48,128]{2,1,0:T(8,128)S(1)} %shard_map.99), channel_id=1, replica_groups={{0,16,32,48},{64,80,96,112},{128,144,160,176},{192,208,224,240},{256,27..., dimensions={0} | all-to-all | bytes 196608 | tf_op jit(solution)/shard_map/all_to_all | solution.py:609
  97.7 1.3 %shard_map.100 = f32[3072,128]{1,0:T(8,128)} custom-call(f32[4,48,128]{2,1,0:T(8,128)S(1)} %all_to_all.26.carry_ref, f32[64,128]{1,0:T(8,128)S(1)} %get-tuple-element.27.ends_ref, f32[3072,128]{1,0:T(8,128)S(1)} %shard_map.98.block_ref), custom_call_target="tpu_custom_call" | custom-call | tf_op jit(solution)/shard_map/pallas_call | solution.py:611
  (7 shorter events, 0.1 us)
Async XLA Ops:
  3.2 49.2 %all-to-all-start = ((f32[512,1,96]{2,1,0:T(1,128)}), f32[512,1,96]{2,1,0:T(1,128)S(1)}, u32[]{:S(2)}, u32[]{:S(2)}) async-start(f32[512,1,96]{2,1,0:T(1,128)} %bitcast.27), calls=%async_computation | async-start | bytes 524288 | tf_op jit(solution)/shard_map/all_to_all | solution.py:570
  54.1 10.4 %all-to-all-start.1 = ((f32[16,24,128]{2,1,0:T(8,128)}), f32[16,24,128]{2,1,0:T(8,128)S(1)}, u32[]{:S(2)}, u32[]{:S(2)}) async-start(f32[16,24,128]{2,1,0:T(8,128)} %get-tuple-element.31), calls=%async_computation.1 | async-start | bytes 393216 | tf_op jit(solution)/shard_map/all_to_all | solution.py:581
  73.1 16.0 %all-to-all-start.3 = ((f32[8,24,128]{2,1,0:T(8,128)}), f32[8,24,128]{2,1,0:T(8,128)S(1)}, u32[]{:S(2)}, u32[]{:S(2)}) async-start(f32[8,24,128]{2,1,0:T(8,128)} %shard_map.97), calls=%async_computation.3 | async-start | bytes 196608 | tf_op jit(solution)/shard_map/all_to_all | solution.py:600

commit v6 on v5

--- a/solution.py
+++ b/solution.py
@@ -19,6 +19,7 @@
 CY = 128
 NEAR = 4
 GROUP = 4
+SPREAD, UNSPREAD = 37, 429
 FINAL_STEPS = 2
 EARLY = 1
 NX_GROUPS = 8
@@ -75,7 +76,8 @@
         before = iota((rows, LANES), 0) < iota((rows, LANES), 1) + chunk * LANES
         ranks.append(jnp.sum(jnp.where(same & before, 1.0, 0.0), axis=0, keepdims=True))
     rank = jnp.concatenate(ranks, axis=1)
-    onehot = jnp.where(iota((peers, bins), 0) == dest, 1.0, 0.0).astype(BF16)
+    place = (dest * UNSPREAD) & (peers - 1)
+    onehot = jnp.where(iota((peers, bins), 0) == place, 1.0, 0.0).astype(BF16)
     for k in (0, 2, 3, 4):
         copies[k].wait()
     alive = jnp.where(iota((1, bins), 1) < live_ref[0], 1.0, 0.0)
@@ -95,46 +97,32 @@
     send_ref[...] = both[:, : SLOTS * WIDTH] + both[:, SLOTS * WIDTH :]
 
 
-def coef_kernel(x_flat, y_flat, x_cols, y_cols, y_rows, mat_ref, tab_ref, edge_ref, block_ref, ends_ref, chain, gammas, betas):
+def coef_kernel(x_flat, y_flat, x_cols, y_cols, y_rows, mat_ref, tab_ref, edge_ref, block_ref, ends_ref, chain, entry):
     own_x = lax.axis_index("gx")
     own_y = lax.axis_index("gy")
     length = y_rows.shape[1] * LANES
     span = x_cols.shape[2] * CX
 
-    def block_scalars(cols, row):
-        steps, blocks = cols.shape[1:]
-
-        def forward(p, value):
-            value = value * cols[0, pl.ds(p, 1), :]
-            gammas[pl.ds(p, 1), :blocks] = value
-            return value
-
-        alpha = lax.fori_loop(0, steps, forward, jnp.ones((1, blocks), F32))
-
-        def backward(k, carried):
-            gamma, beta = carried
-            p = steps - 1 - k
-            later = cols[1, pl.ds(p, 1), :]
-            gamma = cols[2, pl.ds(p, 1), :] * gammas[pl.ds(p, 1), :blocks] + later * gamma
-            beta = beta * later
-            gammas[pl.ds(p, 1), :blocks] = gamma
-            betas[pl.ds(p, 1), :blocks] = beta
-            return gamma, beta
-
-        gamma, beta = lax.fori_loop(
-            0, steps, backward, (jnp.zeros((1, blocks), F32), jnp.ones((1, blocks), F32))
-        )
-        block_ref[row : row + 1, :blocks] = alpha
-        block_ref[row + 1 : row + 2, :blocks] = beta
-        block_ref[row + 2 : row + 3, :blocks] = gamma
-
     block_ref[...] = jnp.zeros(block_ref.shape, F32)
-    block_scalars(y_cols, 3)
-    block_scalars(x_cols, 0)
     blocks = x_cols.shape[2]
+    alpha = jnp.ones((1, blocks), F32)
+    entries = []
+    for p in range(CX):
+        alpha = alpha * x_cols[0, p : p + 1, :]
+        entries.append(alpha)
+    gamma, beta = jnp.zeros((1, blocks), F32), jnp.ones((1, blocks), F32)
+    gammas, betas = [], []
+    for p in reversed(range(CX)):
+        later = x_cols[1, p : p + 1, :]
+        gamma = x_cols[2, p : p + 1, :] * entries[p] + later * gamma
+        beta = beta * later
+        gammas.append(gamma)
+        betas.append(beta)
+    for row, value in enumerate((alpha, beta, gamma)):
+        block_ref[row : row + 1, :blocks] = value
     mine = iota((CX, blocks), 1) == own_x
-    for k, scratch in enumerate((gammas, betas)):
-        picked = jnp.where(mine, scratch[:CX, :blocks] * x_cols[2], 0.0)
+    for k, rows in enumerate((gammas, betas)):
+        picked = jnp.where(mine, jnp.concatenate(rows[::-1], axis=0) * x_cols[2], 0.0)
         ends_ref[k * CX : (k + 1) * CX] = jnp.broadcast_to(
             jnp.sum(picked, axis=1, keepdims=True), (CX, LANES)
         )
@@ -161,21 +149,37 @@
         row_start = jnp.where(lane % CX == x, starts[CX - 1 - x], row_start)
 
     first = own_y * CY
-
-    def fill(n, row):
-        row = jnp.where(lane == n, 1.0, row * y_flat[first + n])
-        chain[pl.ds(n, 1), :] = row
-        return row
-
-    lax.fori_loop(0, CY, fill, jnp.zeros((1, LANES), F32))
-
-    def unfill(k, row):
-        n = CY - 1 - k
-        row = chain[pl.ds(n, 1), :] * y_flat[2 * length + first + n] + row * y_flat[length + first + n]
-        chain[pl.ds(n, 1), :] = row
-        return row
-
-    lax.fori_loop(0, CY, unfill, jnp.zeros((1, LANES), F32))
+    blocks = y_cols.shape[2]
+    unroll = 8
+
+    def forward(k, carried):
+        alpha, row = carried
+        for u in range(unroll):
+            n = k * unroll + u
+            alpha = alpha * y_cols[0, pl.ds(n, 1), :]
+            entry[pl.ds(n, 1), :blocks] = alpha
+            row = jnp.where(lane == n, 1.0, row * y_flat[first + n])
+            chain[pl.ds(n, 1), :] = row
+        return alpha, row
+
+    none = jnp.zeros((1, LANES), F32)
+    one = jnp.ones((1, blocks), F32)
+    alpha, _ = lax.fori_loop(0, CY // unroll, forward, (one, none))
+
+    def backward(k, carried):
+        gamma, beta, row = carried
+        for u in range(unroll):
+            n = CY - 1 - (k * unroll + u)
+            later = y_cols[1, pl.ds(n, 1), :]
+            gamma = y_cols[2, pl.ds(n, 1), :] * entry[pl.ds(n, 1), :blocks] + later * gamma
+            beta = beta * later
+            row = chain[pl.ds(n, 1), :] * y_flat[2 * length + first + n] + row * y_flat[length + first + n]
+            chain[pl.ds(n, 1), :] = row
+        return gamma, beta, row
+
+    gamma, beta, _ = lax.fori_loop(0, CY // unroll, backward, (jnp.zeros((1, blocks), F32), one, none))
+    for row, value in enumerate((alpha, beta, gamma)):
+        block_ref[3 + row : 4 + row, :blocks] = value
     scale = y_rows[2, pl.ds(own_y, 1), :]
     filt = chain[...].T * scale
     high, low = split_two(filt)
@@ -557,7 +561,7 @@
             ((2 * CX, LANES), F32),
         ],
         [smem, smem, vmem, vmem, vmem],
-        [pltpu.VMEM((CY, LANES), F32)] * 3,
+        [pltpu.VMEM((CY, LANES), F32)] * 2,
     )(
         x_flat,
         tab_y.reshape(-1),
@@ -567,7 +571,10 @@
     )
     scalars = call(chain_kernel, [((TAB_ROWS, LANES), F32)], [smem])(coefs[3])
     mat, tab, edge, _, x_ends = coefs
-    moved = a2a(moved.reshape(peers, 1, SLOTS * WIDTH), ("gx", "gy"), split_axis=0, concat_axis=0)
+    order = [[(p * SPREAD) % peers for p in range(peers)]]
+    moved = a2a(
+        moved.reshape(peers, 1, SLOTS * WIDTH), ("gx", "gy"), split_axis=0, concat_axis=0, axis_index_groups=order
+    )
     moved, coefs, sigma, scalars = tie((moved, coefs, sigma, scalars))
     moved = moved.reshape(peers, SLOTS * WIDTH)
     outer = pltpu.VMEM((2 * DEPTH, slots), BF16)

time: 99.6 us -> 99.3 us (level)
  Pallas kernels: 22.2 us -> 18.6 us
  waiting for transfers between devices: 25.4 us -> 28.5 us
    pallas_call x1, Pallas kernels: 6.21 us -> 2.61 us  [local(): call(coef_kernel, [((2 * CY, 2 * CY), BF16), ((4, CY, LANES), F32), ((8,...]
    all_to_all x1, waiting for transfers between devices: 14.7 us -> 17.7 us  [local(): a2a(moved.reshape(peers, 1, SLOTS * WIDTH), ('gx', 'gy'), split_axis=0, c...]
  transfers between devices with their start and end apart: 3 -> 3, of which waited for: 3 -> 3; matrix products, arithmetic and copies ran while one was open for 3% -> 3% of each run, Pallas kernels for 16% -> 12%
where the time goes in v6:
time: 99.3 us; the launch traced here: 98.7 us
  starting transfers between devices  31.2 us (31%)
  waiting for transfers between devices  28.5 us (29%)
  Pallas kernels  18.6 us (19%)
  blocking collectives  16.4 us (17%)
  other arithmetic  1.63 us (2%)
  local copies, waits for them, and re-layouts  1.56 us (2%)
    all_to_all x1, starting transfers between devices, local(): a2a(moved.reshape(peers, 1, SLOTS * WIDTH), ('gx', 'gy'), split_axis=0, c...  24.3 us
    all_to_all x1, waiting for transfers between devices, local(): a2a(moved.reshape(peers, 1, SLOTS * WIDTH), ('gx', 'gy'), split_axis=0, c...  17.7 us
    all_to_all x1, blocking collectives, local(): a2a(carry, 'gx', split_axis=0, concat_axis=0, axis_index_groups=near_groups)  8.51 us
    all_to_all x1, blocking collectives, local(): a2a(sums, 'gx', split_axis=0, concat_axis=0, axis_index_groups=near_groups)  7.86 us
    pallas_call x1, Pallas kernels, local(): call(grid_kernel, [((DEPTH * CX, LANES), F32)], [smem] + [vmem] * 7, [mas...  6.75 us
    all_to_all x1, waiting for transfers between devices, local(): a2a(joined, 'gx', split_axis=0, concat_axis=0, axis_index_groups=far_groups)  5.86 us
    all_to_all x1, waiting for transfers between devices, local(): ends = a2a(ends, 'gy', split_axis=0, concat_axis=0)  4.95 us
    all_to_all x1, starting transfers between devices, local(): ends = a2a(ends, 'gy', split_axis=0, concat_axis=0)  3.52 us
  transfers between devices with their start and end apart: 3, of which 3 were waited for; matrix products, arithmetic and copies ran while one was open for 3% of the time, Pallas kernels for 12%

profile of v6, /device:TPU:1, one launch (start us, length us, event | category | flops | bytes accessed | tf_op | source)
XLA Modules:
  0.0 98.7 jit_solution(9984086250847205221)
XLA Ops:
  0.7 2.5 %shard_map.91 = f32[512,96]{1,0:T(8,128)} custom-call(s32[1]{0:T(128)S(6)} %copy.20.live_ref, f32[1,1024]{1,0:T(1,128)} %bitcast.34, s32[1,1024]{1,0:T(1,128)} %bitcast.35, s32[1,1024]{1,0:T(1,128)} %bitcast.36, f32[6,1024]{1,0:T(8,128)} %refs_3_.1, f32[16,1024]{1,0:T(8,128)} %refs_4_.1), custom_call_target="tpu_custom_call" | custom-call | tf_op jit(solution)/shard_map/pallas_call | solution.py:529
  3.1 24.3 %all-to-all-start = ((f32[512,1,96]{2,1,0:T(1,128)}), f32[512,1,96]{2,1,0:T(1,128)S(1)}, u32[]{:S(2)}, u32[]{:S(2)}) async-start(f32[512,1,96]{2,1,0:T(1,128)} %bitcast.27), calls=%async_computation | async-start | bytes 524288 | tf_op jit(solution)/shard_map/all_to_all | solution.py:575
  27.5 0.8 broadcast_in_dim.7
  28.2 0.7 broadcast_subtract_fusion.1
  28.9 0.1 fusion.7
  29.0 0.1 pad_maximum_fusion.5
  29.1 0.1 stack.48
  29.1 0.1 stack.49
  29.2 0.1 stack.50
  29.3 0.1 copy.16
  29.4 0.1 copy.17
  29.5 0.1 copy.18
  29.5 0.7 fusion.4
  30.3 0.1 fusion.6
  30.3 0.1 fusion.2
  30.5 0.1 copy.19.y_cols
  30.6 2.6 %shard_map.92 = (bf16[256,256]{1,0:T(8,128)(2,1)S(1)}, f32[4,128,128]{2,1,0:T(8,128)S(1)}, f32[8,128]{1,0:T(8,128)S(1)}, f32[8,128]{1,0:T(8,128)S(1)}, f32[64,128]{1,0:T(8,128)S(1)}) custom-call(f32[3072]{0:T(1024)S(1)} %reshape.45.x_flat, f32[6144]{0:T(1024)S(1)} %reshape.46.y_flat, f32[3,32,32]{2,1,0:T(8,128)S(1)} %maximum_bitcast_fusion.x_cols, ...), custom_call_target="tpu_custom_call" | custom-call | tf_op jit(solution)/shard_map/pallas_call | solution.py:554
  33.3 0.8 shard_map.93.scalars.tab
  34.0 17.7 %all-to-all-done = f32[512,1,96]{2,1,0:T(1,128)S(1)} async-done(((f32[512,1,96]{2,1,0:T(1,128)}), f32[512,1,96]{2,1,0:T(1,128)S(1)}, u32[]{:S(2)}, u32[]{:S(2)}) %all-to-all-start) | async-done | bytes 196640 | tf_op jit(solution)/shard_map/all_to_all | solution.py:575
  51.7 0.1 broadcast_in_dim.8.sigma_ref
  51.8 1.7 %shard_map.94 = (f32[96,512]{1,0:T(8,128)S(1)}, f32[16,24,128]{2,1,0:T(8,128)}) custom-call(f32[512,96]{1,0:T(8,128)S(1)} %bitcast.24, f32[96,128]{1,0:T(8,128)S(1)} %broadcast_in_dim.8.sigma_ref, f32[4,128,128]{2,1,0:T(8,128)S(1)} %get-tuple-element.24.tab_ref, f32[208,128]{1,0:T(8,128)S(1)} %shard_map.93.scalars.tab), custom_call_target="tpu_custom_call" | custom-call | tf_op jit(solution)/shard_map/pallas_call | solution.py:582
  53.5 3.5 %all-to-all-start.1 = ((f32[16,24,128]{2,1,0:T(8,128)}), f32[16,24,128]{2,1,0:T(8,128)S(1)}, u32[]{:S(2)}, u32[]{:S(2)}) async-start(f32[16,24,128]{2,1,0:T(8,128)} %get-tuple-element.31), calls=%async_computation.1 | async-start | bytes 393216 | tf_op jit(solution)/shard_map/all_to_all | solution.py:588
  57.1 2.1 %shard_map.95 = (f32[2,96,128]{2,1,0:T(8,128)S(1)}, f32[8,96,128]{2,1,0:T(8,128)S(1)}) custom-call(f32[96,512]{1,0:T(8,128)S(1)} %get-tuple-element.32.turned_ref, f32[512,96]{1,0:T(8,128)S(1)} %bitcast.25, f32[96,128]{1,0:T(8,128)S(1)} %broadcast_in_dim.8.sigma_ref, f32[4,128,128]{2,1,0:T(8,128)S(1)} %get-tuple-element.24.tab_ref, ...), custom_call_target="tpu_custom_call" | custom-call | tf_op jit(solution)/shard_map/pallas_call | solution.py:590
  59.1 5.0 %all-to-all-done.1.ends_ref = f32[16,24,128]{2,1,0:T(8,128)S(1)} async-done(((f32[16,24,128]{2,1,0:T(8,128)}), f32[16,24,128]{2,1,0:T(8,128)S(1)}, u32[]{:S(2)}, u32[]{:S(2)}) %all-to-all-start.1) | async-done | bytes 196640 | tf_op jit(solution)/shard_map/all_to_all | solution.py:588
  64.1 0.2 shard_map.96
  64.3 7.9 %all_to_all.25.sums_ref = f32[4,48,128]{2,1,0:T(8,128)S(1)} all-to-all(f32[4,48,128]{2,1,0:T(8,128)S(1)} %get-tuple-element.34), channel_id=1, replica_groups={{0,16,32,48},{64,80,96,112},{128,144,160,176},{192,208,224,240},{256,27..., dimensions={0} | all-to-all | bytes 196608 | tf_op jit(solution)/shard_map/all_to_all | solution.py:604
  72.2 0.7 shard_map.97
  72.9 3.4 %all-to-all-start.3 = ((f32[8,24,128]{2,1,0:T(8,128)}), f32[8,24,128]{2,1,0:T(8,128)S(1)}, u32[]{:S(2)}, u32[]{:S(2)}) async-start(f32[8,24,128]{2,1,0:T(8,128)} %shard_map.97), calls=%async_computation.3 | async-start | bytes 196608 | tf_op jit(solution)/shard_map/all_to_all | solution.py:607
  76.2 6.8 %shard_map.98.block_ref = f32[3072,128]{1,0:T(8,128)S(1)} custom-call(f32[3072]{0:T(1024)S(1)} %reshape.45.x_flat, f32[96,512]{1,0:T(8,128)S(1)} %get-tuple-element.32.turned_ref, f32[512,96]{1,0:T(8,128)S(1)} %bitcast.26, f32[8,96,128]{2,1,0:T(8,128)S(1)} %get-tuple-element.37.block_ref, f32[96,128]{1,0:T(8,128)S(1)} %broadcast_in_dim.8.sigma_ref, ...), custom_call_target="tpu_custom_call" | custom-call | tf_op jit(solution)/shard_map/pallas_call | solution.py:608
  83.0 5.9 %all-to-all-done.3.joined_ref = f32[8,24,128]{2,1,0:T(8,128)S(1)} async-done(((f32[8,24,128]{2,1,0:T(8,128)}), f32[8,24,128]{2,1,0:T(8,128)S(1)}, u32[]{:S(2)}, u32[]{:S(2)}) %all-to-all-start.3) | async-done | bytes 98336 | tf_op jit(solution)/shard_map/all_to_all | solution.py:607
  88.9 8.5 %all_to_all.26.carry_ref = f32[4,48,128]{2,1,0:T(8,128)S(1)} all-to-all(f32[4,48,128]{2,1,0:T(8,128)S(1)} %shard_map.99), channel_id=1, replica_groups={{0,16,32,48},{64,80,96,112},{128,144,160,176},{192,208,224,240},{256,27..., dimensions={0} | all-to-all | bytes 196608 | tf_op jit(solution)/shard_map/all_to_all | solution.py:616
  97.4 1.3 %shard_map.100 = f32[3072,128]{1,0:T(8,128)} custom-call(f32[4,48,128]{2,1,0:T(8,128)S(1)} %all_to_all.26.carry_ref, f32[64,128]{1,0:T(8,128)S(1)} %get-tuple-element.27.ends_ref, f32[3072,128]{1,0:T(8,128)S(1)} %shard_map.98.block_ref), custom_call_target="tpu_custom_call" | custom-call | tf_op jit(solution)/shard_map/pallas_call | solution.py:618
  (7 shorter events, 0.1 us)
Async XLA Ops:
  3.1 48.6 %all-to-all-start = ((f32[512,1,96]{2,1,0:T(1,128)}), f32[512,1,96]{2,1,0:T(1,128)S(1)}, u32[]{:S(2)}, u32[]{:S(2)}) async-start(f32[512,1,96]{2,1,0:T(1,128)} %bitcast.27), calls=%async_computation | async-start | bytes 524288 | tf_op jit(solution)/shard_map/all_to_all | solution.py:575
  53.5 10.6 %all-to-all-start.1 = ((f32[16,24,128]{2,1,0:T(8,128)}), f32[16,24,128]{2,1,0:T(8,128)S(1)}, u32[]{:S(2)}, u32[]{:S(2)}) async-start(f32[16,24,128]{2,1,0:T(8,128)} %get-tuple-element.31), calls=%async_computation.1 | async-start | bytes 393216 | tf_op jit(solution)/shard_map/all_to_all | solution.py:588
  72.9 16.0 %all-to-all-start.3 = ((f32[8,24,128]{2,1,0:T(8,128)}), f32[8,24,128]{2,1,0:T(8,128)S(1)}, u32[]{:S(2)}, u32[]{:S(2)}) async-start(f32[8,24,128]{2,1,0:T(8,128)} %shard_map.97), calls=%async_computation.3 | async-start | bytes 196608 | tf_op jit(solution)/shard_map/all_to_all | solution.py:607
